TPU v7x, 32 devices: a whole 2x2x4 slice. The times are simulated.
32 devices in a mesh: seq: 8 (over z, x), rows: 4 (over y, core).
Axes of the slice: x: 2, y: 2, z: 4, core: 2. Of those that a mesh axis runs over, the one named last changes fastest.
Arguments:
- states: bfloat16 [8, 4096, 768], P('rows', 'seq'), may hold values from -6 to 6
- cotangent: bfloat16 [8, 4096, 768], P('rows', 'seq'), may hold values from -6 to 6
- subsets: int32 [8], P('rows'), may hold values from 0 to 21
- subset_weight: float32 [22], replicated, may hold values from 0.5 to 2
- gain_attn: float32 [768], replicated, may hold values from 0.1 to 1.9
- shift_attn: float32 [768], replicated, may hold values from -3 to 3
- gain_ffn: float32 [768], replicated, may hold values from 0.1 to 1.9
- shift_ffn: float32 [768], replicated, may hold values from -3 to 3
- query_projection: bfloat16 [768, 768], P(('seq', 'rows')), may hold values from -0.21875 to 0.21875
- pair_projection: bfloat16 [768, 128], P(('seq', 'rows')), may hold values from -0.21875 to 0.21875
- output_projection: bfloat16 [768, 768], P(('seq', 'rows')), may hold values from -6 to 6
- up_projection: bfloat16 [768, 3072], P(('seq', 'rows')), may hold values from -0.21875 to 0.21875
- down_projection: bfloat16 [3072, 768], P(('seq', 'rows')), may hold values from -0.109375 to 0.109375
Outputs:
- layer_out: bfloat16 [8, 4096, 768], P('rows', 'seq')
- grad_states: bfloat16 [8, 4096, 768], P('rows', 'seq')
- grad_gain_attn: float32 [768], P(('seq', 'rows'))
- grad_shift_attn: float32 [768], P(('seq', 'rows'))
- grad_gain_ffn: float32 [768], P(('seq', 'rows'))
- grad_shift_ffn: float32 [768], P(('seq', 'rows'))
- grad_query: float32 [768, 768], P(('seq', 'rows'))
- grad_pair: float32 [768, 128], P(('seq', 'rows'))
- grad_output: float32 [768, 768], P(('seq', 'rows'))
- grad_up: float32 [768, 3072], P(('seq', 'rows'))
- grad_down: float32 [3072, 768], P(('seq', 'rows'))
Inputs may be any that keep to these rules, and one draw needn't show every extreme that they name: `subsets`: a sequence's Pile subset, one of 22.
All inputs are finite; a program needn't handle non-finite values.
Results may differ from a plain program's by a relative error of at most 0.011.
Values may be sent and summed in bfloat16 or wider, within the bound.
A program may use at most 192 MiB of HBM per device.

v0:
```python
import jax
import jax.numpy as jnp
from jax import lax
from jax.sharding import PartitionSpec as P

H = 12
HD = 64
ROT = 16


masked_value = -1e30


def split_up(shard, dim, peers):
    shape = shard.shape
    parts = shard.reshape(*shape[:dim], peers, shape[dim] // peers, *shape[dim + 1 :])
    return jnp.moveaxis(parts, dim, 0)


def summed_on_arrival(shard, axis, dim):
    parts = split_up(shard, dim, lax.axis_size(axis))
    arrived = lax.all_to_all(parts, axis, split_axis=0, concat_axis=0, tiled=True)
    return arrived.astype(jnp.float32).sum(axis=0)


def layer_norm(values, gain, shift):
    center = values - jnp.mean(values, axis=-1, keepdims=True)
    inverse = lax.rsqrt(jnp.mean(center * center, axis=-1, keepdims=True) + 1e-05)
    normed = center * inverse
    return (normed * gain + shift, normed, inverse)


def norm_back(incoming, normed, inverse, gain):
    scaled = incoming * gain
    return inverse * (
        scaled
        - jnp.mean(scaled, axis=-1, keepdims=True)
        - normed * jnp.mean(scaled * normed, axis=-1, keepdims=True)
    )


def rotary_tables(positions):
    half_rot = ROT // 2
    frequency = 10000.0 ** (-2.0 * jnp.arange(half_rot, dtype=jnp.float32) / ROT)
    angles = positions[:, None] * frequency[None, :]
    cosine = jnp.concatenate([jnp.cos(angles), jnp.cos(angles)], axis=-1)
    sine_vals = jnp.concatenate([jnp.sin(angles), jnp.sin(angles)], axis=-1)
    return (cosine, sine_vals)


def rotate(vector, cosine, sine_vals):
    half_rot = ROT // 2
    rotary_part = vector[..., :ROT]
    turned = jnp.concatenate([-rotary_part[..., half_rot:], rotary_part[..., :half_rot]], axis=-1)
    return jnp.concatenate([rotary_part * cosine + turned * sine_vals, vector[..., ROT:]], axis=-1)


def local_fold(full_keys, update, initial, steps_count, key_block):

    def advance(step_index, current):
        anchor = step_index * key_block
        part_kv = lax.dynamic_slice_in_dim(full_keys, anchor, key_block, 1)
        return update(current, part_kv, anchor)

    return lax.fori_loop(0, steps_count, advance, initial)


def local(
    states,
    cotangent,
    subsets,
    subset_weight,
    gain_attn,
    shift_attn,
    gain_ffn,
    shift_ffn,
    query_projection,
    pair_projection,
    output_projection,
    up_projection,
    down_projection,
):
    seq_here = states.shape[0]
    local_len = states.shape[1]
    model_width = states.shape[2]
    token_count = seq_here * local_len
    length = local_len * lax.axis_size("seq")
    offset = lax.axis_index("seq") * local_len
    last_row = offset + local_len - 1
    key_block = max(min(length, 512), local_len)
    rows_here = offset + jnp.arange(local_len, dtype=jnp.int32)
    cosine, sine_vals = rotary_tables(rows_here.astype(jnp.float32))
    score_scale = HD ** (-0.5)
    gathered = (
        lax.all_gather(query_projection, ("seq", "rows"), axis=0, tiled=True),
        lax.all_gather(pair_projection, ("seq", "rows"), axis=0, tiled=True),
        lax.all_gather(output_projection, ("seq", "rows"), axis=0, tiled=True),
        lax.all_gather(up_projection, ("seq", "rows"), axis=0, tiled=True),
        lax.all_gather(down_projection, ("seq", "rows"), axis=0, tiled=True),
    )
    full_query, full_pair, full_output, full_up, full_down = gathered
    source = states.astype(jnp.float32).reshape(token_count, model_width)
    normed_attn, unit_attn, inverse_attn = layer_norm(source, gain_attn, shift_attn)
    normed_ffn = unit_attn * gain_ffn + shift_ffn
    attention_input = normed_attn.astype(jnp.bfloat16)
    feedforward_input = normed_ffn.astype(jnp.bfloat16)
    query_preactivation = jnp.dot(attention_input, full_query, preferred_element_type=jnp.float32)
    pair_preactivation = jnp.dot(
        attention_input, full_pair, preferred_element_type=jnp.float32
    ).reshape(seq_here, local_len, 2 * HD)
    queries = rotate(
        query_preactivation.reshape(seq_here, local_len, H, HD),
        cosine[None, :, None, :],
        sine_vals[None, :, None, :],
    ).astype(jnp.bfloat16)
    key_values = jnp.concatenate(
        [
            rotate(pair_preactivation[..., :HD], cosine[None], sine_vals[None]),
            pair_preactivation[..., HD:],
        ],
        axis=2,
    ).astype(jnp.bfloat16)

    def block_scores(part_kv, anchor):
        scores = (
            jnp.einsum(
                "sqhd,skd->shqk", queries, part_kv[..., :HD], preferred_element_type=jnp.float32
            )
            * score_scale
        )
        columns = anchor + jnp.arange(part_kv.shape[1], dtype=jnp.int32)
        allowed = (columns[None, :] <= rows_here[:, None])[None, None]
        return (scores, allowed)

    def stats_step(current, part_kv, anchor):

        def stats_work(state_in):
            running, denom_sum = state_in
            scores, allowed = block_scores(part_kv, anchor)
            new_top = jnp.maximum(
                running, jnp.max(jnp.where(allowed, scores, masked_value), axis=-1)
            )
            exp_terms = jnp.where(allowed, jnp.exp(scores - new_top[..., None]), 0.0)
            return (new_top, denom_sum * jnp.exp(running - new_top) + jnp.sum(exp_terms, axis=-1))

        return lax.cond(anchor <= last_row, stats_work, lambda state_in: state_in, current)

    start_stats = (
        jnp.full((seq_here, H, local_len), masked_value, jnp.float32),
        jnp.zeros((seq_here, H, local_len), jnp.float32),
    )
    steps_count = last_row // key_block + 1
    full_keys = lax.all_gather(key_values, "seq", axis=1, tiled=True)
    running, denom_sum = local_fold(full_keys, stats_step, start_stats, steps_count, key_block)
    logsum = running + jnp.log(denom_sum)

    def mix_step(current, part_kv, anchor):

        def mix_work(accum):
            scores, allowed = block_scores(part_kv, anchor)
            prob_low = jnp.where(allowed, jnp.exp(scores - logsum[..., None]), 0.0).astype(
                jnp.bfloat16
            )
            return accum + jnp.einsum(
                "shqk,skd->sqhd", prob_low, part_kv[..., HD:], preferred_element_type=jnp.float32
            )

        return lax.cond(anchor <= last_row, mix_work, lambda accum: accum, current)

    start_mix = jnp.zeros((seq_here, local_len, H, HD), jnp.float32)
    attention_output = local_fold(full_keys, mix_step, start_mix, steps_count, key_block)
    attended_low = attention_output.reshape(token_count, model_width).astype(jnp.bfloat16)
    up_preactivation = jnp.dot(feedforward_input, full_up, preferred_element_type=jnp.float32)
    gelu_output = jax.nn.gelu(up_preactivation, approximate=False).astype(jnp.bfloat16)
    residual_branch = jnp.dot(attended_low, full_output, preferred_element_type=jnp.float32)
    residual_branch = residual_branch + jnp.dot(
        gelu_output, full_down, preferred_element_type=jnp.float32
    )
    layer_out = (
        (source + residual_branch).astype(jnp.bfloat16).reshape(seq_here, local_len, model_width)
    )
    table_rows = jnp.arange(subset_weight.shape[0], dtype=jnp.int32)
    row_scale = jnp.sum(
        jnp.where(table_rows[None, :] == subsets[:, None], subset_weight[None, :], 0.0), axis=1
    )
    upstream = (cotangent.astype(jnp.float32) * row_scale[:, None, None]).reshape(
        token_count, model_width
    )
    branch_grad = upstream.astype(jnp.bfloat16)
    back_query, back_pair, back_output, back_up, back_down = gathered
    grad_down = jnp.einsum(
        "tf,td->fd", gelu_output, branch_grad, preferred_element_type=jnp.float32
    )
    act_grad = jnp.einsum("td,fd->tf", branch_grad, back_down, preferred_element_type=jnp.float32)
    gelu_pull = jax.vjp(
        lambda argument: jax.nn.gelu(argument, approximate=False), up_preactivation
    )[1]
    up_grad = gelu_pull(act_grad)[0].astype(jnp.bfloat16)
    grad_up = jnp.einsum(
        "td,tf->df", feedforward_input, up_grad, preferred_element_type=jnp.float32
    )
    ffn_input_grad = jnp.einsum("tf,df->td", up_grad, back_up, preferred_element_type=jnp.float32)
    grad_output = jnp.einsum(
        "tc,td->cd", attended_low, branch_grad, preferred_element_type=jnp.float32
    )
    out_grad = jnp.einsum(
        "td,cd->tc", branch_grad, back_output, preferred_element_type=jnp.float32
    ).astype(jnp.bfloat16)
    out_grad = out_grad.reshape(seq_here, local_len, H, HD)
    row_delta = jnp.einsum("sqhd,sqhd->shq", out_grad.astype(jnp.float32), attention_output)

    def grad_step(current, part_kv, anchor):

        def grad_work(state_in):
            query_acc, pair_acc = state_in
            scores, allowed = block_scores(part_kv, anchor)
            probs = jnp.where(allowed, jnp.exp(scores - logsum[..., None]), 0.0)
            prob_low = probs.astype(jnp.bfloat16)
            prob_grad = jnp.einsum(
                "sqhd,skd->shqk", out_grad, part_kv[..., HD:], preferred_element_type=jnp.float32
            )
            score_grad = (probs * (prob_grad - row_delta[..., None])).astype(jnp.bfloat16)
            query_acc = query_acc + score_scale * jnp.einsum(
                "shqk,skd->sqhd", score_grad, part_kv[..., :HD], preferred_element_type=jnp.float32
            )
            key_grad = score_scale * jnp.einsum(
                "shqk,sqhd->skd", score_grad, queries, preferred_element_type=jnp.float32
            )
            value_grad = jnp.einsum(
                "shqk,sqhd->skd", prob_low, out_grad, preferred_element_type=jnp.float32
            )
            previous = lax.dynamic_slice_in_dim(pair_acc, anchor, part_kv.shape[1], 1)
            pair_acc = lax.dynamic_update_slice_in_dim(
                pair_acc, previous + jnp.concatenate([key_grad, value_grad], axis=2), anchor, 1
            )
            return (query_acc, pair_acc)

        return lax.cond(anchor <= last_row, grad_work, lambda state_in: state_in, current)

    start_grad = (
        jnp.zeros((seq_here, local_len, H, HD), jnp.float32),
        jnp.zeros((seq_here, length, 2 * HD), jnp.float32),
    )
    query_grad, pair_terms = local_fold(full_keys, grad_step, start_grad, steps_count, key_block)
    pair_grad = summed_on_arrival(pair_terms.astype(jnp.bfloat16), "seq", 1)
    query_pre_grad = rotate(query_grad, cosine[None, :, None, :], -sine_vals[None, :, None, :])
    query_pre_grad = query_pre_grad.reshape(token_count, model_width).astype(jnp.bfloat16)
    pair_pre_grad = jnp.concatenate(
        [rotate(pair_grad[..., :HD], cosine[None], -sine_vals[None]), pair_grad[..., HD:]], axis=2
    )
    pair_pre_grad = pair_pre_grad.reshape(token_count, 2 * HD).astype(jnp.bfloat16)
    grad_query = jnp.einsum(
        "td,te->de", attention_input, query_pre_grad, preferred_element_type=jnp.float32
    )
    grad_pair = jnp.einsum(
        "td,te->de", attention_input, pair_pre_grad, preferred_element_type=jnp.float32
    )
    attn_input_grad = jnp.einsum(
        "te,de->td", query_pre_grad, back_query, preferred_element_type=jnp.float32
    )
    attn_input_grad = attn_input_grad + jnp.einsum(
        "te,de->td", pair_pre_grad, back_pair, preferred_element_type=jnp.float32
    )
    grad_gain_attn = jnp.sum(attn_input_grad * unit_attn, axis=0)
    grad_shift_attn = jnp.sum(attn_input_grad, axis=0)
    grad_gain_ffn = jnp.sum(ffn_input_grad * unit_attn, axis=0)
    grad_shift_ffn = jnp.sum(ffn_input_grad, axis=0)
    grad_states = upstream + norm_back(attn_input_grad, unit_attn, inverse_attn, gain_attn)
    grad_states = grad_states + norm_back(ffn_input_grad, unit_attn, inverse_attn, gain_ffn)
    grad_states = grad_states.astype(jnp.bfloat16).reshape(seq_here, local_len, model_width)
    homes = (
        lax.psum_scatter(grad_query, ("seq", "rows"), scatter_dimension=0, tiled=True),
        lax.psum_scatter(grad_pair, ("seq", "rows"), scatter_dimension=0, tiled=True),
        lax.psum_scatter(grad_output, ("seq", "rows"), scatter_dimension=0, tiled=True),
        lax.psum_scatter(grad_up, ("seq", "rows"), scatter_dimension=0, tiled=True),
        lax.psum_scatter(grad_down, ("seq", "rows"), scatter_dimension=0, tiled=True),
        lax.psum_scatter(grad_gain_attn, ("seq", "rows"), scatter_dimension=0, tiled=True),
        lax.psum_scatter(grad_shift_attn, ("seq", "rows"), scatter_dimension=0, tiled=True),
        lax.psum_scatter(grad_gain_ffn, ("seq", "rows"), scatter_dimension=0, tiled=True),
        lax.psum_scatter(grad_shift_ffn, ("seq", "rows"), scatter_dimension=0, tiled=True),
    )
    return (
        layer_out,
        grad_states,
        homes[5],
        homes[6],
        homes[7],
        homes[8],
        homes[0],
        homes[1],
        homes[2],
        homes[3],
        homes[4],
    )


def solution(mesh):
    return jax.shard_map(
        local,
        mesh=mesh,
        in_specs=(
            P("rows", "seq", None),
            P("rows", "seq", None),
            P("rows"),
            P(),
            P(),
            P(),
            P(),
            P(),
            P(("seq", "rows"), None),
            P(("seq", "rows"), None),
            P(("seq", "rows"), None),
            P(("seq", "rows"), None),
            P(("seq", "rows"), None),
        ),
        out_specs=(
            P("rows", "seq", None),
            P("rows", "seq", None),
            P(("seq", "rows")),
            P(("seq", "rows")),
            P(("seq", "rows")),
            P(("seq", "rows")),
            P(("seq", "rows"), None),
            P(("seq", "rows"), None),
            P(("seq", "rows"), None),
            P(("seq", "rows"), None),
            P(("seq", "rows"), None),
        ),
        check_vma=False,
    )
```

profile of v0, /device:TPU:0, one launch (start us, length us, event | category | flops | bytes accessed | tf_op | source)
XLA Modules:
  0.0 1396.2 jit_solution(855635948056339447)
XLA Ops:
  11.0 44.0 %all_gather.18 = bf16[768,128]{1,0:T(8,128)(2,1)S(1)} all-gather(bf16[24,128]{1,0:T(8,128)(2,1)} %param.34), channel_id=1, replica_groups=mesh['seq'=8,'rows'=4] {'seq','rows'}, dimensions={0}, use_global_device_ids=true | all-gather | bytes 202752 | tf_op jit(solution)/shard_map/all_gather | solution.py:96
  75.0 48.8 %all-gather.10.cloned.1.call-done = bf16[768,768]{1,0:T(8,128)(2,1)} async-done(((bf16[24,768]{1,0:T(8,128)(2,1)}), bf16[768,768]{1,0:T(8,128)(2,1)}) %all-gather.10.cloned.1.call-update) | async-done | bytes 1179664 | tf_op jit(solution)/shard_map/all_gather | solution.py:97
  137.4 39.1 %all-gather.6.cloned.1.call-done = bf16[2,4096,128]{1,2,0:T(8,128)(2,1)} async-done(((bf16[2,512,128]{1,2,0:T(8,128)(2,1)}), bf16[2,4096,128]{1,2,0:T(8,128)(2,1)}) %all-gather.6.cloned.1.call-update) | async-done | bytes 2097168 | tf_op jit(solution)/shard_map/all_gather | solution.py:153
  176.5 10.6 while.40
  176.8 10.3 conditional.9
  189.8 9.9 while.41
  189.8 9.9 conditional.10
  190.0 9.6 bitcast_add_fusion
  207.8 56.6 %while.42 = (s32[]{:T(128)}, f32[2,512,12,64]{1,3,2,0:T(8,128)}, f32[2,4096,128]{1,2,0:T(8,128)}, s32[]{:T(128)}, s32[]{:T(128)}, /*index=5*/bf16[2,4096,128]{1,...) while((s32[]{:T(128)}, f32[2,512,12,64]{1,3,2,0:T(8,128)}, ...), condition=%wide.region_16.17_spmd.clone, body=%wide.region_13.16_spmd.clone.sunk | while | flops 4091610112 | bytes 180662672 | solution.py:65
  208.2 56.0 %conditional.11 = ((f32[2,512,12,64]{1,3,2,0:T(8,128)}, f32[2,4096,128]{1,2,0:T(8,128)})) conditional(s32[]{:T(128)} %convert_element_type.221, (f32[2,512,12,64]{1,3,2,0:T(8,128)}, f32[2,4096,128]{1,2,0:T(8,128)}) %tuple.142, (s32[]{:T(128)}, s32[]{:T(128)}, bf16[2,4096,128]{1,2,0:T(8,128)(2,1)}, bf16[2,512,12,64]{1,3,2,0:T(8,128)(2,1)S(1)}, ...), branch_computations={%region_14.14_spmd, %region_15.15_spmd} | conditional | flops 4091610112 | bytes 180660384 | solution.py:238
  208.3 11.2 fusion.39
  219.7 15.9 %fusion.27 = bf16[2,12,512,512]{2,3,1,0:T(8,128)(2,1)} fusion(f32[2,512,512,12]{2,1,3,0:T(8,128)} %fusion.39, f32[2,12,512]{2,1,0:T(8,128)S(1)} %get-tuple-element.353, f32[2,12,512]{2,1,0:T(8,128)} %get-tuple-element.351, pred[512,512]{0,1:T(8,128)(4,1)S(1)} %broadcast_compare_fusion.2, bf16[2,512,12,64]{1,3,2,0:T(8,128)(2,1)} %get-tuple-element.352, ...), kind=kOutput, calls=%fused_computation.34 | convolution fusion | flops 843055104 | bytes 39829512 | tf_op jit(solution)/shard_map/while/body/cond/branch_1_fun/sqhd,skd->shqk/dot_general | solution.py:219
  244.3 12.1 fusion.34
  281.3 527.3 %all-to-all-start = ((bf16[8,2,512,128]{2,3,1,0:T(8,128)(2,1)}), bf16[8,2,512,128]{2,3,1,0:T(8,128)(2,1)}, u32[]{:S(2)}, u32[]{:S(2)}) async-start(bf16[8,2,512,128]{2,3,1,0:T(8,128)(2,1)} %copy.80), calls=%async_computation | async-start | bytes 4194304 | tf_op jit(solution)/shard_map/all_to_all | solution.py:22
  818.2 44.8 %all-to-all-done = bf16[8,2,512,128]{2,3,1,0:T(8,128)(2,1)} async-done(((bf16[8,2,512,128]{2,3,1,0:T(8,128)(2,1)}), bf16[8,2,512,128]{2,3,1,0:T(8,128)(2,1)}, u32[]{:S(2)}, u32[]{:S(2)}) %all-to-all-start) | async-done | bytes 2097184 | tf_op jit(solution)/shard_map/all_to_all | solution.py:22
  868.0 35.8 %multiply_convert_fusion = (bf16[1024,3072]{1,0:T(8,128)(2,1)}, f32[1024,3072]{1,0:T(8,128)}, f32[1024,3072]{1,0:T(8,128)}) fusion(bf16[1024,768]{1,0:T(8,128)(2,1)S(1)} %copy-done.24, bf16[768,3072]{1,0:T(8,128)(2,1)} %all-gather.12.cloned.1.call-done), kind=kOutput, calls=%fused_computation.61 | convolution fusion | flops 5036310528 | bytes 37748736 | tf_op jit(solution)/shard_map/dot_general | solution.py:173
  903.7 15.7 %add_convert_fusion = bf16[1024,3072]{1,0:T(8,128)(2,1)} fusion(f32[1024,3072]{1,0:T(8,128)} %get-tuple-element.612, f32[1024,3072]{1,0:T(8,128)} %get-tuple-element.639, bf16[1024,768]{1,0:T(8,128)(2,1)S(1)} %copy-done.26, bf16[3072,768]{1,0:T(8,128)(2,1)} %all-gather.14.cloned.1.call-done), kind=kOutput, calls=%fused_computation.60 | convolution fusion | flops 4875878400 | bytes 37748736 | tf_op jit(solution)/shard_map/td,fd->tf/dot_general | solution.py:194
  919.4 10.4 fusion.99
  930.1 10.2 fusion.100
  945.6 8.8 fusion.96
  958.5 39.0 %all-reduce.5 = (f32[768]{0:T(1024)S(1)}, f32[768]{0:T(1024)S(1)}, f32[768]{0:T(1024)S(1)}, f32[768]{0:T(1024)S(1)}) all-reduce(f32[768]{0:T(1024)S(1)} %get-tuple-element.543, f32[768]{0:T(1024)S(1)} %get-tuple-element.548, f32[768]{0:T(1024)S(1)} %get-tuple-element.552, ...), channel_id=2, replica_groups=mesh['seq'=8,'rows'=4] {'seq','rows'}, use_global_device_ids=true, to_apply=%region_23.24.clone | all-reduce | flops 3072 | bytes 24576
  1015.9 89.8 %reduce-scatter.16.cloned.1.call-done = f32[24,128]{1,0:T(8,128)} async-done(((f32[768,128]{1,0:T(8,128)}), f32[24,128]{1,0:T(8,128)}) %reduce-scatter.16.cloned.1.call-update) | async-done | bytes 12304
  1105.6 142.2 %reduce-scatter.12.cloned.1.call-done = f32[24,3072]{1,0:T(8,128)} async-done(((f32[768,3072]{1,0:T(8,128)}), f32[24,3072]{1,0:T(8,128)}) %reduce-scatter.12.cloned.1.call-update) | async-done | bytes 294928 | tf_op jit(solution)/shard_map/reduce_scatter | solution.py:275
  1247.9 141.0 %reduce-scatter.14.cloned.1.call-done = f32[96,768]{1,0:T(8,128)} async-done(((f32[3072,768]{1,0:T(8,128)}), f32[96,768]{1,0:T(8,128)}) %reduce-scatter.14.cloned.1.call-update) | async-done | bytes 294928 | tf_op jit(solution)/shard_map/reduce_scatter | solution.py:276
  (219 shorter events, 134.3 us)
Async XLA Ops:
  7.2 50.5 %copy-start.1 = (bf16[2,512,768]{2,1,0:T(8,128)(2,1)S(1)}, bf16[2,512,768]{2,1,0:T(8,128)(2,1)}, u32[]{:S(2)}) copy-start(bf16[2,512,768]{2,1,0:T(8,128)(2,1)} %param.25) | copy-start | bytes 4718596
  7.2 50.5 %copy-start.43 = (f32[768]{0:T(1024)S(1)}, f32[768]{0:T(1024)}, u32[]{:S(2)}) copy-start(f32[768]{0:T(1024)} %param.29) | copy-start | bytes 9220
  7.2 50.5 %copy-start.47 = (f32[768]{0:T(1024)S(1)}, f32[768]{0:T(1024)}, u32[]{:S(2)}) copy-start(f32[768]{0:T(1024)} %param.30) | copy-start | bytes 9220
  7.2 61.9 %all-gather.8.cloned.1.call-start = ((), (), s32[]{:S(2)}) async-start(), calls=%async_computation.7 | async-start | bytes 1216512 | tf_op jit(solution)/shard_map/all_gather | solution.py:95
  7.9 115.9 %all-gather.10.cloned.1.call-start = ((), (), s32[]{:S(2)}) async-start(), calls=%async_computation.8 | async-start | bytes 1216512 | tf_op jit(solution)/shard_map/all_gather | solution.py:97
  8.7 167.8 %all-gather.6.cloned.1.call-start = ((), (), s32[]{:S(2)}) async-start(), calls=%async_computation.6 | async-start | bytes 2359296 | tf_op jit(solution)/shard_map/all_gather | solution.py:153
  58.4 12.3 copy-start.7
  60.7 70.9 %copy-start.30 = (f32[512,16]{0,1:T(8,128)}, f32[512,16]{0,1:T(8,128)S(1)}, u32[]{:S(2)}) copy-start(f32[512,16]{0,1:T(8,128)S(1)} %get-tuple-element.641) | copy-start | bytes 98308
  63.1 804.9 %all-gather.12.cloned.1.call-start = ((), (), s32[]{:S(2)}) async-start(), calls=%async_computation.9 | async-start | bytes 4866048 | tf_op jit(solution)/shard_map/all_gather | solution.py:98
  63.7 840.1 %all-gather.14.cloned.1.call-start = ((), (), s32[]{:S(2)}) async-start(), calls=%async_computation.10 | async-start | bytes 4866048 | tf_op jit(solution)/shard_map/all_gather | solution.py:99
  64.3 951.6 %reduce-scatter.8.cloned.1.call-start = ((), (), s32[]{:S(2)}) async-start(), calls=%async_computation.11 | async-start | bytes 2433024 | tf_op jit(solution)/shard_map/reduce_scatter | solution.py:272
  219.7 15.9 %copy-start.12 = (pred[512,512]{0,1:T(8,128)(4,1)}, pred[512,512]{0,1:T(8,128)(4,1)S(1)}, u32[]{:S(2)}) copy-start(pred[512,512]{0,1:T(8,128)(4,1)S(1)} %broadcast_compare_fusion.2) | copy-start | bytes 786436 | tf_op jit(solution)/shard_map/while/body/cond
  244.3 14.1 %copy-start = (bf16[2,12,512,512]{2,3,1,0:T(8,128)(2,1)S(1)}, bf16[2,12,512,512]{2,3,1,0:T(8,128)(2,1)}, u32[]{:S(2)}) copy-start(bf16[2,12,512,512]{2,3,1,0:T(8,128)(2,1)} %fusion.27) | copy-start | bytes 37748740 | tf_op jit(solution)/shard_map/while/body/cond
  281.3 527.4 %copy-start.4 = (f32[2,512,12,64]{1,3,2,0:T(8,128)S(1)}, f32[2,512,12,64]{1,3,2,0:T(8,128)}, u32[]{:S(2)}) copy-start(f32[2,512,12,64]{1,3,2,0:T(8,128)} %get-tuple-element.388) | copy-start | bytes 9437188
  281.3 581.6 %all-to-all-start = ((bf16[8,2,512,128]{2,3,1,0:T(8,128)(2,1)}), bf16[8,2,512,128]{2,3,1,0:T(8,128)(2,1)}, u32[]{:S(2)}, u32[]{:S(2)}) async-start(bf16[8,2,512,128]{2,3,1,0:T(8,128)(2,1)} %copy.80), calls=%async_computation | async-start | bytes 4194304 | tf_op jit(solution)/shard_map/all_to_all | solution.py:22
  808.7 207.2 %reduce-scatter.10.cloned.1.call-start = ((), (), s32[]{:S(2)}) async-start(), calls=%async_computation.12 | async-start | bytes 2433024 | tf_op jit(solution)/shard_map/reduce_scatter | solution.py:274
  815.0 290.6 %reduce-scatter.16.cloned.1.call-start = ((), (), s32[]{:S(2)}) async-start(), calls=%async_computation.15 | async-start | bytes 405504
  816.4 49.9 %copy-start.9 = (bf16[2,512,768]{2,1,0:T(8,128)(2,1)S(1)}, bf16[2,512,768]{2,1,0:T(8,128)(2,1)}, u32[]{:S(2)}) copy-start(bf16[2,512,768]{2,1,0:T(8,128)(2,1)} %copy-done.7) | copy-start | bytes 4718596
  818.2 49.8 %copy-start.24 = (bf16[1024,768]{1,0:T(8,128)(2,1)S(1)}, bf16[1024,768]{1,0:T(8,128)(2,1)}, u32[]{:S(2)}) copy-start(bf16[1024,768]{1,0:T(8,128)(2,1)} %fusion.68) | copy-start | bytes 4718596
  867.7 36.1 %copy-start.26 = (bf16[1024,768]{1,0:T(8,128)(2,1)S(1)}, bf16[1024,768]{1,0:T(8,128)(2,1)}, u32[]{:S(2)}) copy-start(bf16[1024,768]{1,0:T(8,128)(2,1)} %bitcast_convert_fusion) | copy-start | bytes 4718596
  867.7 380.2 %reduce-scatter.12.cloned.1.call-start = ((), (), s32[]{:S(2)}) async-start(), calls=%async_computation.13 | async-start | bytes 9732096 | tf_op jit(solution)/shard_map/reduce_scatter | solution.py:275
  929.8 459.1 %reduce-scatter.14.cloned.1.call-start = ((), (), s32[]{:S(2)}) async-start(), calls=%async_computation.14 | async-start | bytes 9732096 | tf_op jit(solution)/shard_map/reduce_scatter | solution.py:276
  945.5 8.8 copy-start.3
  945.5 8.8 copy-start.33
  (40 other events, 153.2 us)
Sparse Core Ops, SparseCore 0:
  11.0 56.8 all-gather.7
  70.8 53.0 all-gather.9
  126.4 50.0 all-gather.5
  179.3 61.7 all-gather.11
  243.8 62.3 all-gather.13
  312.0 589.3 reduce-scatter.7
  908.0 98.1 reduce-scatter.9
  1011.8 93.8 reduce-scatter.15
  1113.1 134.7 reduce-scatter.11
  1254.2 134.5 reduce-scatter.13
where the time goes:
time: 1400 us
  starting transfers between devices  528 us (38%)
  waiting for transfers between devices  508 us (36%)
  matrix products  180 us (13%)
  blocking collectives  83 us (6%)
  local copies, waits for them, and re-layouts  41.3 us (3%)
  other arithmetic  39.6 us (3%)
  between operations  15.5 us (1%)
    all_to_all x1, starting transfers between devices, summed_on_arrival(): lax.all_to_all(parts, axis, split_axis=0, concat_axis=0, tiled=True)  527 us
    reduce_scatter x1, waiting for transfers between devices, local(): lax.psum_scatter(grad_up, ('seq', 'rows'), scatter_dimension=0, tiled=True)  142 us
    reduce_scatter x1, waiting for transfers between devices, local(): lax.psum_scatter(grad_down, ('seq', 'rows'), scatter_dimension=0, tiled=T...  141 us
    unnamed x11, waiting for transfers between devices  92.3 us
    all_gather x1, waiting for transfers between devices, local(): lax.all_gather(output_projection, ('seq', 'rows'), axis=0, tiled=True)  48.8 us
    all_to_all x1, waiting for transfers between devices, summed_on_arrival(): lax.all_to_all(parts, axis, split_axis=0, concat_axis=0, tiled=True)  44.8 us
    all_gather x1, blocking collectives, local(): lax.all_gather(pair_projection, ('seq', 'rows'), axis=0, tiled=True)  44 us
    all_gather x1, waiting for transfers between devices, local(): full_keys = lax.all_gather(key_values, 'seq', axis=1, tiled=True)  39.1 us
  transfers between devices with their start and end apart: 11, of which 6 were waited for; matrix products, arithmetic and copies ran while one was open for 18% of the time, Pallas kernels for 0%

commit v1 on v0

v1 whole, which is shorter than its diff:
```python
import functools
import jax
import jax.numpy as jnp
from jax import lax
from jax.experimental import pallas as pl
from jax.experimental.pallas import tpu as pltpu

H = 12
HD = 64
LN2 = 0.6931471805599453


def dot(a, b, ca, cb):
    return lax.dot_general(a, b, (((ca,), (cb,)), ((), ())), preferred_element_type=jnp.float32)


def three_parts(x):
    hi = x.astype(jnp.bfloat16)
    rest = x - hi.astype(jnp.float32)
    mid = rest.astype(jnp.bfloat16)
    low = (rest - mid.astype(jnp.float32)).astype(jnp.bfloat16)
    return hi, mid, low


def attn_kernel(
    M, tk, G,
    seq_ref, row_ref, wide_ref,
    q_ref, g_ref, ka_ref, va_ref,
    o_ref, dq_ref, dkv_ref,
    qs, gs, qt, gt, stash, oacc, dqacc, top,
):
    t = pl.program_id(0)
    seq = seq_ref[t]
    row0 = row_ref[t]
    rows_all = H * M
    f32, bf16 = jnp.float32, jnp.bfloat16

    @pl.when(t == 0)
    def _():
        qs[...] = jnp.zeros_like(qs)
        dkv_ref[...] = jnp.zeros_like(dkv_ref)

    for h in range(H):
        qs[h * M:(h + 1) * M, :HD] = q_ref[:, h * HD:(h + 1) * HD]
    oacc[...] = jnp.zeros_like(oacc)
    dqacc[...] = jnp.zeros_like(dqacc)
    n_full = row0 // tk

    def keys(ref, kt):
        return ref[seq, pl.ds(pl.multiple_of(kt * tk, tk), tk), :]

    def allowed(kt):
        row = row0 + (lax.broadcasted_iota(jnp.int32, (G, tk), 0) & (M - 1))
        col = kt * tk + lax.broadcasted_iota(jnp.int32, (G, tk), 1)
        return col <= row

    def scores(kt, g, masked):
        s = dot(qs[g * G:(g + 1) * G, :], keys(ka_ref, kt), 1, 1)
        if masked:
            s = jnp.where(allowed(kt), s, -1e30)
        return s

    @pl.when(wide_ref[0] != 0)
    def _():
        for h in range(H):
            qs[h * M:(h + 1) * M, HD:] = jnp.zeros((M, 128 - HD), bf16)
        top[...] = jnp.full_like(top, -1e30)

        def peak(kt, masked):
            for g in range(rows_all // G):
                s = scores(kt, g, masked)
                part = s[:, :128]
                for j in range(1, tk // 128):
                    part = jnp.maximum(part, s[:, j * 128:(j + 1) * 128])
                r = slice(g * G, (g + 1) * G)
                top[r, :] = jnp.maximum(top[r, :], part)

        lax.fori_loop(0, n_full, lambda kt, _: (peak(kt, False), 0)[1], 0)
        peak(n_full, True)
        for h in range(H):
            r = slice(h * M, (h + 1) * M)
            best = -jnp.max(top[r, :], axis=1, keepdims=True)
            for j, part in enumerate(three_parts(best)):
                qs[r, HD + j:HD + j + 1] = part

    def first(kt, masked):
        v = keys(va_ref, kt)
        for g in range(rows_all // G):
            r = slice(g * G, (g + 1) * G)
            e = jnp.exp2(scores(kt, g, masked)).astype(bf16)
            stash[kt, r, :] = e
            oacc[r, :] += dot(e, v, 1, 0)

    lax.fori_loop(0, n_full, lambda kt, _: (first(kt, False), 0)[1], 0)
    first(n_full, True)

    for p in range(H // 2):
        outs = []
        for h in (2 * p, 2 * p + 1):
            r = slice(h * M, (h + 1) * M)
            acc = oacc[r, :]
            inverse = 1.0 / acc[:, HD:HD + 1]
            out = acc[:, :HD] * inverse
            outs.append(out)
            low = (g_ref[:, h * HD:(h + 1) * HD].astype(f32) * inverse).astype(bf16)
            delta = -jnp.sum(low.astype(f32) * out, axis=1, keepdims=True)
            parts = three_parts(delta)
            gs[r, :] = jnp.concatenate(
                [low, *parts, jnp.zeros((M, 128 - HD - 3), bf16)], axis=1)
        o_ref[:, p * 128:(p + 1) * 128] = jnp.concatenate(outs, axis=1).astype(bf16)
    qt[...] = qs[...].T
    gt[...] = gs[...].T

    def second(kt):
        k = keys(ka_ref, kt)
        v = keys(va_ref, kt)
        dk = jnp.zeros((HD, tk), f32)
        dv = jnp.zeros((HD, tk), f32)
        for g in range(rows_all // G):
            r = slice(g * G, (g + 1) * G)
            e = stash[kt, r, :]
            slope = (e.astype(f32) * dot(gs[r, :], v, 1, 1)).astype(bf16)
            dqacc[r, :] += dot(slope, k, 1, 0)
            dk = dk + dot(qt[:HD, r], slope, 1, 0)
            dv = dv + dot(gt[:HD, r], e, 1, 0)
        c = pl.ds(pl.multiple_of(kt * tk, tk), tk)
        dkv_ref[seq, :HD, c] += dk
        dkv_ref[seq, HD:, c] += dv

    lax.fori_loop(0, n_full + 1, lambda kt, _: (second(kt), 0)[1], 0)
    for p in range(H // 2):
        both = [dqacc[h * M:(h + 1) * M, :HD] for h in (2 * p, 2 * p + 1)]
        dq_ref[:, p * 128:(p + 1) * 128] = jnp.concatenate(both, axis=1)


def attention(seqs, rows, wide, q, g, ka, va, M, tk=512):
    G = 4 * M
    slots = q.shape[0] // M
    S, L, _ = ka.shape
    width = H * HD
    grid_spec = pltpu.PrefetchScalarGridSpec(
        num_scalar_prefetch=3,
        grid=(slots,),
        in_specs=[
            pl.BlockSpec((M, width), lambda t, *_: (t, 0)),
            pl.BlockSpec((M, width), lambda t, *_: (t, 0)),
            pl.BlockSpec((S, L, 128), lambda t, *_: (0, 0, 0), pipeline_mode=pl.Buffered(1)),
            pl.BlockSpec((S, L, 128), lambda t, *_: (0, 0, 0), pipeline_mode=pl.Buffered(1)),
        ],
        out_specs=[
            pl.BlockSpec((M, width), lambda t, *_: (t, 0)),
            pl.BlockSpec((M, width), lambda t, *_: (t, 0)),
            pl.BlockSpec((S, 128, L), lambda t, *_: (0, 0, 0), pipeline_mode=pl.Buffered(1)),
        ],
        scratch_shapes=[
            pltpu.VMEM((H * M, 128), jnp.bfloat16),
            pltpu.VMEM((H * M, 128), jnp.bfloat16),
            pltpu.VMEM((128, H * M), jnp.bfloat16),
            pltpu.VMEM((128, H * M), jnp.bfloat16),
            pltpu.VMEM((L // tk, H * M, tk), jnp.bfloat16),
            pltpu.VMEM((H * M, 128), jnp.float32),
            pltpu.VMEM((H * M, 128), jnp.float32),
            pltpu.VMEM((H * M, 128), jnp.float32),
        ],
    )
    pairs = slots * M * H * L // 2
    return pl.pallas_call(
        functools.partial(attn_kernel, M, tk, G),
        grid_spec=grid_spec,
        out_shape=[
            jax.ShapeDtypeStruct((slots * M, width), jnp.bfloat16),
            jax.ShapeDtypeStruct((slots * M, width), jnp.float32),
            jax.ShapeDtypeStruct((S, 128, L), jnp.float32),
        ],
        compiler_params=pltpu.CompilerParams(vmem_limit_bytes=56 << 20),
        cost_estimate=pl.CostEstimate(flops=12 * pairs * 64, bytes_accessed=16 << 20, transcendentals=pairs),
        name="attention",
    )(seqs, rows, wide, q, g, ka, va)


def gelu_both(x):
    z = jnp.abs(x) * 0.7071067811865476
    s = 1.0 / (1.0 + 0.3275911 * z)
    poly = s * (0.127414796 + s * (-0.142248368 + s * (0.710706871 + s * (-0.7265760135 + s * 0.5307027145))))
    bell = jnp.exp(-z * z)
    tail = poly * bell
    phi = jnp.where(x >= 0.0, 1.0 - tail, tail)
    return x * phi, phi + x * (bell * 0.3989422804014327)


def ffn_kernel(C, x_ref, b_ref, up_ref, down_ref, out_ref, dx_ref, gup_ref, gdown_ref, act_s, ug_s):
    f = pl.program_id(0)
    T = x_ref.shape[0]

    @pl.when(f == 0)
    def _():
        out_ref[...] = jnp.zeros_like(out_ref)
        dx_ref[...] = jnp.zeros_like(dx_ref)

    up = up_ref[...]
    down = down_ref[...]
    for c in range(T // C):
        r = slice(c * C, (c + 1) * C)
        u = dot(x_ref[r, :], up, 1, 0)
        a = dot(b_ref[r, :], down, 1, 1)
        act, slope = gelu_both(u)
        act = act.astype(jnp.bfloat16)
        ug = (a * slope).astype(jnp.bfloat16)
        act_s[r, :] = act
        ug_s[r, :] = ug
        out_ref[r, :] += dot(act, down, 1, 0)
        dx_ref[r, :] += dot(ug, up, 1, 1)
    gup_ref[...] = dot(x_ref[...], ug_s[...], 0, 0).astype(gup_ref.dtype)
    gdown_ref[...] = dot(act_s[...], b_ref[...], 0, 0).astype(gdown_ref.dtype)


def ffn(x, b, up, down, F=512, C=256, wire=jnp.bfloat16):
    T, D = x.shape
    FF = up.shape[1]
    C = min(C, T)
    f32, bf16 = jnp.float32, jnp.bfloat16
    whole = lambda f: (0, 0)
    return pl.pallas_call(
        functools.partial(ffn_kernel, C),
        grid=(FF // F,),
        in_specs=[
            pl.BlockSpec((T, D), whole, pipeline_mode=pl.Buffered(1)),
            pl.BlockSpec((T, D), whole, pipeline_mode=pl.Buffered(1)),
            pl.BlockSpec((D, F), lambda f: (0, f)),
            pl.BlockSpec((F, D), lambda f: (f, 0)),
        ],
        out_specs=[
            pl.BlockSpec((T, D), whole, pipeline_mode=pl.Buffered(1)),
            pl.BlockSpec((T, D), whole, pipeline_mode=pl.Buffered(1)),
            pl.BlockSpec((D, F), lambda f: (0, f)),
            pl.BlockSpec((F, D), lambda f: (f, 0)),
        ],
        out_shape=[
            jax.ShapeDtypeStruct((T, D), f32),
            jax.ShapeDtypeStruct((T, D), f32),
            jax.ShapeDtypeStruct((D, FF), wire),
            jax.ShapeDtypeStruct((FF, D), wire),
        ],
        scratch_shapes=[pltpu.VMEM((T, F), bf16), pltpu.VMEM((T, F), bf16)],
        compiler_params=pltpu.CompilerParams(vmem_limit_bytes=56 << 20),
        cost_estimate=pl.CostEstimate(flops=12 * T * D * FF, bytes_accessed=32 << 20, transcendentals=T * FF),
        name="feedforward",
    )(x, b, up, down)


ROT = 16


def layer_norm(values):
    center = values - jnp.mean(values, axis=-1, keepdims=True)
    inverse = lax.rsqrt(jnp.mean(center * center, axis=-1, keepdims=True) + 1e-05)
    return center * inverse, inverse


def norm_back(incoming, normed, inverse, gain):
    scaled = incoming * gain
    return inverse * (
        scaled
        - jnp.mean(scaled, axis=-1, keepdims=True)
        - normed * jnp.mean(scaled * normed, axis=-1, keepdims=True)
    )


def rotary_tables(positions):
    half_rot = ROT // 2
    frequency = 10000.0 ** (-2.0 * jnp.arange(half_rot, dtype=jnp.float32) / ROT)
    angles = positions[:, None] * frequency[None, :]
    cosine = jnp.concatenate([jnp.cos(angles), jnp.cos(angles)], axis=-1)
    sine_vals = jnp.concatenate([jnp.sin(angles), jnp.sin(angles)], axis=-1)
    return (cosine, sine_vals)


def rotate(vector, cosine, sine_vals):
    half_rot = ROT // 2
    rotary_part = vector[..., :ROT]
    turned = jnp.concatenate([-rotary_part[..., half_rot:], rotary_part[..., :half_rot]], axis=-1)
    return jnp.concatenate([rotary_part * cosine + turned * sine_vals, vector[..., ROT:]], axis=-1)


def scatter_sum(part, dims=("seq", "rows")):
    for axis in dims:
        part = lax.psum_scatter(part, axis, scatter_dimension=0, tiled=True)
    return part


def local(
    states, cotangent, subsets, subset_weight, gain_attn, shift_attn, gain_ffn, shift_ffn,
    query_projection, pair_projection, output_projection, up_projection, down_projection,
):
    f32, bf16 = jnp.float32, jnp.bfloat16
    both = ("seq", "rows")
    here, length_here, D = states.shape
    T = here * length_here
    n_seq, n = lax.axis_size("seq"), lax.axis_size("seq") * lax.axis_size("rows")
    length = length_here * n_seq
    offset = lax.axis_index("seq") * length_here
    M = min(128, length_here)
    FF = up_projection.shape[1]
    scale = HD ** -0.5

    small = jnp.concatenate([query_projection, pair_projection, output_projection], axis=1)
    small = lax.all_gather(small, both, axis=0, tiled=True)
    big = jnp.stack([up_projection, down_projection.reshape(up_projection.shape)])
    big = lax.all_gather(big, both, axis=1, tiled=True)
    full_query, full_pair, full_output = small[:, :D], small[:, D:D + 2 * HD], small[:, D + 2 * HD:]
    full_up, full_down = big[0], big[1].reshape(FF, D)

    source = states.astype(f32).reshape(T, D)
    unit, inverse = layer_norm(source)
    attention_input = (unit * gain_attn + shift_attn).astype(bf16)
    feedforward_input = (unit * gain_ffn + shift_ffn).astype(bf16)
    table_rows = jnp.arange(subset_weight.shape[0], dtype=jnp.int32)
    row_scale = jnp.sum(
        jnp.where(table_rows[None, :] == subsets[:, None], subset_weight[None, :], 0.0), axis=1
    )
    upstream = (cotangent.astype(f32) * row_scale[:, None, None]).reshape(T, D)
    branch_grad = upstream.astype(bf16)

    rows_here = offset + jnp.arange(length_here, dtype=jnp.int32)
    cosine, sine_vals = rotary_tables(rows_here.astype(f32))
    query_pre = jnp.dot(attention_input, full_query, preferred_element_type=f32)
    pair_pre = jnp.dot(attention_input, full_pair, preferred_element_type=f32)
    pair_pre = pair_pre.reshape(here, length_here, 2 * HD)
    queries = rotate(
        query_pre.reshape(here, length_here, H, HD) * (scale / LN2),
        cosine[None, :, None, :], sine_vals[None, :, None, :],
    ).astype(bf16).reshape(T, D)
    key_values = jnp.concatenate(
        [rotate(pair_pre[..., :HD], cosine[None], sine_vals[None]), pair_pre[..., HD:]], axis=2
    ).astype(bf16)
    out_grad = lax.dot_general(
        branch_grad, full_output, (((1,), (1,)), ((), ())), preferred_element_type=f32
    ).astype(bf16)

    all_kv = lax.all_gather(key_values, "seq", axis=1, tiled=True)
    ones = jnp.ones((here, length, 3), bf16)
    zeros = jnp.zeros((here, length, HD - 3), bf16)
    ka = jnp.concatenate([all_kv[..., :HD], ones, zeros], axis=-1)
    va = jnp.concatenate([all_kv[..., HD:], ones, zeros], axis=-1)
    q_norm = jnp.max(jnp.sum(jnp.square(queries.astype(f32).reshape(T, H, HD)), axis=-1))
    k_norm = jnp.max(jnp.sum(jnp.square(all_kv[..., :HD].astype(f32)), axis=-1))
    wide = (q_norm * k_norm > 60.0 ** 2).astype(jnp.int32).reshape(1)

    tiles = length_here // M
    slot = jnp.arange(here * tiles, dtype=jnp.int32)
    attended, query_grad, pair_terms = attention(
        slot // tiles, offset + (slot % tiles) * M, wide, queries, out_grad, ka, va, M,
        tk=min(512, length))

    ffn_out, ffn_input_grad, grad_up, grad_down = ffn(
        feedforward_input, branch_grad, full_up, full_down)

    ffn_grads = jnp.concatenate(
        [grad_up.reshape(n, -1, D), grad_down.reshape(n, -1, D)], axis=1)
    ffn_grads = scatter_sum(ffn_grads)[0]
    half = ffn_grads.shape[0] // 2
    grad_up = ffn_grads[:half].reshape(-1, FF).astype(f32)
    grad_down = ffn_grads[half:].astype(f32)

    pair_terms = pair_terms.astype(bf16).reshape(here, 2 * HD, n_seq, length_here)
    pair_terms = jnp.moveaxis(pair_terms, 2, 0)
    arrived = lax.all_to_all(pair_terms, "seq", split_axis=0, concat_axis=0, tiled=True)
    pair_grad = jnp.swapaxes(arrived.astype(f32).sum(axis=0), 1, 2)

    residual = jnp.dot(attended, full_output, preferred_element_type=f32) + ffn_out
    layer_out = (source + residual).astype(bf16).reshape(here, length_here, D)
    grad_output = lax.dot_general(
        attended, branch_grad, (((0,), (0,)), ((), ())), preferred_element_type=f32)

    query_pre_grad = rotate(
        query_grad.reshape(here, length_here, H, HD) * scale,
        cosine[None, :, None, :], -sine_vals[None, :, None, :],
    ).reshape(T, D).astype(bf16)
    pair_pre_grad = jnp.concatenate(
        [rotate(pair_grad[..., :HD] * LN2, cosine[None], -sine_vals[None]), pair_grad[..., HD:]], axis=2
    ).reshape(T, 2 * HD).astype(bf16)
    pre_grad = jnp.concatenate([query_pre_grad, pair_pre_grad], axis=1)
    grad_qp = lax.dot_general(
        attention_input, pre_grad, (((0,), (0,)), ((), ())), preferred_element_type=f32)
    attn_input_grad = lax.dot_general(
        pre_grad, small[:, :D + 2 * HD], (((1,), (1,)), ((), ())), preferred_element_type=f32)

    sums = jnp.stack([
        jnp.sum(attn_input_grad * unit, axis=0), jnp.sum(attn_input_grad, axis=0),
        jnp.sum(ffn_input_grad * unit, axis=0), jnp.sum(ffn_input_grad, axis=0)], axis=1)
    sums = jnp.concatenate([sums, jnp.zeros((D, 124), f32)], axis=1)
    grad_states = upstream + norm_back(attn_input_grad, unit, inverse, gain_attn)
    grad_states = grad_states + norm_back(ffn_input_grad, unit, inverse, gain_ffn)
    grad_states = grad_states.astype(bf16).reshape(here, length_here, D)

    last = jnp.concatenate([grad_qp, grad_output, sums], axis=1).astype(bf16)
    last = lax.psum_scatter(last, both, scatter_dimension=0, tiled=True).astype(f32)
    at = D + 2 * HD
    vectors = last[:, at + D:]
    return (
        layer_out, grad_states,
        vectors[:, 0], vectors[:, 1], vectors[:, 2], vectors[:, 3],
        last[:, :D], last[:, D:at], last[:, at:at + D], grad_up, grad_down,
    )


def solution(mesh):
    from jax.sharding import PartitionSpec as P

    blocks, owned = P("rows", "seq", None), P(("seq", "rows"), None)
    vector = P(("seq", "rows"))
    return jax.shard_map(
        local,
        mesh=mesh,
        in_specs=(blocks, blocks, P("rows"), P(), P(), P(), P(), P()) + (owned,) * 5,
        out_specs=(blocks, blocks) + (vector,) * 4 + (owned,) * 5,
        check_vma=False,
    )
```

time: 1400 us -> 666 us (0.48)
  starting transfers between devices: 528 us -> 144 us
  waiting for transfers between devices: 508 us -> 269 us
  matrix products: 180 us -> 26.4 us
  Pallas kernels: 0 us -> 87.1 us
  blocking collectives: 83 us -> 0 us
  local copies, waits for them, and re-layouts: 41.3 us -> 73 us
    all_to_all x1, starting transfers between devices: 527 us -> 143 us  [local(): lax.all_to_all(pair_terms, 'seq', split_axis=0, concat_axis=0, tiled=True)]
    reduce_scatter x4 -> x3, waiting for transfers between devices: 283 us -> 115 us  [the longest x1 91.8 us: local(): lax.psum_scatter(last, both, scatter_dimension=0, tiled=True).astype(f32)]
    dot_general x22 -> x7, matrix products: 180 us -> 26.4 us  [the longest x1 6.85 us: local(): lax.dot_general(pre_grad, small[:, :D + 2 * HD], (((1,), (1,)), ((), ()))...]
    unnamed x11 -> x6, waiting for transfers between devices: 92.3 us -> 0.58 us
    pallas_call x0 -> x2, Pallas kernels: none -> 87.1 us  [the longest x1 46.1 us: attention(): pl.pallas_call(functools.partial(attn_kernel, M, tk, G), grid_spec=grid_s...]
    all_gather x1 -> x0, blocking collectives: 44 us -> none  [local(): lax.all_gather(pair_projection, ('seq', 'rows'), axis=0, tiled=True)]
    all_gather x5 -> x3, waiting for transfers between devices: 87.9 us -> 128 us  [the longest x1 74.9 us: local(): big = lax.all_gather(big, both, axis=1, tiled=True)]
    unnamed x1 -> x0, blocking collectives: 39 us -> none
  transfers between devices with their start and end apart: 11 -> 7, of which waited for: 6 -> 5; matrix products, arithmetic and copies ran while one was open for 18% -> 21% of each run, Pallas kernels for 0% -> 13%
where the time goes in v1:
time: 666 us; the launch traced here: 662 us
  waiting for transfers between devices  269 us (40%)
  starting transfers between devices  144 us (22%)
  Pallas kernels  87.1 us (13%)
  local copies, waits for them, and re-layouts  73 us (11%)
  other arithmetic  46.4 us (7%)
  matrix products  26.4 us (4%)
  between operations  16.3 us (2%)
    all_to_all x1, starting transfers between devices, local(): lax.all_to_all(pair_terms, 'seq', split_axis=0, concat_axis=0, tiled=True)  143 us
    reduce_scatter x1, waiting for transfers between devices, local(): lax.psum_scatter(last, both, scatter_dimension=0, tiled=True).astype(f32)  91.8 us
    all_gather x1, waiting for transfers between devices, local(): big = lax.all_gather(big, both, axis=1, tiled=True)  74.9 us
    all_gather x1, waiting for transfers between devices, local(): small = lax.all_gather(small, both, axis=0, tiled=True)  52.9 us
    pallas_call x1, Pallas kernels, attention(): pl.pallas_call(functools.partial(attn_kernel, M, tk, G), grid_spec=grid_s...  46.1 us
    pallas_call x1, Pallas kernels, ffn(): pl.pallas_call(functools.partial(ffn_kernel, C), grid=(FF // F,), in_spec...  41 us
    all_to_all x1, waiting for transfers between devices, local(): lax.all_to_all(pair_terms, 'seq', split_axis=0, concat_axis=0, tiled=True)  25.7 us
    reduce_scatter x2, waiting for transfers between devices, scatter_sum(): part = lax.psum_scatter(part, axis, scatter_dimension=0, tiled=True)  22.9 us
  transfers between devices with their start and end apart: 7, of which 5 were waited for; matrix products, arithmetic and copies ran while one was open for 21% of the time, Pallas kernels for 13%

profile of v1, /device:TPU:0, one launch (start us, length us, event | category | flops | bytes accessed | tf_op | source)
XLA Modules:
  0.0 661.5 jit_solution(3986436211964675795)
XLA Ops:
  19.2 52.9 %all-gather.4.cloned.1.call-done = bf16[768,1664]{1,0:T(8,128)(2,1)} async-done(((bf16[24,1664]{1,0:T(8,128)(2,1)}), bf16[768,1664]{1,0:T(8,128)(2,1)}) %all-gather.4.cloned.1.call-update) | async-done | bytes 2555920 | tf_op jit(solution)/shard_map/all_gather | solution.py:307
  81.6 74.9 %all-gather.8.cloned.1.call-done = bf16[2,768,3072]{2,1,0:T(8,128)(2,1)} async-done(((bf16[2,24,3072]{2,1,0:T(8,128)(2,1)}), bf16[2,768,3072]{2,1,0:T(8,128)(2,1)}) %all-gather.8.cloned.1.call-update) | async-done | bytes 9437200 | tf_op jit(solution)/shard_map/all_gather | solution.py:309
  156.5 8.3 %fusion.52 = (bf16[1,768,3072]{2,1,0:T(8,128)(2,1)}, bf16[768,3072]{1,0:T(8,128)(2,1)}) fusion(bf16[2,768,3072]{2,1,0:T(8,128)(2,1)} %all-gather.8.cloned.1.call-done), kind=kLoop, calls=%fused_computation.122 | loop fusion | bytes 18874368 | tf_op jit(solution)/shard_map/slice | solution.py:311
  164.8 8.5 %reshape_squeeze.3.down_ref = bf16[3072,768]{1,0:T(8,128)(2,1)} reshape(bf16[1,768,3072]{2,1,0:T(8,128)(2,1)} %get-tuple-element.43) | data formatting | bytes 9437184 | tf_op jit(solution)/shard_map/reshape;squeeze | solution.py:311
  173.3 41.0 %feedforward.1 = (f32[1024,768]{1,0:T(8,128)}, f32[1024,768]{1,0:T(8,128)}, bf16[768,3072]{1,0:T(8,128)(2,1)}, bf16[3072,768]{1,0:T(8,128)(2,1)}) custom-call(bf16[1024,768]{1,0:T(8,128)(2,1)} %fusion.18.x_ref, bf16[1024,768]{1,0:T(8,128)(2,1)} %bitcast_convert_fusion.b_ref, bf16[768,3072]{1,0:T(8,128)(2,1)} %get-tuple-element.44.up_ref, ...), custom_call_target="tpu_custom_call" | custom-call | flops 28991029248 | bytes 33554432 | tf_op jit(solution)/shard_map/feedforward/pallas_call | solution.py:223
  214.3 8.5 %reshape.249 = bf16[32,96,768]{2,1,0:T(8,128)(2,1)} reshape(bf16[768,3072]{1,0:T(8,128)(2,1)} %get-tuple-element.23) | data formatting | bytes 9437184 | tf_op jit(solution)/shard_map/reshape | solution.py:359
  222.8 7.6 %pad_maximum_fusion = bf16[32,192,768]{2,1,0:T(8,128)(2,1)} fusion(bf16[32,96,768]{2,1,0:T(8,128)(2,1)} %bitcast.122, bf16[32,96,768]{2,1,0:T(8,128)(2,1)} %reshape.249), kind=kLoop, calls=%fused_computation | loop fusion | flops 18874368 | bytes 18874368 | tf_op jit(solution)/shard_map/concatenate | solution.py:358
  236.0 3.7 convolution_multiply_fusion
  247.0 4.3 convolution_convert_fusion.g_ref
  251.3 2.8 multiply_reduce_fusion
  256.0 3.0 fusion.54
  259.1 3.4 maximum_maximum_fusion.1
  262.5 46.1 %attention.1 = (bf16[1024,768]{1,0:T(8,128)(2,1)}, f32[1024,768]{1,0:T(8,128)}, f32[2,128,4096]{2,1,0:T(8,128)}) custom-call(s32[8]{0:T(128)} %get-tuple-element.73.seq_ref, s32[8]{0:T(128)} %get-tuple-element.74.row_ref, s32[1]{0:T(128)} %bitcast.7.wide_ref, bf16[1024,768]{1,0:T(8,128)(2,1)} %copy.150.q_ref, ...), custom_call_target="tpu_custom_call" | custom-call | flops 19327352832 | bytes 16777216 | tf_op jit(solution)/shard_map/attention/pallas_call | solution.py:167
  312.6 143.3 %all-to-all-start = ((bf16[8,2,128,512]{3,2,1,0:T(8,128)(2,1)}), bf16[8,2,128,512]{3,2,1,0:T(8,128)(2,1)}, u32[]{:S(2)}, u32[]{:S(2)}) async-start(bf16[8,2,128,512]{3,2,1,0:T(8,128)(2,1)} %bitcast.118), calls=%async_computation | async-start | bytes 4194304 | tf_op jit(solution)/shard_map/all_to_all | solution.py:367
  456.0 3.7 broadcast_multiply_fusion
  459.7 3.7 copy.151
  463.4 5.6 mul.240
  479.0 25.7 %all-to-all-done = bf16[8,2,128,512]{3,2,1,0:T(8,128)(2,1)} async-done(((bf16[8,2,128,512]{3,2,1,0:T(8,128)(2,1)}), bf16[8,2,128,512]{3,2,1,0:T(8,128)(2,1)}, u32[]{:S(2)}, u32[]{:S(2)}) %all-to-all-start) | async-done | bytes 2097184 | tf_op jit(solution)/shard_map/all_to_all | solution.py:367
  508.8 6.8 %fusion.27 = (bf16[768]{0:T(1024)(128)(2,1)S(1)}, f32[1024]{0:T(1024)S(1)}, f32[1024]{0:T(1024)S(1)}, bf16[768]{0:T(1024)(128)(2,1)S(1)}, bf16[768]{0:T(1024)(12...) fusion(bf16[2,512,768]{2,1,0:T(8,128)(2,1)} %param.13, ...), kind=kOutput, calls=%fused_computation.38 | convolution fusion | flops 1426318336 | bytes 11112448 | tf_op jit(solution)/shard_map/dot_general | solution.py:385
  517.7 3.4 fusion.26
  523.1 3.0 concatenate.75
  528.0 4.8 fusion.29
  532.8 91.8 %reduce-scatter.4.cloned.1.call-done = bf16[24,1792]{1,0:T(8,128)(2,1)} async-done(((bf16[768,1792]{1,0:T(8,128)(2,1)}), bf16[24,1792]{1,0:T(8,128)(2,1)}) %reduce-scatter.4.cloned.1.call-update) | async-done | bytes 86032 | tf_op jit(solution)/shard_map/reduce_scatter | solution.py:397
  629.0 22.9 %reduce-scatter.8.cloned.1.call-done = bf16[1,192,768]{2,1,0:T(8,128)(2,1)} async-done(((bf16[4,192,768]{2,1,0:T(8,128)(2,1)}), bf16[1,192,768]{2,1,0:T(8,128)(2,1)}) %reduce-scatter.8.cloned.1.call-update) | async-done | bytes 294928 | tf_op jit(solution)/shard_map/reduce_scatter | solution.py:287
  (139 shorter events, 65.6 us)
Async XLA Ops:
  7.2 6.2 copy-start
  7.2 6.8 %copy-start.19 = (s32[2]{0:T(128)S(1)}, s32[2]{0:T(128)}, u32[]{:S(2)}) copy-start(s32[2]{0:T(128)} %param.15) | copy-start | bytes 28
  7.2 6.8 %copy-start.18 = (f32[22]{0:T(128)S(1)}, f32[22]{0:T(128)}, u32[]{:S(2)}) copy-start(f32[22]{0:T(128)} %param.16) | copy-start | bytes 268
  7.2 7.2 %copy-start.13 = (f32[768]{0:T(1024)S(1)}, f32[768]{0:T(1024)}, u32[]{:S(2)}) copy-start(f32[768]{0:T(1024)} %param.19) | copy-start | bytes 9220
  7.2 7.2 %copy-start.14 = (f32[768]{0:T(1024)S(1)}, f32[768]{0:T(1024)}, u32[]{:S(2)}) copy-start(f32[768]{0:T(1024)} %param.20) | copy-start | bytes 9220
  7.2 64.8 %all-gather.4.cloned.1.call-start = ((), (), s32[]{:S(2)}) async-start(), calls=%async_computation.4 | async-start | bytes 2635776 | tf_op jit(solution)/shard_map/all_gather | solution.py:307
  8.8 147.7 %all-gather.8.cloned.1.call-start = ((), (), s32[]{:S(2)}) async-start(), calls=%async_computation.6 | async-start | bytes 9732096 | tf_op jit(solution)/shard_map/all_gather | solution.py:309
  11.6 239.8 %all-gather.6.cloned.1.call-start = ((), (), s32[]{:S(2)}) async-start(), calls=%async_computation.5 | async-start | bytes 2359296 | tf_op jit(solution)/shard_map/all_gather | solution.py:340
  17.9 54.2 %copy-start.15 = (f32[768]{0:T(1024)S(1)}, f32[768]{0:T(1024)}, u32[]{:S(2)}) copy-start(f32[768]{0:T(1024)} %param.18) | copy-start | bytes 9220
  17.9 54.2 %copy-start.16 = (f32[768]{0:T(1024)S(1)}, f32[768]{0:T(1024)}, u32[]{:S(2)}) copy-start(f32[768]{0:T(1024)} %param.17) | copy-start | bytes 9220
  81.4 444.8 %reduce-scatter.6.cloned.1.call-start = ((), (), s32[]{:S(2)}) async-start(), calls=%async_computation.8 | async-start | bytes 10616832 | tf_op jit(solution)/shard_map/reduce_scatter | solution.py:287
  312.6 192.1 %all-to-all-start = ((bf16[8,2,128,512]{3,2,1,0:T(8,128)(2,1)}), bf16[8,2,128,512]{3,2,1,0:T(8,128)(2,1)}, u32[]{:S(2)}, u32[]{:S(2)}) async-start(bf16[8,2,128,512]{3,2,1,0:T(8,128)(2,1)} %bitcast.118), calls=%async_computation | async-start | bytes 4194304 | tf_op jit(solution)/shard_map/all_to_all | solution.py:367
  455.9 168.7 %reduce-scatter.4.cloned.1.call-start = ((), (), s32[]{:S(2)}) async-start(), calls=%async_computation.7 | async-start | bytes 2838528 | tf_op jit(solution)/shard_map/reduce_scatter | solution.py:397
  469.0 2.7 copy-start.3
  469.0 3.3 slice-start
  472.9 3.7 copy-start.6
  472.9 3.7 copy-start.20
  508.7 6.9 %copy-start.10 = (bf16[1024,128]{0,1:T(8,128)(2,1)}, bf16[1024,128]{0,1:T(8,128)(2,1)S(1)}, u32[]{:S(2)}) copy-start(bf16[1024,128]{0,1:T(8,128)(2,1)S(1)} %copy.159) | copy-start | bytes 786436
  508.8 8.9 %copy-start.1 = (bf16[2,512,768]{2,1,0:T(8,128)(2,1)S(1)}, bf16[2,512,768]{2,1,0:T(8,128)(2,1)}, u32[]{:S(2)}) copy-start(bf16[2,512,768]{2,1,0:T(8,128)(2,1)} %param.13) | copy-start | bytes 4718596
  508.8 8.9 %copy-start.4 = (f32[1024,768]{1,0:T(8,128)S(1)}, f32[1024,768]{1,0:T(8,128)}, u32[]{:S(2)}) copy-start(f32[1024,768]{1,0:T(8,128)} %get-tuple-element.22) | copy-start | bytes 9437188
  508.8 8.9 %copy-start.17 = (f32[768]{0:T(1024)S(1)}, f32[768]{0:T(1024)}, u32[]{:S(2)}) copy-start(f32[768]{0:T(1024)} %param.17) | copy-start | bytes 9220
  517.7 3.4 copy-start.5
  517.7 3.4 copy-start.11
  526.1 125.8 %reduce-scatter.8.cloned.1.call-start = ((), (), s32[]{:S(2)}) async-start(), calls=%async_computation.9 | async-start | bytes 1474560 | tf_op jit(solution)/shard_map/reduce_scatter | solution.py:287
  (6 other events, 9.9 us)
Sparse Core Ops, SparseCore 0:
  11.5 60.5 all-gather.3
  75.5 80.9 all-gather.7
  159.3 47.8 all-gather.5
  230.5 162.0 reduce-scatter.5
  526.2 98.3 reduce-scatter.3
  627.2 24.6 reduce-scatter.7

commit v2 on v1

v2 whole, which is shorter than its diff:
```python
import functools
import jax
import jax.numpy as jnp
import numpy as np
from jax import lax
from jax.experimental import pallas as pl
from jax.experimental.pallas import tpu as pltpu

H = 12
HD = 64
LN2 = 0.6931471805599453


def dot(a, b, ca, cb):
    return lax.dot_general(a, b, (((ca,), (cb,)), ((), ())), preferred_element_type=jnp.float32)


def three_parts(x):
    hi = x.astype(jnp.bfloat16)
    rest = x - hi.astype(jnp.float32)
    mid = rest.astype(jnp.bfloat16)
    low = (rest - mid.astype(jnp.float32)).astype(jnp.bfloat16)
    return hi, mid, low


ROT = 16


def turn_tables(length, M):
    frequency = 10000.0 ** (-2.0 * np.arange(ROT // 2) / ROT)
    lanes = np.zeros(HD)
    lanes[:ROT] = np.concatenate([frequency, frequency])
    lanes = np.concatenate([lanes, lanes])

    def table(places):
        angles = places[:, None] * lanes[None, :]
        return np.concatenate([np.cos(angles), np.sin(angles)], axis=1).astype(np.float32)

    return table(np.arange(M)), table(np.arange(0, length, M))


def turn_factors(near, far):
    cn, sn, cf, sf = near[:, :128], near[:, 128:], far[:, :128], far[:, 128:]
    sine = sf * cn + cf * sn
    lane = lax.broadcasted_iota(jnp.int32, sine.shape, 1) & (HD - 1)
    low = jnp.where(lane < ROT // 2, sine, 0.0)
    high = jnp.where((lane >= ROT // 2) & (lane < ROT), sine, 0.0)
    return cf * cn - sf * sn, low, high


def turn(z, cosine, low, high):
    return z * cosine - pltpu.roll(z, 120, 1) * low + pltpu.roll(z, 8, 1) * high


def turn_back(z, cosine, low, high):
    return z * cosine + pltpu.roll(z, 120, 1) * low - pltpu.roll(z, 8, 1) * high


def attn_kernel(
    M, tk, own, first_call,
    slot_ref, seq_ref, row_ref, on_ref,
    q_ref, g_ref, other_ref, near_ref, far_ref, kv_ref, *refs,
):
    if not first_call:
        refs = refs[2:]
        before_ref, refs = refs[0], refs[1:]
    o_ref, dq_ref, dkv_ref = refs[:3]
    ka, va, qs, gs, qt, gt, stash, oacc, dqacc, top, limit = refs[3:]
    t = pl.program_id(0)
    seq = seq_ref[t]
    row0 = row_ref[t]
    G = 4 * M
    groups = [slice(g * G, (g + 1) * G) for g in range(H // 4)]
    heads = [slice(h * M, (h + 1) * M) for h in range(H)]
    f32, bf16 = jnp.float32, jnp.bfloat16
    parts_, count, block, _ = kv_ref.shape

    @pl.when(t == 0)
    def _():
        if first_call:
            dkv_ref[...] = jnp.zeros_like(dkv_ref)
        else:
            dkv_ref[...] = before_ref[...]
        lane = lax.broadcasted_iota(jnp.int32, (block, HD), 1)
        ones = jnp.where(lane < 3, 1.0, 0.0).astype(bf16)

        def arrange(i, most):
            for s in range(count):
                kv = kv_ref[i, s]
                rows = pl.ds(pl.multiple_of(i * block, block), block)
                ka[s, rows, :] = jnp.concatenate([kv[:, :HD], ones], axis=1)
                va[s, rows, :] = jnp.concatenate([kv[:, HD:], ones], axis=1)
                k = kv[:, :HD].astype(f32)
                most = jnp.maximum(most, jnp.max(jnp.sum(k * k, axis=1, keepdims=True)))
            return most

        limit[0] = lax.fori_loop(0, parts_, arrange, jnp.float32(0.0))

    @pl.when(on_ref[t] != 0)
    def _():
        taken = slot_ref[t] >= own
        q_in = q_ref[...] if other_ref is None else jnp.where(taken, other_ref[0, 0], q_ref[...])
        g_in = g_ref[...] if other_ref is None else jnp.where(taken, other_ref[0, 1], g_ref[...])
        for h in range(H):
            qs[heads[h], :HD] = q_in[:, h * HD:(h + 1) * HD]
            qs[heads[h], HD:] = jnp.zeros((M, 128 - HD), bf16)
        oacc[...] = jnp.zeros_like(oacc)
        dqacc[...] = jnp.zeros_like(dqacc)
        n_full = row0 // tk

        def keys(ref, kt):
            return ref[seq, pl.ds(pl.multiple_of(kt * tk, tk), tk), :]

        def allowed(kt):
            row = row0 + (lax.broadcasted_iota(jnp.int32, (G, tk), 0) & (M - 1))
            col = kt * tk + lax.broadcasted_iota(jnp.int32, (G, tk), 1)
            return col <= row

        def scores(kt, r, masked):
            s = dot(qs[r, :], keys(ka, kt), 1, 1)
            if masked:
                s = jnp.where(allowed(kt), s, -1e30)
            return s

        most = jnp.float32(0.0)
        for r in groups:
            q = qs[r, :].astype(f32)
            most = jnp.maximum(most, jnp.max(jnp.sum(q * q, axis=1, keepdims=True)))

        @pl.when(most * limit[0] > 3600.0)
        def _():
            top[...] = jnp.full_like(top, -1e30)

            def peak(kt, masked):
                for r in groups:
                    s = scores(kt, r, masked)
                    part = s[:, :128]
                    for j in range(1, tk // 128):
                        part = jnp.maximum(part, s[:, j * 128:(j + 1) * 128])
                    top[r, :] = jnp.maximum(top[r, :], part)

            lax.fori_loop(0, n_full, lambda kt, _: (peak(kt, False), 0)[1], 0)
            peak(n_full, True)
            for r in heads:
                best = -jnp.max(top[r, :], axis=1, keepdims=True)
                for j, part in enumerate(three_parts(best)):
                    qs[r, HD + j:HD + j + 1] = part

        def first(kt, masked):
            v = keys(va, kt)
            for r in groups:
                e = jnp.exp2(scores(kt, r, masked)).astype(bf16)
                stash[kt, r, :] = e
                oacc[r, :] += dot(e, v, 1, 0)

        lax.fori_loop(0, n_full, lambda kt, _: (first(kt, False), 0)[1], 0)
        first(n_full, True)

        for p in range(H // 2):
            outs = []
            for h in (2 * p, 2 * p + 1):
                r = heads[h]
                acc = oacc[r, :]
                inverse = 1.0 / acc[:, HD:HD + 1]
                out = acc[:, :HD] * inverse
                outs.append(out)
                low = (g_in[:, h * HD:(h + 1) * HD].astype(f32) * inverse).astype(bf16)
                delta = -jnp.sum(low.astype(f32) * out, axis=1, keepdims=True)
                gs[r, :] = jnp.concatenate(
                    [low, *three_parts(delta), jnp.zeros((M, 128 - HD - 3), bf16)], axis=1)
            o_ref[:, p * 128:(p + 1) * 128] = jnp.concatenate(outs, axis=1).astype(bf16)
        qt[...] = qs[...].T
        gt[...] = gs[...].T

        def second(kt):
            k = keys(ka, kt)
            v = keys(va, kt)
            dk = jnp.zeros((HD, tk), f32)
            dv = jnp.zeros((HD, tk), f32)
            for r in groups:
                e = stash[kt, r, :]
                slope = (e.astype(f32) * dot(gs[r, :], v, 1, 1)).astype(bf16)
                dqacc[r, :] += dot(slope, k, 1, 0)
                dk = dk + dot(qt[:HD, r], slope, 1, 0)
                dv = dv + dot(gt[:HD, r], e, 1, 0)
            c = pl.ds(pl.multiple_of(kt * tk, tk), tk)
            dkv_ref[seq, :HD, c] += dk
            dkv_ref[seq, HD:, c] += dv

        lax.fori_loop(0, n_full + 1, lambda kt, _: (second(kt), 0)[1], 0)
        factors = turn_factors(near_ref[...], far_ref[pl.ds(row0 // M, 1), :])
        for p in range(H // 2):
            z = jnp.concatenate([dqacc[heads[h], :HD] for h in (2 * p, 2 * p + 1)], axis=1)
            dq_ref[:, p * 128:(p + 1) * 128] = (turn_back(z, *factors) * HD ** -0.5).astype(bf16)


def attention(tables, q, g, others, kv, M, tk, most, before=None):
    width = H * HD
    steps = tables[0].shape[0]
    own = q.shape[0] // M
    parts, S, block, _ = kv.shape
    L = parts * block
    near, far = turn_tables(L, M)
    whole = pl.Buffered(1)
    tile = pl.BlockSpec((M, width), lambda t, slot, *_: (slot[t], 0))
    near_spec = pl.BlockSpec(near.shape, lambda t, *_: (0, 0), pipeline_mode=whole)
    far_spec = pl.BlockSpec(far.shape, lambda t, *_: (0, 0), pipeline_mode=whole)
    mine = pl.BlockSpec((M, width), lambda t, slot, *_: (jnp.minimum(slot[t], own - 1), 0))
    taken = pl.BlockSpec((1, 2, M, width), lambda t, slot, *_: (jnp.maximum(slot[t] - own, 0), 0, 0, 0))
    sums = pl.BlockSpec((S, 128, L), lambda t, *_: (0, 0, 0), pipeline_mode=whole)
    anywhere = pl.BlockSpec(memory_space=pl.ANY)
    bf16, f32 = jnp.bfloat16, jnp.float32
    pairs = steps * M * H * L // 3
    kernel = functools.partial(attn_kernel, M, tk, own, before is None)
    operands, specs = [q, g], [mine, mine]
    if others is None:
        inner = kernel
        kernel = lambda a, b, c, d, q_ref, g_ref, *refs: inner(a, b, c, d, q_ref, g_ref, None, *refs)
    else:
        operands, specs = operands + [others], specs + [taken]
    operands += [near, far, kv]
    specs += [near_spec, far_spec, pl.BlockSpec(kv.shape, lambda t, *_: (0, 0, 0, 0), pipeline_mode=whole)]
    aliases = {}
    if before is not None:
        aliases = {4 + len(operands) + i: i for i in range(3)}
        operands, specs = operands + list(before), specs + [anywhere, anywhere, sums]
    slots = jax.ShapeDtypeStruct(((own + most) * M, width), bf16)
    return pl.pallas_call(
        kernel,
        grid_spec=pltpu.PrefetchScalarGridSpec(
            num_scalar_prefetch=4,
            grid=(steps,),
            in_specs=specs,
            out_specs=[tile, tile, sums],
            scratch_shapes=[
                pltpu.VMEM((S, L, 128), bf16),
                pltpu.VMEM((S, L, 128), bf16),
                pltpu.VMEM((H * M, 128), bf16),
                pltpu.VMEM((H * M, 128), bf16),
                pltpu.VMEM((128, H * M), bf16),
                pltpu.VMEM((128, H * M), bf16),
                pltpu.VMEM((L // tk, H * M, tk), bf16),
                pltpu.VMEM((H * M, 128), f32),
                pltpu.VMEM((H * M, 128), f32),
                pltpu.VMEM((H * M, 128), f32),
                pltpu.SMEM((1,), f32),
            ],
        ),
        out_shape=[slots, slots, jax.ShapeDtypeStruct((S, 128, L), f32)],
        input_output_aliases=aliases,
        compiler_params=pltpu.CompilerParams(vmem_limit_bytes=58 << 20),
        cost_estimate=pl.CostEstimate(flops=1 << 20, bytes_accessed=1 << 16, transcendentals=0),
        name="attention",
    )(*tables, *operands)


def gelu_both(x):
    z = jnp.abs(x) * 0.7071067811865476
    s = 1.0 / (1.0 + 0.3275911 * z)
    poly = s * (0.127414796 + s * (-0.142248368 + s * (0.710706871 + s * (-0.7265760135 + s * 0.5307027145))))
    bell = jnp.exp(-z * z)
    tail = poly * bell
    phi = jnp.where(x >= 0.0, 1.0 - tail, tail)
    return x * phi, phi + x * (bell * 0.3989422804014327)


def ffn_kernel(C, x_ref, b_ref, up_ref, down_ref, out_ref, dx_ref, gup_ref, gdown_ref, act_s, ug_s):
    f = pl.program_id(0)
    T = x_ref.shape[0]

    @pl.when(f == 0)
    def _():
        out_ref[...] = jnp.zeros_like(out_ref)
        dx_ref[...] = jnp.zeros_like(dx_ref)

    up = up_ref[...]
    down = down_ref[...]
    for c in range(T // C):
        r = slice(c * C, (c + 1) * C)
        u = dot(x_ref[r, :], up, 1, 0)
        a = dot(b_ref[r, :], down, 1, 1)
        act, slope = gelu_both(u)
        act = act.astype(jnp.bfloat16)
        ug = (a * slope).astype(jnp.bfloat16)
        act_s[r, :] = act
        ug_s[r, :] = ug
        out_ref[r, :] += dot(act, down, 1, 0)
        dx_ref[r, :] += dot(ug, up, 1, 1)
    gup_ref[...] = dot(x_ref[...], ug_s[...], 0, 0).astype(gup_ref.dtype)
    gdown_ref[...] = dot(act_s[...], b_ref[...], 0, 0).astype(gdown_ref.dtype)


def ffn(x, b, up, down, F=512, C=256, wire=jnp.bfloat16):
    T, D = x.shape
    FF = up.shape[1]
    C = min(C, T)
    f32, bf16 = jnp.float32, jnp.bfloat16
    whole = lambda f: (0, 0)
    return pl.pallas_call(
        functools.partial(ffn_kernel, C),
        grid=(FF // F,),
        in_specs=[
            pl.BlockSpec((T, D), whole, pipeline_mode=pl.Buffered(1)),
            pl.BlockSpec((T, D), whole, pipeline_mode=pl.Buffered(1)),
            pl.BlockSpec((D, F), lambda f: (0, f)),
            pl.BlockSpec((F, D), lambda f: (f, 0)),
        ],
        out_specs=[
            pl.BlockSpec((T, D), whole, pipeline_mode=pl.Buffered(1)),
            pl.BlockSpec((T, D), whole, pipeline_mode=pl.Buffered(1)),
            pl.BlockSpec((D, F), lambda f: (0, f)),
            pl.BlockSpec((F, D), lambda f: (f, 0)),
        ],
        out_shape=[
            jax.ShapeDtypeStruct((T, D), f32),
            jax.ShapeDtypeStruct((T, D), f32),
            jax.ShapeDtypeStruct((D, FF), wire),
            jax.ShapeDtypeStruct((FF, D), wire),
        ],
        scratch_shapes=[pltpu.VMEM((T, F), bf16), pltpu.VMEM((T, F), bf16)],
        compiler_params=pltpu.CompilerParams(vmem_limit_bytes=56 << 20),
        cost_estimate=pl.CostEstimate(flops=12 * T * D * FF, bytes_accessed=32 << 20, transcendentals=T * FF),
        name="feedforward",
    )(x, b, up, down)


def ffn_packed_kernel(C, n_rows, x_ref, b_ref, up_ref, down_ref, out_ref, dx_ref, grads_ref, act_s, ug_s, wide, ups):
    f = pl.program_id(0)
    T, D = x_ref.shape
    groups, each, _, count, _ = up_ref.shape
    tiles = ups.shape[0]
    n = groups * each
    owned = D // n
    f32, bf16 = jnp.float32, jnp.bfloat16

    @pl.when(f == 0)
    def _():
        out_ref[...] = jnp.zeros_like(out_ref)
        dx_ref[...] = jnp.zeros_like(dx_ref)

        def unpack(d, _):
            part = up_ref[d // each, lax.rem(d, each), 0].astype(f32)
            for j in range(tiles):
                at = pl.ds(pl.multiple_of(d * owned, 8), owned)
                wide[j, at, :] = part[j * owned:(j + 1) * owned]
            return 0

        lax.fori_loop(0, n, unpack, 0)
        for j in range(tiles):
            ups[j] = wide[j].astype(bf16)

    up = ups[f]
    down = down_ref[...].reshape(D, D)
    for c in range(T // C):
        r = slice(c * C, (c + 1) * C)
        u = dot(x_ref[r, :], up, 1, 0)
        a = dot(b_ref[r, :], down, 1, 1)
        act, slope = gelu_both(u)
        act = act.astype(bf16)
        ug = (a * slope).astype(bf16)
        act_s[r, :] = act
        ug_s[r, :] = ug
        out_ref[r, :] += dot(act, down, 1, 0)
        dx_ref[r, :] += dot(ug, up, 1, 1)
    wide[f] = dot(x_ref[...], ug_s[...], 0, 0)
    grad_down = dot(act_s[...], b_ref[...], 0, 0).astype(bf16)
    for k in range(each):
        at = f * each + k
        grads_ref[lax.rem(at, n_rows), at // n_rows, count:] = grad_down[k * count:(k + 1) * count]

    @pl.when(f == tiles - 1)
    def _():
        def pack(d, _):
            at = pl.ds(pl.multiple_of(d * owned, 8), owned)
            part = jnp.concatenate([wide[j, at, :] for j in range(tiles)], axis=0)
            grads_ref[lax.rem(d, n_rows), d // n_rows, :count] = part.astype(bf16)
            return 0

        lax.fori_loop(0, n, pack, 0)


def ffn_packed(x, b, packed, n_seq, n_rows, C=256):
    T, D = x.shape
    n, count = packed.shape[0], packed.shape[1] // 2
    FF = n * count
    tiles = FF // D
    each = n // tiles
    packed = packed.reshape(tiles, each, 2, count, D)
    f32, bf16 = jnp.float32, jnp.bfloat16
    once = pl.Buffered(1)
    whole = lambda f: (0, 0)
    return pl.pallas_call(
        functools.partial(ffn_packed_kernel, C, n_rows),
        grid=(tiles,),
        in_specs=[
            pl.BlockSpec((T, D), whole, pipeline_mode=once),
            pl.BlockSpec((T, D), whole, pipeline_mode=once),
            pl.BlockSpec((tiles, each, 1, count, D), lambda f: (0, 0, 0, 0, 0), pipeline_mode=once),
            pl.BlockSpec((1, each, 1, count, D), lambda f: (f, 0, 1, 0, 0)),
        ],
        out_specs=[
            pl.BlockSpec((T, D), whole, pipeline_mode=once),
            pl.BlockSpec((T, D), whole, pipeline_mode=once),
            pl.BlockSpec((n_rows, n_seq, 2 * count, D), lambda f: (0, 0, 0, 0), pipeline_mode=once),
        ],
        out_shape=[
            jax.ShapeDtypeStruct((T, D), f32),
            jax.ShapeDtypeStruct((T, D), f32),
            jax.ShapeDtypeStruct((n_rows, n_seq, 2 * count, D), bf16),
        ],
        scratch_shapes=[
            pltpu.VMEM((T, D), bf16), pltpu.VMEM((T, D), bf16),
            pltpu.VMEM((tiles, D, D), f32), pltpu.VMEM((tiles, D, D), bf16),
        ],
        compiler_params=pltpu.CompilerParams(vmem_limit_bytes=60 << 20),
        cost_estimate=pl.CostEstimate(flops=1 << 20, bytes_accessed=1 << 16, transcendentals=0),
        name="feedforward",
    )(x, b, packed, packed)


MESH = pl.DeviceIdType.MESH


def bits_of(n_seq, n_rows):
    high = [("seq", 1 << b) for b in reversed(range(n_seq.bit_length() - 1))]
    return high + [("rows", 1 << b) for b in reversed(range(n_rows.bit_length() - 1))]


def place(bits):
    return [lax.rem(lax.axis_index(axis) // weight, 2) for axis, weight in bits]


def partner(bit):
    axis, weight = bit
    mine = lax.axis_index(axis)
    return {axis: mine + weight - 2 * weight * lax.rem(mine // weight, 2)}


def greet(bits):
    barrier = pltpu.get_barrier_semaphore()
    for bit in bits:
        pl.semaphore_signal(barrier, inc=1, device_id=partner(bit), device_id_type=MESH)
    pl.semaphore_wait(barrier, len(bits))


def routes(bits):
    n = len(bits)
    one = list(range(n))
    other = list(range(n))
    near = max(i for i in range(n) if bits[i][0] == "seq")
    if near + 1 < n - 1:
        other[near], other[near + 1] = other[near + 1], other[near]
    return one, other


def gather_kernel(bits, count, *refs):
    shards, fulls = refs[:count], refs[count:2 * count]
    own_sem, send_sem, recv_sem = refs[2 * count:]
    me = place(bits)
    orders = routes(bits)
    locals_ = []
    for a in range(count):
        copy = pltpu.make_async_copy(shards[a], fulls[a].at[tuple(me)], own_sem.at[a])
        copy.start()
        locals_.append(copy)
    greet(bits)
    for copy in locals_:
        copy.wait()
    held = [set(), set()]
    for stage in range(len(bits)):
        copies = []
        for half in (0, 1):
            b = orders[half][stage]
            for a in range(count):
                rows = shards[a].shape[0] // 2
                where = tuple(slice(None) if i in held[half] else me[i] for i in range(len(bits)))
                piece = fulls[a].at[where + (pl.ds(half * rows, rows),)]
                copy = pltpu.make_async_remote_copy(
                    src_ref=piece, dst_ref=piece,
                    send_sem=send_sem.at[a, half, stage], recv_sem=recv_sem.at[a, half, stage],
                    device_id=partner(bits[b]), device_id_type=MESH)
                copy.start()
                copies.append(copy)
            held[half].add(b)
        for copy in copies:
            copy.wait()


def gather(shards, n_seq, n_rows, collective_id):
    bits = bits_of(n_seq, n_rows)
    count = len(shards)
    outs = pl.pallas_call(
        functools.partial(gather_kernel, bits, count),
        out_shape=[jax.ShapeDtypeStruct((2,) * len(bits) + s.shape, s.dtype) for s in shards],
        in_specs=[pl.BlockSpec(memory_space=pl.ANY)] * count,
        out_specs=[pl.BlockSpec(memory_space=pl.ANY)] * count,
        scratch_shapes=[
            pltpu.SemaphoreType.DMA((count,)),
            pltpu.SemaphoreType.DMA((count, 2, len(bits))),
            pltpu.SemaphoreType.DMA((count, 2, len(bits))),
        ],
        compiler_params=pltpu.CompilerParams(collective_id=collective_id, has_side_effects=True),
        name="gather",
    )(*shards)
    return [o.reshape((n_seq * n_rows,) + s.shape) for o, s in zip(outs, shards)]


def scatter_kernel(bits, width, x_ref, out_ref, *refs):
    n = len(bits)
    send = refs[:n]
    recv = refs[n:2 * n]
    acc = refs[2 * n:3 * n]
    send_sem, recv_sem = refs[3 * n:]
    rows = x_ref.shape[1]
    f32, bf16 = jnp.float32, jnp.bfloat16
    me = place(bits)
    orders = [list(reversed(o)) for o in routes(bits)]
    greet(bits)

    def spread(half, stage, j, own):
        left = sorted(orders[half][stage:])
        b = orders[half][stage]
        rest = [i for i in left if i != b]
        index = 0
        for i in left:
            if i == b:
                bit = me[b] if own else 1 - me[b]
            else:
                bit = lax.rem(j // (1 << (len(rest) - 1 - rest.index(i))), 2)
            index = index * 2 + bit
        return index

    def block(half, stage, at):
        if stage == 0:
            low = x_ref[at, :, half * 2 * width:half * 2 * width + width]
            high = x_ref[at, :, half * 2 * width + width:(half + 1) * 2 * width]
            return jnp.concatenate([low, high], axis=0)
        return acc[stage - 1][half, at]

    for stage in range(n):
        size = 1 << (n - 1 - stage)
        copies = []
        for half in (0, 1):
            def fill(j, _, half=half, stage=stage):
                send[stage][half, j] = block(half, stage, spread(half, stage, j, False)).astype(bf16)
                return 0
            lax.fori_loop(0, size, fill, 0)
            copy = pltpu.make_async_remote_copy(
                src_ref=send[stage].at[half], dst_ref=recv[stage].at[half],
                send_sem=send_sem.at[half, stage], recv_sem=recv_sem.at[half, stage],
                device_id=partner(bits[orders[half][stage]]), device_id_type=MESH)
            copy.start()
            copies.append(copy)
        for half in (0, 1):
            copies[half].wait()

            def add(j, _, half=half, stage=stage):
                own = block(half, stage, spread(half, stage, j, True))
                acc[stage][half, j] = own + recv[stage][half, j].astype(f32)
                return 0
            lax.fori_loop(0, size, add, 0)
    for half in (0, 1):
        total = acc[n - 1][half, 0]
        out_ref[:, half * 2 * width:half * 2 * width + width] = total[:rows]
        out_ref[:, half * 2 * width + width:(half + 1) * 2 * width] = total[rows:]


def scatter(x, n_seq, n_rows, collective_id):
    bits = bits_of(n_seq, n_rows)
    n, rows, columns = x.shape
    width = columns // 4
    shapes = [(2, 1 << (len(bits) - 1 - s), 2 * rows, width) for s in range(len(bits))]
    return pl.pallas_call(
        functools.partial(scatter_kernel, bits, width),
        out_shape=jax.ShapeDtypeStruct((rows, columns), jnp.float32),
        in_specs=[pl.BlockSpec(memory_space=pltpu.VMEM)],
        out_specs=pl.BlockSpec(memory_space=pltpu.VMEM),
        scratch_shapes=[pltpu.VMEM(s, jnp.bfloat16) for s in shapes]
        + [pltpu.VMEM(s, jnp.bfloat16) for s in shapes]
        + [pltpu.VMEM(s, jnp.float32) for s in shapes]
        + [pltpu.SemaphoreType.DMA((2, len(bits))), pltpu.SemaphoreType.DMA((2, len(bits)))],
        compiler_params=pltpu.CompilerParams(
            collective_id=collective_id, has_side_effects=True, vmem_limit_bytes=40 << 20),
        name="scatter",
    )(x)


def front_kernel(
    bits, here, M, chunk,
    x_ref, c_ref, scale_ref, norm_ref, near_ref, far_ref, sq_ref, pr_ref,
    q_ref, g_ref, kv_ref, xa_ref, xf_ref, b_ref, wide_ref, wp,
    sq_all, pr_all, stage_q, stage_o, stage_p,
    own_sem, send_sem, recv_sem, kv_send, kv_recv,
):
    f32, bf16 = jnp.float32, jnp.bfloat16
    T, D = x_ref.shape
    n = len(bits)
    me = place(bits)
    seq_bits = [i for i in range(n) if bits[i][0] == "seq"]
    own = [pltpu.make_async_copy(s, d.at[tuple(me)], own_sem.at[i])
           for i, (s, d) in enumerate(((sq_ref, sq_all), (pr_ref, pr_all)))]
    for copy in own:
        copy.start()
    greet(bits)
    for copy in own:
        copy.wait()

    def normalize(i):
        r = slice(i * chunk, (i + 1) * chunk)
        x = x_ref[r, :].astype(f32)
        x = x - jnp.mean(x, axis=1, keepdims=True)
        unit = x * lax.rsqrt(jnp.mean(x * x, axis=1, keepdims=True) + 1e-05)
        xa_ref[r, :] = (unit * norm_ref[0:1, :] + norm_ref[1:2, :]).astype(bf16)
        xf_ref[r, :] = (unit * norm_ref[2:3, :] + norm_ref[3:4, :]).astype(bf16)
        part = i * chunk // (T // here)
        b_ref[r, :] = (c_ref[r, :].astype(f32) * scale_ref[part:part + 1, :]).astype(bf16)

    orders = routes(bits)
    held = [set(), set()]
    chunks = T // chunk
    for stage in range(n):
        copies = []
        for half in (0, 1):
            b = orders[half][stage]
            for a, full in enumerate((pr_all, sq_all)):
                rows = full.shape[-2]
                if half == 0:
                    part = pl.ds(0, rows // 32 * 16)
                else:
                    part = pl.ds(rows // 32 * 16, rows - rows // 32 * 16)
                where = tuple(slice(None) if i in held[half] else me[i] for i in range(n))
                piece = full.at[where + (part,)]
                copy = pltpu.make_async_remote_copy(
                    src_ref=piece, dst_ref=piece,
                    send_sem=send_sem.at[a, half, stage], recv_sem=recv_sem.at[a, half, stage],
                    device_id=partner(bits[b]), device_id_type=MESH)
                copy.start()
                copies.append(copy)
            held[half].add(b)
        for i in range(chunks):
            if i % n == stage:
                normalize(i)
        for copy in copies:
            copy.wait()

    owned = D // (1 << n)
    for d in range(1 << n):
        at = tuple((d >> (n - 1 - i)) & 1 for i in range(n))
        r = slice(d * owned, (d + 1) * owned)
        squares = sq_all[at].astype(f32)
        stage_q[r, :] = squares[:owned]
        stage_o[r, :] = squares[owned:2 * owned]
        stage_p[r, :] = pr_all[at].astype(f32)[:owned]
    wp[...] = stage_p[...].astype(bf16)

    block = lax.axis_index("seq")
    per = T // here // M
    tables = []
    for j in range(per):
        tables.append(turn_factors(near_ref[...], far_ref[pl.ds(block * per + j, 1), :]))

    first = lax.broadcasted_iota(jnp.int32, (M, 128), 1) < HD
    at = tuple(me[i] for i in seq_bits)
    for s in range(here):
        for j in range(per):
            r = slice((s * per + j) * M, (s * per + j + 1) * M)
            kv = dot(xa_ref[r, :], wp[...], 1, 0)
            turned = turn(kv, *tables[j])
            kv_ref[at + (s, pl.ds(j * M, M))] = jnp.where(first, turned, kv).astype(bf16)

    def kv_stage(k, held):
        copies = []
        for half in (0, 1):
            order = seq_bits if half == 0 else seq_bits[-1:] + seq_bits[:-1]
            b = order[k]
            rows = T // here // 2
            where = tuple(slice(None) if i in held[half] else me[i] for i in seq_bits)
            piece = kv_ref.at[where + (slice(None), pl.ds(half * rows, rows))]
            copy = pltpu.make_async_remote_copy(
                src_ref=piece, dst_ref=piece, send_sem=kv_send.at[half, k], recv_sem=kv_recv.at[half, k],
                device_id=partner(bits[b]), device_id_type=MESH)
            copy.start()
            copies.append(copy)
            held[half].add(b)
        return copies

    def queries(i):
        r = slice(i * chunk, (i + 1) * chunk)
        z = dot(xa_ref[r, :], wide_ref[0], 1, 0)
        for j in range(chunk // M):
            tab = tables[(i * chunk // M + j) % per]
            for p in range(D // 128):
                c = slice(p * 128, (p + 1) * 128)
                part = turn(z[j * M:(j + 1) * M, c], *tab) * (HD ** -0.5 / LN2)
                q_ref[i * chunk + j * M:i * chunk + (j + 1) * M, c] = part.astype(bf16)

    def gradients(i):
        r = slice(i * chunk, (i + 1) * chunk)
        g_ref[r, :] = dot(b_ref[r, :], wide_ref[1], 1, 1).astype(bf16)

    held = [set(), set()]
    jobs = [functools.partial(f, i) for f in (queries, gradients) for i in range(chunks)]
    for k in range(len(seq_bits)):
        copies = kv_stage(k, held)
        if k == 0:
            wide_ref[0] = stage_q[...].astype(bf16)
            wide_ref[1] = stage_o[...].astype(bf16)
        for i, job in enumerate(jobs):
            if i * len(seq_bits) // len(jobs) == k:
                job()
        for copy in copies:
            copy.wait()


def front(x, c, scale, norms, squares, pairs, here, length, M, n_seq, n_rows, collective_id, chunk=256):
    bits = bits_of(n_seq, n_rows)
    n = len(bits)
    n_s = n_seq.bit_length() - 1
    T, D = x.shape
    f32, bf16 = jnp.float32, jnp.bfloat16
    near, far = turn_tables(length, M)
    vmem = pl.BlockSpec(memory_space=pltpu.VMEM)
    token = jax.ShapeDtypeStruct((T, D), bf16)
    outs = pl.pallas_call(
        functools.partial(front_kernel, bits, here, M, chunk),
        out_shape=[token, token, jax.ShapeDtypeStruct((2,) * n_s + (here, T // here, 128), bf16), token, token, token,
                   jax.ShapeDtypeStruct((2, D, D), bf16), jax.ShapeDtypeStruct((D, 128), bf16)],
        in_specs=[vmem] * 8,
        out_specs=[vmem] * 8,
        scratch_shapes=[
            pltpu.VMEM((2,) * n + squares.shape, bf16),
            pltpu.VMEM((2,) * n + pairs.shape, bf16),
            pltpu.VMEM((D, D), f32),
            pltpu.VMEM((D, D), f32),
            pltpu.VMEM((D, 128), f32),
            pltpu.SemaphoreType.DMA((2,)),
            pltpu.SemaphoreType.DMA((2, 2, n)),
            pltpu.SemaphoreType.DMA((2, 2, n)),
            pltpu.SemaphoreType.DMA((2, n_s)),
            pltpu.SemaphoreType.DMA((2, n_s)),
        ],
        compiler_params=pltpu.CompilerParams(
            collective_id=collective_id, has_side_effects=True, vmem_limit_bytes=56 << 20),
        name="front",
    )(x, c, scale, norms, near, far, squares, pairs)
    q, g, kv, xa, xf, b, wide, pair = outs
    return q, g, kv.reshape(n_seq, here, T // here, 128), xa, xf, b, wide, pair


def layer_norm(values):
    center = values - jnp.mean(values, axis=-1, keepdims=True)
    inverse = lax.rsqrt(jnp.mean(center * center, axis=-1, keepdims=True) + 1e-05)
    return center * inverse, inverse


def norm_back(incoming, normed, inverse, gain):
    scaled = incoming * gain
    return inverse * (
        scaled
        - jnp.mean(scaled, axis=-1, keepdims=True)
        - normed * jnp.mean(scaled * normed, axis=-1, keepdims=True)
    )


def rotary_tables(positions):
    half_rot = ROT // 2
    frequency = 10000.0 ** (-2.0 * jnp.arange(half_rot, dtype=jnp.float32) / ROT)
    angles = positions[:, None] * frequency[None, :]
    cosine = jnp.concatenate([jnp.cos(angles), jnp.cos(angles)], axis=-1)
    sine_vals = jnp.concatenate([jnp.sin(angles), jnp.sin(angles)], axis=-1)
    return (cosine, sine_vals)


def rotate(vector, cosine, sine_vals):
    half_rot = ROT // 2
    rotary_part = vector[..., :ROT]
    turned = jnp.concatenate([-rotary_part[..., half_rot:], rotary_part[..., :half_rot]], axis=-1)
    return jnp.concatenate([rotary_part * cosine + turned * sine_vals, vector[..., ROT:]], axis=-1)


def plan(n, here, per, M, tk):
    order = [(s, j) for j in reversed(range(per)) for s in range(here)]
    row = lambda i, j: (i * per + j) * M
    price = lambda first: first // tk + 1.4
    moved = [0] * n
    for i in range(n // 2, n):
        load = lambda k: max(
            sum(price(row(i, j)) for _, j in order[k:]),
            sum(price(row(n - 1 - i, j)) for _, j in order) + sum(price(row(i, j)) for _, j in order[:k]))
        moved[i] = min(range(len(order)), key=load)
    most = max(moved)
    takes = [[(here * per + k, s, row(n - 1 - i, j)) for k, (s, j) in enumerate(order[:moved[n - 1 - i]])] if i < n // 2 else []
             for i in range(n)]
    keeps = [[(s * per + j, s, row(i, j)) for s, j in order[moved[i]:]] for i in range(n)]
    cost = lambda steps: sum(price(x[2]) for x in steps)
    mean = sum(cost(t) + cost(k) for t, k in zip(takes, keeps)) / n
    lists = ([], [], [])
    for take, keep in zip(takes, keeps):
        keep = list(keep)
        head, middle = [], list(take)
        while keep and cost(head) + price(keep[0][2]) / 2 < 0.22 * mean:
            head.append(keep.pop(0))
        while keep and cost(middle) + price(keep[0][2]) / 2 < 0.56 * mean and cost(keep) > 0.22 * mean:
            middle.append(keep.pop(0))
        for part, steps in zip(lists, (head, middle, keep)):
            part.append(steps)
    tables = []
    for part in lists:
        size = max(1, max(len(w) for w in part))
        full = [[x + (1,) for x in w] + [(w[-1] if w else (0, 0, 0)) + (0,)] * (size - len(w)) for w in part]
        tables.append(np.array(full, np.int32))
    return order, moved, most, tables


def local(
    mesh, states, cotangent, subsets, subset_weight, gain_attn, shift_attn, gain_ffn, shift_ffn,
    query_projection, pair_projection, output_projection, up_projection, down_projection,
):
    f32, bf16 = jnp.float32, jnp.bfloat16
    both = ("seq", "rows")
    here, length_here, D = states.shape
    T = here * length_here
    n_seq, n_rows = mesh.shape["seq"], mesh.shape["rows"]
    n = n_seq * n_rows
    length = length_here * n_seq
    block = lax.axis_index("seq")
    offset = block * length_here
    M = min(128, length_here)
    per = length_here // M
    tk = min(512, length)
    FF = up_projection.shape[1]
    P = 2 * HD
    scale = HD ** -0.5
    own_rows = query_projection.shape[0]
    aligned = (2 * own_rows) % 16 == 0 and own_rows % 8 == 0

    rows_here = offset + jnp.arange(length_here, dtype=jnp.int32)
    cosine, sine_vals = rotary_tables(rows_here.astype(f32))
    source = states.astype(f32).reshape(T, D)
    unit, inverse = layer_norm(source)
    table_rows = jnp.arange(subset_weight.shape[0], dtype=jnp.int32)
    row_scale = jnp.sum(
        jnp.where(table_rows[None, :] == subsets[:, None], subset_weight[None, :], 0.0), axis=1
    )
    upstream = (cotangent.astype(f32) * row_scale[:, None, None]).reshape(T, D)

    if aligned:
        tiles = FF // D
        packed = jnp.concatenate([
            jnp.swapaxes(up_projection.reshape(own_rows, tiles, D), 0, 1).reshape(-1, D), down_projection])
        packed = lax.all_gather(packed, both, axis=0)
        squares = jnp.concatenate([query_projection, output_projection], axis=0)
        pairs = jnp.pad(pair_projection, ((0, -own_rows % 32), (0, 0)))
        norms = jnp.stack([gain_attn, shift_attn, gain_ffn, shift_ffn])
        scales = jnp.broadcast_to(row_scale[:, None], (here, D))
        queries, out_grad, all_kv, attention_input, feedforward_input, branch_grad, squares, full_pair = front(
            states.reshape(T, D), cotangent.reshape(T, D), scales, norms, squares, pairs,
            here, length, M, n_seq, n_rows, 1)
        full_query, full_output = squares[0], squares[1]
    else:
        big = jnp.stack([up_projection, down_projection.reshape(up_projection.shape)])
        big = lax.all_gather(big, both, axis=1, tiled=True)
        full_up, full_down = big[0], big[1].reshape(FF, D)
        small = jnp.concatenate([query_projection, pair_projection, output_projection], axis=1)
        small = lax.all_gather(small, both, axis=0, tiled=True)
        full_query, full_pair, full_output = small[:, :D], small[:, D:D + P], small[:, D + P:]
        attention_input = (unit * gain_attn + shift_attn).astype(bf16)
        feedforward_input = (unit * gain_ffn + shift_ffn).astype(bf16)
        branch_grad = upstream.astype(bf16)
        pair_pre = jnp.dot(attention_input, full_pair, preferred_element_type=f32)
        pair_pre = pair_pre.reshape(here, length_here, P)
        key_values = jnp.concatenate(
            [rotate(pair_pre[..., :HD], cosine[None], sine_vals[None]), pair_pre[..., HD:]], axis=2
        ).astype(bf16)
        query_pre = jnp.dot(attention_input, full_query, preferred_element_type=f32)
        queries = rotate(
            query_pre.reshape(here, length_here, H, HD) * (scale / LN2),
            cosine[None, :, None, :], sine_vals[None, :, None, :],
        ).astype(bf16).reshape(T, D)
        out_grad = lax.dot_general(
            branch_grad, full_output, (((1,), (1,)), ((), ())), preferred_element_type=f32
        ).astype(bf16)
        all_kv = lax.all_gather(key_values, "seq", axis=0)

    order, moved, most, tables = plan(n_seq, here, per, M, tk)
    own = here * per
    q_tiles, g_tiles = queries.reshape(own, M, D), out_grad.reshape(own, M, D)
    others = []
    for k in range(most):
        s, j = order[k]
        pairs_of = [(i, n_seq - 1 - i) for i in range(n_seq) if moved[i] > k]
        others.append(lax.ppermute(jnp.stack([q_tiles[s * per + j], g_tiles[s * per + j]]), "seq", pairs_of))
    steps = []
    for table in tables:
        mine = jnp.asarray(table)[block]
        steps.append(tuple(mine[:, c] for c in range(4)))
    done = attention(steps[0], queries, out_grad, None, all_kv, M, tk, most)

    ffn_x, done = lax.optimization_barrier((feedforward_input, done))
    if aligned:
        ffn_out, ffn_input_grad, ffn_grads = ffn_packed(ffn_x, branch_grad, packed, n_seq, n_rows)
    else:
        ffn_out, ffn_input_grad, grad_up, grad_down = ffn(ffn_x, branch_grad, full_up, full_down)
        ffn_grads = jnp.concatenate(
            [grad_up.reshape(n_seq, n_rows, -1, D), grad_down.reshape(n_seq, n_rows, -1, D)], axis=2)
        ffn_grads = jnp.swapaxes(ffn_grads, 0, 1)
    done, ffn_out = lax.optimization_barrier((done, ffn_out))
    ffn_grads = lax.psum_scatter(ffn_grads, "rows", scatter_dimension=0, tiled=True)[0]
    ffn_grads = lax.psum_scatter(ffn_grads, "seq", scatter_dimension=0, tiled=True)[0]
    half = ffn_grads.shape[0] // 2
    final_up = ffn_grads[:half]
    if aligned:
        final_up = jnp.swapaxes(final_up.reshape(FF // D, own_rows, D), 0, 1)
    final_up = final_up.reshape(-1, FF).astype(f32)
    final_down = ffn_grads[half:].astype(f32)

    done = attention(steps[1], queries, out_grad, jnp.stack(others), all_kv, M, tk, most, done)
    backs = []
    for k in range(most):
        pairs_of = [(n_seq - 1 - i, i) for i in range(n_seq) if moved[i] > k]
        tile = slice((own + k) * M, (own + k + 1) * M)
        backs.append(lax.ppermute(jnp.stack([done[0][tile], done[1][tile]]), "seq", pairs_of))
    attended, query_pre_grad, pair_terms = attention(steps[2], queries, out_grad, None, all_kv, M, tk, most, done)
    a_own, d_own = list(attended.reshape(-1, M, D)[:own]), list(query_pre_grad.reshape(-1, M, D)[:own])
    count = jnp.asarray(np.array(moved, np.int32))[block]
    for k in range(most):
        s, j = order[k]
        at = s * per + j
        a_own[at] = jnp.where(count > k, backs[k][0], a_own[at])
        d_own[at] = jnp.where(count > k, backs[k][1], d_own[at])
    attended, query_pre_grad = jnp.concatenate(a_own), jnp.concatenate(d_own)

    pair_terms = pair_terms.astype(bf16).reshape(here, P, n_seq, length_here)
    pair_terms = jnp.moveaxis(pair_terms, 2, 0)
    arrived = lax.all_to_all(pair_terms, "seq", split_axis=0, concat_axis=0, tiled=True)
    pair_grad = jnp.swapaxes(arrived.astype(f32).sum(axis=0), 1, 2)

    residual = jnp.dot(attended, full_output, preferred_element_type=f32) + ffn_out
    layer_out = (source + residual).astype(bf16).reshape(here, length_here, D)
    grad_output = lax.dot_general(
        attended, branch_grad, (((0,), (0,)), ((), ())), preferred_element_type=f32)
    grad_query = lax.dot_general(
        attention_input, query_pre_grad, (((0,), (0,)), ((), ())), preferred_element_type=f32)
    attn_input_grad = lax.dot_general(
        query_pre_grad, full_query, (((1,), (1,)), ((), ())), preferred_element_type=f32)

    pair_pre_grad = jnp.concatenate(
        [rotate(pair_grad[..., :HD] * LN2, cosine[None], -sine_vals[None]), pair_grad[..., HD:]], axis=2
    ).reshape(T, P).astype(bf16)
    grad_pair = lax.dot_general(
        attention_input, pair_pre_grad, (((0,), (0,)), ((), ())), preferred_element_type=f32)
    attn_input_grad = attn_input_grad + lax.dot_general(
        pair_pre_grad, full_pair, (((1,), (1,)), ((), ())), preferred_element_type=f32)

    sums = jnp.stack([
        jnp.sum(attn_input_grad * unit, axis=0), jnp.sum(attn_input_grad, axis=0),
        jnp.sum(ffn_input_grad * unit, axis=0), jnp.sum(ffn_input_grad, axis=0)], axis=1)
    grad_states = upstream + norm_back(attn_input_grad, unit, inverse, gain_attn)
    grad_states = grad_states + norm_back(ffn_input_grad, unit, inverse, gain_ffn)
    grad_states = grad_states.astype(bf16).reshape(here, length_here, D)

    last = jnp.concatenate([grad_query, grad_pair, jnp.pad(sums, ((0, 0), (0, 124))), grad_output], axis=1)
    if aligned:
        last = jnp.pad(last, ((0, 0), (0, -last.shape[1] % 512)))
        last = scatter(last.reshape(n, own_rows, -1), n_seq, n_rows, 3)
    else:
        last = lax.psum_scatter(last.astype(bf16), both, scatter_dimension=0, tiled=True).astype(f32)
    vectors = last[:, D + P:]
    at = D + P + 128
    return (
        layer_out, grad_states,
        vectors[:, 0], vectors[:, 1], vectors[:, 2], vectors[:, 3],
        last[:, :D], last[:, D:D + P], last[:, at:at + D], final_up, final_down,
    )


def solution(mesh):
    from jax.sharding import PartitionSpec as P

    blocks, owned = P("rows", "seq", None), P(("seq", "rows"), None)
    vector = P(("seq", "rows"))
    return jax.shard_map(
        functools.partial(local, mesh),
        mesh=mesh,
        in_specs=(blocks, blocks, P("rows"), P(), P(), P(), P(), P()) + (owned,) * 5,
        out_specs=(blocks, blocks) + (vector,) * 4 + (owned,) * 5,
        check_vma=False,
    )
```

time: 666 us -> 575 us (0.86)
  Pallas kernels: 87.1 us -> 373 us
  waiting for transfers between devices: 269 us -> 59.7 us
  starting transfers between devices: 144 us -> 39.8 us
  local copies, waits for them, and re-layouts: 73 us -> 33 us
  other arithmetic: 46.4 us -> 30.5 us
  matrix products: 26.4 us -> 16.8 us
    pallas_call x2 -> x6, Pallas kernels: 87.1 us -> 373 us  [the longest x3 139 us: attention(): pl.pallas_call(kernel, grid_spec=pltpu.PrefetchScalarGridSpec(num_scalar_...]
    all_gather x3 -> x1, waiting for transfers between devices: 128 us -> 0.01 us  [local(): packed = lax.all_gather(packed, both, axis=0)]
    all_to_all x1, starting transfers between devices: 143 us -> 26.4 us  [local(): lax.all_to_all(pair_terms, 'seq', split_axis=0, concat_axis=0, tiled=True)]
    reduce_scatter x3 -> x2, waiting for transfers between devices: 115 us -> 0.01 us  [the longest x1 0.01 us: local(): lax.psum_scatter(ffn_grads, 'rows', scatter_dimension=0, tiled=True)[0]]
    ppermute x0 -> x6, waiting for transfers between devices: none -> 59.7 us  [the longest x3 40.9 us: local(): lax.ppermute(jnp.stack([done[0][tile], done[1][tile]]), 'seq', pairs_of)]
    all_to_all x1, waiting for transfers between devices: 25.7 us -> 0.01 us  [local(): lax.all_to_all(pair_terms, 'seq', split_axis=0, concat_axis=0, tiled=True)]
    ppermute x0 -> x6, starting transfers between devices: none -> 13.4 us  [the longest x3 9.4 us: local(): lax.ppermute(jnp.stack([done[0][tile], done[1][tile]]), 'seq', pairs_of)]
    mul x4 -> x0, local copies, waits for them, and re-layouts: 11.3 us -> none  [the longest x2 9.28 us: local(): query_grad.reshape(here, length_here, H, HD) * scale]
  transfers between devices with their start and end apart: 7 -> 10, of which waited for: 5 -> 6; matrix products, arithmetic and copies ran while one was open for 21% -> 13% of each run, Pallas kernels for 13% -> 57%
where the time goes in v2:
time: 575 us; the launch traced here: 569 us
  Pallas kernels  373 us (65%)
  waiting for transfers between devices  59.7 us (10%)
  starting transfers between devices  39.8 us (7%)
  local copies, waits for them, and re-layouts  33 us (6%)
  other arithmetic  30.5 us (5%)
  matrix products  16.8 us (3%)
  between operations  16.4 us (3%)
    pallas_call x3, Pallas kernels, attention(): pl.pallas_call(kernel, grid_spec=pltpu.PrefetchScalarGridSpec(num_scalar_...  139 us
    pallas_call x1, Pallas kernels, front(): pl.pallas_call(functools.partial(front_kernel, bits, here, M, chunk), out...  111 us
    pallas_call x1, Pallas kernels, scatter(): pl.pallas_call(functools.partial(scatter_kernel, bits, width), out_shape=...  75.5 us
    pallas_call x1, Pallas kernels, ffn_packed(): pl.pallas_call(functools.partial(ffn_packed_kernel, C, n_rows), grid=(til...  47.2 us
    ppermute x3, waiting for transfers between devices, local(): lax.ppermute(jnp.stack([done[0][tile], done[1][tile]]), 'seq', pairs_of)  40.9 us
    all_to_all x1, starting transfers between devices, local(): lax.all_to_all(pair_terms, 'seq', split_axis=0, concat_axis=0, tiled=True)  26.4 us
    ppermute x3, waiting for transfers between devices, local(): lax.ppermute(jnp.stack([q_tiles[s * per + j], g_tiles[s * per + j]]), 'se...  18.8 us
  transfers between devices with their start and end apart: 10, of which 6 were waited for; matrix products, arithmetic and copies ran while one was open for 13% of the time, Pallas kernels for 57%

profile of v2, /device:TPU:0, one launch (start us, length us, event | category | flops | bytes accessed | tf_op | source)
XLA Modules:
  0.0 569.1 jit_solution(1506602277065279954)
XLA Ops:
  17.5 111.5 %front.1 = (bf16[1024,768]{1,0:T(8,128)(2,1)}, bf16[1024,768]{1,0:T(8,128)(2,1)}, bf16[2,2,2,2,512,128]{5,4,3,2,1,0:T(8,128)(2,1)}, bf16[1024,768]{1,0:T(8,128)(...) custom-call(bf16[1024,768]{1,0:T(8,128)(2,1)} %bitcast.195, ...), custom_call_target="tpu_custom_call" | custom-call | tf_op jit(solution)/shard_map/front/pallas_call | solution.py:724
  130.2 40.2 %attention.3 = (bf16[1408,768]{1,0:T(8,128)(2,1)}, bf16[1408,768]{1,0:T(8,128)(2,1)}, f32[2,128,4096]{2,1,0:T(8,128)}) custom-call(s32[6]{0:T(128)} %get-tuple-element.122.a, s32[6]{0:T(128)} %get-tuple-element.121.b, s32[6]{0:T(128)} %get-tuple-element.120.c, s32[6]{0:T(128)} %get-tuple-element.119.d, bf16[1024,768]{1,0:T(8,128)(2,1)} %get-tuple-element.39.q_ref, ...), custom_call_target="tpu_custom_call" | custom-call | flops 1048576 | bytes 65536 | tf_op jit(solution)/shard_map/attention/pallas_call | solution.py:228
  170.4 47.2 %feedforward.1 = (f32[1024,768]{1,0:T(8,128)}, f32[1024,768]{1,0:T(8,128)}, bf16[4,8,192,768]{3,2,1,0:T(8,128)(2,1)}) custom-call(bf16[1024,768]{1,0:T(8,128)(2,1)} %get-tuple-element.49.x_ref, bf16[1024,768]{1,0:T(8,128)(2,1)} %get-tuple-element.50.b_ref, bf16[4,8,2,96,768]{4,3,2,1,0:T(8,128)(2,1)} %bitcast.193, bf16[4,8,2,96,768]{4,3,2,1,0:T(8,128)(2,1)} %bitcast.194), custom_call_target="tpu_custom_call" | custom-call | flops 1048576 | bytes 65536 | tf_op jit(solution)/shard_map/feedforward/pallas_call | solution.py:392
  231.1 2.6 convert_multiply_fusion
  233.7 3.1 collective-permute-done.2
  236.8 8.5 %collective-permute-done.1 = bf16[2,128,768]{2,1,0:T(8,128)(2,1)} collective-permute-done((bf16[2,128,768]{2,1,0:T(8,128)(2,1)}, bf16[2,128,768]{2,1,0:T(8,128)(2,1)}, u32[]{:S(2)}, u32[]{:S(2)}) %collective-permute-start.1) | collective-permute-done | bytes 393248 | tf_op jit(solution)/shard_map/ppermute | solution.py:892
  245.3 7.1 %collective-permute-done = bf16[2,128,768]{2,1,0:T(8,128)(2,1)} collective-permute-done((bf16[2,128,768]{2,1,0:T(8,128)(2,1)}, bf16[2,128,768]{2,1,0:T(8,128)(2,1)}, u32[]{:S(2)}, u32[]{:S(2)}) %collective-permute-start) | collective-permute-done | bytes 393248 | tf_op jit(solution)/shard_map/ppermute | solution.py:892
  254.7 78.1 %attention.4 = (bf16[1408,768]{1,0:T(8,128)(2,1)}, bf16[1408,768]{1,0:T(8,128)(2,1)}, f32[2,128,4096]{2,1,0:T(8,128)}) custom-call(s32[5]{0:T(128)} %get-tuple-element.118.slot_ref, s32[5]{0:T(128)} %get-tuple-element.117.seq_ref, s32[5]{0:T(128)} %get-tuple-element.116.row_ref, ...), custom_call_target="tpu_custom_call", output_to_operand_aliasing={{0}: (10, {}), {1}: (11, {}), {2}: (12, {})} | custom-call | flops 1048576 | bytes 65536 | tf_op jit(solution)/shard_map/attention/pallas_call | solution.py:228
  335.1 20.4 %attention.5 = (bf16[1408,768]{1,0:T(8,128)(2,1)}, bf16[1408,768]{1,0:T(8,128)(2,1)}, f32[2,128,4096]{2,1,0:T(8,128)}) custom-call(s32[4]{0:T(128)} %get-tuple-element.86.a, s32[4]{0:T(128)} %get-tuple-element.85.b, s32[4]{0:T(128)} %get-tuple-element.84.c, s32[4]{0:T(128)} %get-tuple-element.83.d, ...), custom_call_target="tpu_custom_call", output_to_operand_aliasing={{0}: (9, {}), {1}: (10, {}), {2}: (11, {})} | custom-call | flops 1048576 | bytes 65536 | tf_op jit(solution)/shard_map/attention/pallas_call | solution.py:228
  355.5 2.5 convert_element_type.56
  359.5 26.4 %all-to-all-start = ((bf16[8,2,128,512]{3,2,1,0:T(8,128)(2,1)}), bf16[8,2,128,512]{3,2,1,0:T(8,128)(2,1)}, u32[]{:S(2)}, u32[]{:S(2)}) async-start(bf16[8,2,128,512]{3,2,1,0:T(8,128)(2,1)} %bitcast.200), calls=%async_computation | async-start | bytes 4194304 | tf_op jit(solution)/shard_map/all_to_all | solution.py:935
  388.7 6.6 %collective-permute-start.3 = (bf16[2,128,768]{2,1,0:T(8,128)(2,1)S(1)}, bf16[2,128,768]{2,1,0:T(8,128)(2,1)S(1)}, u32[]{:S(2)}, u32[]{:S(2)}) collective-permute-start(bf16[2,128,768]{2,1,0:T(8,128)(2,1)S(1)} %pad_maximum_fusion.5), channel_id=1, source_target_pairs={{4,24},{0,28},{5,25},{1,29},{6,26},{2,30},{7,27},{3,31}} | collective-permute-start | bytes 1179656 | tf_op jit(solution)/shard_map/ppermute | solution.py:922
  399.2 30.1 %collective-permute-done.3 = bf16[2,128,768]{2,1,0:T(8,128)(2,1)S(1)} collective-permute-done((bf16[2,128,768]{2,1,0:T(8,128)(2,1)S(1)}, bf16[2,128,768]{2,1,0:T(8,128)(2,1)S(1)}, u32[]{:S(2)}, u32[]{:S(2)}) %collective-permute-start.3) | collective-permute-done | bytes 393248 | tf_op jit(solution)/shard_map/ppermute | solution.py:922
  430.4 7.4 %collective-permute-done.4 = bf16[2,128,768]{2,1,0:T(8,128)(2,1)S(1)} collective-permute-done((bf16[2,128,768]{2,1,0:T(8,128)(2,1)S(1)}, bf16[2,128,768]{2,1,0:T(8,128)(2,1)S(1)}, u32[]{:S(2)}, u32[]{:S(2)}) %collective-permute-start.4) | collective-permute-done | bytes 393248 | tf_op jit(solution)/shard_map/ppermute | solution.py:922
  440.1 3.4 collective-permute-done.5
  444.6 2.9 fusion.45
  447.5 2.9 fusion.43
  450.5 2.6 fusion.4
  459.1 6.3 %fusion.18 = (f32[768]{0:T(1024)S(1)}, f32[1024]{0:T(1024)S(1)}, f32[1024]{0:T(1024)S(1)}, f32[768]{0:T(1024)S(1)}, f32[768]{0:T(1024)S(1)}, /*index=5*/f32[1024...) fusion(bf16[2,512,768]{2,1,0:T(8,128)(2,1)S(1)} %copy-done, f32[1024]{0:T(1024)S(1)} %bitcast.213, ...), kind=kOutput, calls=%fused_computation.25 | convolution fusion | flops 1222108160 | bytes 13805568 | tf_op jit(solution)/shard_map/dot_general | solution.py:944
  467.1 2.7 pad_maximum_fusion
  469.7 6.2 %copy.61 = f32[768,1792]{1,0:T(8,128)} copy(f32[768,1792]{0,1:T(8,128)} %pad_maximum_fusion) | data formatting | bytes 11010048
  475.9 3.5 pad.14.clone
  479.4 75.5 %scatter.1 = f32[24,2048]{1,0:T(8,128)S(1)} custom-call(f32[32,24,2048]{2,1,0:T(8,128)S(1)} %bitcast.192), custom_call_target="tpu_custom_call" | custom-call | tf_op jit(solution)/shard_map/scatter/pallas_call | solution.py:573
  557.0 3.0 fusion.1
  (128 shorter events, 52.1 us)
Async XLA Ops:
  7.2 163.2 %all-gather.3.cloned.1.call-start = ((), (), s32[]{:S(2)}) async-start(), calls=%async_computation.5 | async-start | bytes 9732096 | tf_op jit(solution)/shard_map/all_gather | solution.py:851
  9.8 443.3 %reduce-scatter.3.cloned.1.call-start = ((), (), s32[]{:S(2)}) async-start(), calls=%async_computation.3 | async-start | bytes 11796480 | tf_op jit(solution)/shard_map/reduce_scatter | solution.py:908
  217.6 9.3 %copy-start = (bf16[2,512,768]{2,1,0:T(8,128)(2,1)S(1)}, bf16[2,512,768]{2,1,0:T(8,128)(2,1)}, u32[]{:S(2)}) copy-start(bf16[2,512,768]{2,1,0:T(8,128)(2,1)} %param.25) | copy-start | bytes 4718596
  219.9 16.9 %collective-permute-start.2 = (bf16[2,128,768]{2,1,0:T(8,128)(2,1)}, bf16[2,128,768]{2,1,0:T(8,128)(2,1)S(1)}, u32[]{:S(2)}, u32[]{:S(2)}) collective-permute-start(bf16[2,128,768]{2,1,0:T(8,128)(2,1)} %pad_maximum_fusion.4), channel_id=1, source_target_pairs={{24,4},{28,0},{25,5},{29,1},{26,6},{30,2},{27,7},{31,3}} | collective-permute-start | bytes 1179656 | tf_op jit(solution)/shard_map/ppermute | solution.py:892
  222.0 9.1 %copy-start.3 = (bf16[2,512,768]{2,1,0:T(8,128)(2,1)S(1)}, bf16[2,512,768]{2,1,0:T(8,128)(2,1)}, u32[]{:S(2)}) copy-start(bf16[2,512,768]{2,1,0:T(8,128)(2,1)} %param.26) | copy-start | bytes 4718596
  222.0 23.3 %collective-permute-start.1 = (bf16[2,128,768]{2,1,0:T(8,128)(2,1)}, bf16[2,128,768]{2,1,0:T(8,128)(2,1)}, u32[]{:S(2)}, u32[]{:S(2)}) collective-permute-start(bf16[2,128,768]{2,1,0:T(8,128)(2,1)} %pad_maximum_fusion.3), channel_id=1, source_target_pairs={{20,8},{24,4},{28,0},{21,9},{25,5},{29,1},{22,10},{26,6},{30,2},{2... | collective-permute-start | bytes 1179656 | tf_op jit(solution)/shard_map/ppermute | solution.py:892
  224.2 28.3 %collective-permute-start = (bf16[2,128,768]{2,1,0:T(8,128)(2,1)}, bf16[2,128,768]{2,1,0:T(8,128)(2,1)}, u32[]{:S(2)}, u32[]{:S(2)}) collective-permute-start(bf16[2,128,768]{2,1,0:T(8,128)(2,1)} %pad_maximum_fusion.2), channel_id=1, source_target_pairs={{16,12},{20,8},{24,4},{28,0},{17,13},{21,9},{25,5},{29,1},{18,14},... | collective-permute-start | bytes 1179656 | tf_op jit(solution)/shard_map/ppermute | solution.py:892
  359.5 26.4 %copy-start.15 = (f32[2,512]{1,0:T(2,128)S(1)}, f32[2,512]{1,0:T(2,128)}, u32[]{:S(2)}) copy-start(f32[2,512]{1,0:T(2,128)} %fusion.3) | copy-start | bytes 12292
  359.5 26.4 %copy-start.20 = (s32[8]{0:T(128)S(1)}, s32[8]{0:T(128)}, u32[]{:S(2)}) copy-start(s32[8]{0:T(128)} %constant.61.clone) | copy-start | bytes 100
  359.5 29.0 %copy-start.16 = (f32[1,4,2,128]{3,2,1,0:T(2,128)S(1)}, f32[1,4,2,128]{3,2,1,0:T(2,128)}, u32[]{:S(2)}) copy-start(f32[1,4,2,128]{3,2,1,0:T(2,128)} %get-tuple-element.112) | copy-start | bytes 12292
  359.5 29.1 %copy-start.12 = (f32[512,8]{0,1:T(8,128)S(1)}, f32[512,8]{0,1:T(8,128)}, u32[]{:S(2)}) copy-start(f32[512,8]{0,1:T(8,128)} %get-tuple-element.114) | copy-start | bytes 49156
  359.5 93.6 %all-to-all-start = ((bf16[8,2,128,512]{3,2,1,0:T(8,128)(2,1)}), bf16[8,2,128,512]{3,2,1,0:T(8,128)(2,1)}, u32[]{:S(2)}, u32[]{:S(2)}) async-start(bf16[8,2,128,512]{3,2,1,0:T(8,128)(2,1)} %bitcast.200), calls=%async_computation | async-start | bytes 4194304 | tf_op jit(solution)/shard_map/all_to_all | solution.py:935
  385.9 174.0 %reduce-scatter.5.cloned.1.call-start = ((), (), s32[]{:S(2)}) async-start(), calls=%async_computation.4 | async-start | bytes 2654208 | tf_op jit(solution)/shard_map/reduce_scatter | solution.py:909
  385.9 13.3 %copy-start.1 = (bf16[1408,768]{1,0:T(8,128)(2,1)S(1)}, bf16[1408,768]{1,0:T(8,128)(2,1)}, u32[]{:S(2)}) copy-start(bf16[1408,768]{1,0:T(8,128)(2,1)} %get-tuple-element.58) | copy-start | bytes 6488068
  388.7 40.7 %collective-permute-start.3 = (bf16[2,128,768]{2,1,0:T(8,128)(2,1)S(1)}, bf16[2,128,768]{2,1,0:T(8,128)(2,1)S(1)}, u32[]{:S(2)}, u32[]{:S(2)}) collective-permute-start(bf16[2,128,768]{2,1,0:T(8,128)(2,1)S(1)} %pad_maximum_fusion.5), channel_id=1, source_target_pairs={{4,24},{0,28},{5,25},{1,29},{6,26},{2,30},{7,27},{3,31}} | collective-permute-start | bytes 1179656 | tf_op jit(solution)/shard_map/ppermute | solution.py:922
  395.3 42.5 %collective-permute-start.4 = (bf16[2,128,768]{2,1,0:T(8,128)(2,1)S(1)}, bf16[2,128,768]{2,1,0:T(8,128)(2,1)S(1)}, u32[]{:S(2)}, u32[]{:S(2)}) collective-permute-start(bf16[2,128,768]{2,1,0:T(8,128)(2,1)S(1)} %pad_maximum_fusion.6), channel_id=1, source_target_pairs={{12,16},{8,20},{4,24},{0,28},{13,17},{9,21},{5,25},{1,29},{14,18},... | collective-permute-start | bytes 1179656 | tf_op jit(solution)/shard_map/ppermute | solution.py:922
  396.7 46.8 %collective-permute-start.5 = (bf16[2,128,768]{2,1,0:T(8,128)(2,1)S(1)}, bf16[2,128,768]{2,1,0:T(8,128)(2,1)S(1)}, u32[]{:S(2)}, u32[]{:S(2)}) collective-permute-start(bf16[2,128,768]{2,1,0:T(8,128)(2,1)S(1)} %pad_maximum_fusion.7), channel_id=1, source_target_pairs={{8,20},{4,24},{0,28},{9,21},{5,25},{1,29},{10,22},{6,26},{2,30},{1... | collective-permute-start | bytes 1179656 | tf_op jit(solution)/shard_map/ppermute | solution.py:922
  437.8 6.8 %copy-start.10 = (bf16[1024,768]{1,0:T(8,128)(2,1)S(1)}, bf16[1024,768]{1,0:T(8,128)(2,1)}, u32[]{:S(2)}) copy-start(bf16[1024,768]{1,0:T(8,128)(2,1)} %get-tuple-element.50.b_ref) | copy-start | bytes 4718596
  444.5 2.9 copy-start.11
  447.5 3.0 copy-start.19
  459.1 6.8 %copy-start.8 = (f32[768,768]{0,1:T(8,128)S(1)}, f32[768,768]{0,1:T(8,128)}, u32[]{:S(2)}) copy-start(f32[768,768]{0,1:T(8,128)} %fusion.43) | copy-start | bytes 7077892
  475.9 81.1 %copy-start.6 = (f32[1024,768]{1,0:T(8,128)S(1)}, f32[1024,768]{1,0:T(8,128)}, u32[]{:S(2)}) copy-start(f32[1024,768]{1,0:T(8,128)} %get-tuple-element.123) | copy-start | bytes 9437188
  479.4 77.5 %copy-start.2 = (f32[2,512,768]{2,1,0:T(8,128)S(1)}, f32[2,512,768]{2,1,0:T(8,128)}, u32[]{:S(2)}) copy-start(f32[2,512,768]{2,1,0:T(8,128)} %convert_multiply_fusion) | copy-start | bytes 9437188
  479.4 77.5 %copy-start.5 = (f32[1024,768]{1,0:T(8,128)S(1)}, f32[1024,768]{1,0:T(8,128)}, u32[]{:S(2)}) copy-start(f32[1024,768]{1,0:T(8,128)} %get-tuple-element.64) | copy-start | bytes 9437188
  (7 other events, 17.2 us)
Sparse Core Ops, SparseCore 0:
  11.5 111.8 all-gather.2
  217.7 75.8 reduce-scatter.2
  453.2 103.3 reduce-scatter.4

commit v3 on v2

--- a/solution.py
+++ b/solution.py
@@ -194,7 +194,7 @@
             dq_ref[:, p * 128:(p + 1) * 128] = (turn_back(z, *factors) * HD ** -0.5).astype(bf16)
 
 
-def attention(tables, q, g, others, kv, M, tk, most, before=None):
+def attention(tables, q, g, others, skip, kv, M, tk, most, before=None):
     width = H * HD
     steps = tables[0].shape[0]
     own = q.shape[0] // M
@@ -206,7 +206,7 @@
     near_spec = pl.BlockSpec(near.shape, lambda t, *_: (0, 0), pipeline_mode=whole)
     far_spec = pl.BlockSpec(far.shape, lambda t, *_: (0, 0), pipeline_mode=whole)
     mine = pl.BlockSpec((M, width), lambda t, slot, *_: (jnp.minimum(slot[t], own - 1), 0))
-    taken = pl.BlockSpec((1, 2, M, width), lambda t, slot, *_: (jnp.maximum(slot[t] - own, 0), 0, 0, 0))
+    taken = pl.BlockSpec((1, 2, M, width), lambda t, slot, *_: (jnp.maximum(slot[t] - own - skip, 0), 0, 0, 0))
     sums = pl.BlockSpec((S, 128, L), lambda t, *_: (0, 0, 0), pipeline_mode=whole)
     anywhere = pl.BlockSpec(memory_space=pl.ANY)
     bf16, f32 = jnp.bfloat16, jnp.float32
@@ -254,6 +254,41 @@
     )(*tables, *operands)
 
 
+MESH = pl.DeviceIdType.MESH
+
+
+def bits_of(n_seq, n_rows):
+    high = [("seq", 1 << b) for b in reversed(range(n_seq.bit_length() - 1))]
+    return high + [("rows", 1 << b) for b in reversed(range(n_rows.bit_length() - 1))]
+
+
+def place(bits):
+    return [lax.rem(lax.axis_index(axis) // weight, 2) for axis, weight in bits]
+
+
+def partner(bit):
+    axis, weight = bit
+    mine = lax.axis_index(axis)
+    return {axis: mine + weight - 2 * weight * lax.rem(mine // weight, 2)}
+
+
+def greet(bits):
+    barrier = pltpu.get_barrier_semaphore()
+    for bit in bits:
+        pl.semaphore_signal(barrier, inc=1, device_id=partner(bit), device_id_type=MESH)
+    pl.semaphore_wait(barrier, len(bits))
+
+
+def routes(bits):
+    n = len(bits)
+    one = list(range(n))
+    other = list(range(n))
+    near = max(i for i in range(n) if bits[i][0] == "seq")
+    if near + 1 < n - 1:
+        other[near], other[near + 1] = other[near + 1], other[near]
+    return one, other
+
+
 def gelu_both(x):
     z = jnp.abs(x) * 0.7071067811865476
     s = 1.0 / (1.0 + 0.3275911 * z)
@@ -324,7 +359,12 @@
     )(x, b, up, down)
 
 
-def ffn_packed_kernel(C, n_rows, x_ref, b_ref, up_ref, down_ref, out_ref, dx_ref, grads_ref, act_s, ug_s, wide, ups):
+def ffn_packed_kernel(
+    C, bits, M, order, moved,
+    x_ref, b_ref, up_ref, down_ref, kv_ref, q_ref, g_ref,
+    out_ref, dx_ref, grads_ref, all_kv, others,
+    act_s, ug_s, wide, ups, own_sem, kv_send, kv_recv, tile_send, tile_recv,
+):
     f = pl.program_id(0)
     T, D = x_ref.shape
     groups, each, _, count, _ = up_ref.shape
@@ -332,6 +372,59 @@
     n = groups * each
     owned = D // n
     f32, bf16 = jnp.float32, jnp.bfloat16
+    stages = len(bits)
+    me = place(bits)
+    block = lax.axis_index("seq")
+    n_seq = len(moved)
+    local = kv_ref.shape[1]
+
+    def kv_copies(stage):
+        copies = []
+        for half in (0, 1):
+            route = list(range(stages)) if half == 0 else [stages - 1] + list(range(stages - 1))
+            at = tuple(slice(None) if i in route[:stage] else me[i] for i in range(stages))
+            piece = all_kv.at[at + (slice(None), pl.ds(half * (local // 2), local // 2))]
+            copies.append(pltpu.make_async_remote_copy(
+                src_ref=piece, dst_ref=piece, send_sem=kv_send.at[half, stage], recv_sem=kv_recv.at[half, stage],
+                device_id=partner(bits[route[stage]]), device_id_type=MESH))
+        return copies
+
+    def tile_copies(k):
+        r = pl.ds(order[k] * M, M)
+        return [pltpu.make_async_remote_copy(
+            src_ref=ref.at[r], dst_ref=others.at[k, i], send_sem=tile_send.at[k, i], recv_sem=tile_recv.at[k, i],
+            device_id={"seq": n_seq - 1 - block}, device_id_type=MESH) for i, ref in enumerate((q_ref, g_ref))]
+
+    def among(devices):
+        return functools.reduce(jnp.logical_or, [block == i for i in devices])
+
+    @pl.when(f == 0)
+    def _():
+        own = pltpu.make_async_copy(kv_ref, all_kv.at[tuple(me)], own_sem)
+        own.start()
+        barrier = pltpu.get_barrier_semaphore()
+        for bit in bits:
+            pl.semaphore_signal(barrier, inc=1, device_id=partner(bit), device_id_type=MESH)
+        pl.semaphore_signal(barrier, inc=1, device_id={"seq": n_seq - 1 - block}, device_id_type=MESH)
+        pl.semaphore_wait(barrier, stages + 1)
+        own.wait()
+
+    for stage in range(stages):
+        @pl.when(f == min(stage, tiles - 1))
+        def _(stage=stage):
+            if stage > 0:
+                for copy in kv_copies(stage - 1):
+                    copy.wait()
+            for copy in kv_copies(stage):
+                copy.start()
+
+    @pl.when(f == 1)
+    def _():
+        for k in range(len(order)):
+            @pl.when(among([i for i in range(n_seq) if moved[i] > k]))
+            def _(k=k):
+                for copy in tile_copies(k):
+                    copy.start()
 
     @pl.when(f == 0)
     def _():
@@ -366,20 +459,32 @@
     grad_down = dot(act_s[...], b_ref[...], 0, 0).astype(bf16)
     for k in range(each):
         at = f * each + k
-        grads_ref[lax.rem(at, n_rows), at // n_rows, count:] = grad_down[k * count:(k + 1) * count]
+        grads_ref[at, count:] = grad_down[k * count:(k + 1) * count]
 
     @pl.when(f == tiles - 1)
     def _():
         def pack(d, _):
             at = pl.ds(pl.multiple_of(d * owned, 8), owned)
             part = jnp.concatenate([wide[j, at, :] for j in range(tiles)], axis=0)
-            grads_ref[lax.rem(d, n_rows), d // n_rows, :count] = part.astype(bf16)
+            grads_ref[d, :count] = part.astype(bf16)
             return 0
 
         lax.fori_loop(0, n, pack, 0)
-
-
-def ffn_packed(x, b, packed, n_seq, n_rows, C=256):
+        for copy in kv_copies(stages - 1):
+            copy.wait()
+        for k in range(len(order)):
+            @pl.when(among([i for i in range(n_seq) if moved[i] > k]))
+            def _(k=k):
+                for copy in tile_copies(k):
+                    copy.wait_send()
+
+            @pl.when(among([n_seq - 1 - i for i in range(n_seq) if moved[i] > k]))
+            def _(k=k):
+                for copy in tile_copies(k):
+                    copy.wait_recv()
+
+
+def ffn_packed(x, b, packed, kv, q, g, order, moved, M, n_seq, collective_id, C=256):
     T, D = x.shape
     n, count = packed.shape[0], packed.shape[1] // 2
     FF = n * count
@@ -389,221 +494,92 @@
     f32, bf16 = jnp.float32, jnp.bfloat16
     once = pl.Buffered(1)
     whole = lambda f: (0, 0)
-    return pl.pallas_call(
-        functools.partial(ffn_packed_kernel, C, n_rows),
+    bits = bits_of(n_seq, 1)
+    anywhere = pl.BlockSpec(memory_space=pl.ANY)
+    out, dx, grads, all_kv, others = pl.pallas_call(
+        functools.partial(ffn_packed_kernel, C, bits, M, tuple(order), tuple(moved)),
         grid=(tiles,),
         in_specs=[
             pl.BlockSpec((T, D), whole, pipeline_mode=once),
             pl.BlockSpec((T, D), whole, pipeline_mode=once),
             pl.BlockSpec((tiles, each, 1, count, D), lambda f: (0, 0, 0, 0, 0), pipeline_mode=once),
             pl.BlockSpec((1, each, 1, count, D), lambda f: (f, 0, 1, 0, 0)),
+            anywhere, anywhere, anywhere,
         ],
         out_specs=[
             pl.BlockSpec((T, D), whole, pipeline_mode=once),
             pl.BlockSpec((T, D), whole, pipeline_mode=once),
-            pl.BlockSpec((n_rows, n_seq, 2 * count, D), lambda f: (0, 0, 0, 0), pipeline_mode=once),
+            pl.BlockSpec((n, 2 * count, D), lambda f: (0, 0, 0), pipeline_mode=once),
+            anywhere, anywhere,
         ],
         out_shape=[
             jax.ShapeDtypeStruct((T, D), f32),
             jax.ShapeDtypeStruct((T, D), f32),
-            jax.ShapeDtypeStruct((n_rows, n_seq, 2 * count, D), bf16),
+            jax.ShapeDtypeStruct((n, 2 * count, D), bf16),
+            jax.ShapeDtypeStruct((2,) * len(bits) + kv.shape, bf16),
+            jax.ShapeDtypeStruct((len(order), 2, M, D), bf16),
         ],
         scratch_shapes=[
             pltpu.VMEM((T, D), bf16), pltpu.VMEM((T, D), bf16),
             pltpu.VMEM((tiles, D, D), f32), pltpu.VMEM((tiles, D, D), bf16),
+            pltpu.SemaphoreType.DMA,
+            pltpu.SemaphoreType.DMA((2, len(bits))), pltpu.SemaphoreType.DMA((2, len(bits))),
+            pltpu.SemaphoreType.DMA((len(order), 2)), pltpu.SemaphoreType.DMA((len(order), 2)),
         ],
-        compiler_params=pltpu.CompilerParams(vmem_limit_bytes=60 << 20),
+        compiler_params=pltpu.CompilerParams(
+            collective_id=collective_id, has_side_effects=True, vmem_limit_bytes=60 << 20),
         cost_estimate=pl.CostEstimate(flops=1 << 20, bytes_accessed=1 << 16, transcendentals=0),
         name="feedforward",
-    )(x, b, packed, packed)
-
-
-MESH = pl.DeviceIdType.MESH
-
-
-def bits_of(n_seq, n_rows):
-    high = [("seq", 1 << b) for b in reversed(range(n_seq.bit_length() - 1))]
-    return high + [("rows", 1 << b) for b in reversed(range(n_rows.bit_length() - 1))]
-
-
-def place(bits):
-    return [lax.rem(lax.axis_index(axis) // weight, 2) for axis, weight in bits]
-
-
-def partner(bit):
-    axis, weight = bit
-    mine = lax.axis_index(axis)
-    return {axis: mine + weight - 2 * weight * lax.rem(mine // weight, 2)}
-
-
-def greet(bits):
-    barrier = pltpu.get_barrier_semaphore()
-    for bit in bits:
-        pl.semaphore_signal(barrier, inc=1, device_id=partner(bit), device_id_type=MESH)
-    pl.semaphore_wait(barrier, len(bits))
-
-
-def routes(bits):
+    )(x, b, packed, packed, kv, q, g)
+    return out, dx, grads, all_kv.reshape((n_seq,) + kv.shape), others
+
+
+def streams_of(bits, squares, hidden):
     n = len(bits)
-    one = list(range(n))
-    other = list(range(n))
+    one, other = routes(bits)
     near = max(i for i in range(n) if bits[i][0] == "seq")
-    if near + 1 < n - 1:
-        other[near], other[near + 1] = other[near + 1], other[near]
-    return one, other
-
-
-def gather_kernel(bits, count, *refs):
-    shards, fulls = refs[:count], refs[count:2 * count]
-    own_sem, send_sem, recv_sem = refs[2 * count:]
-    me = place(bits)
-    orders = routes(bits)
-    locals_ = []
-    for a in range(count):
-        copy = pltpu.make_async_copy(shards[a], fulls[a].at[tuple(me)], own_sem.at[a])
-        copy.start()
-        locals_.append(copy)
-    greet(bits)
-    for copy in locals_:
-        copy.wait()
-    held = [set(), set()]
-    for stage in range(len(bits)):
-        copies = []
-        for half in (0, 1):
-            b = orders[half][stage]
-            for a in range(count):
-                rows = shards[a].shape[0] // 2
-                where = tuple(slice(None) if i in held[half] else me[i] for i in range(len(bits)))
-                piece = fulls[a].at[where + (pl.ds(half * rows, rows),)]
-                copy = pltpu.make_async_remote_copy(
-                    src_ref=piece, dst_ref=piece,
-                    send_sem=send_sem.at[a, half, stage], recv_sem=recv_sem.at[a, half, stage],
-                    device_id=partner(bits[b]), device_id_type=MESH)
-                copy.start()
-                copies.append(copy)
-            held[half].add(b)
-        for copy in copies:
-            copy.wait()
-
-
-def gather(shards, n_seq, n_rows, collective_id):
-    bits = bits_of(n_seq, n_rows)
-    count = len(shards)
-    outs = pl.pallas_call(
-        functools.partial(gather_kernel, bits, count),
-        out_shape=[jax.ShapeDtypeStruct((2,) * len(bits) + s.shape, s.dtype) for s in shards],
-        in_specs=[pl.BlockSpec(memory_space=pl.ANY)] * count,
-        out_specs=[pl.BlockSpec(memory_space=pl.ANY)] * count,
-        scratch_shapes=[
-            pltpu.SemaphoreType.DMA((count,)),
-            pltpu.SemaphoreType.DMA((count, 2, len(bits))),
-            pltpu.SemaphoreType.DMA((count, 2, len(bits))),
-        ],
-        compiler_params=pltpu.CompilerParams(collective_id=collective_id, has_side_effects=True),
-        name="gather",
-    )(*shards)
-    return [o.reshape((n_seq * n_rows,) + s.shape) for o, s in zip(outs, shards)]
-
-
-def scatter_kernel(bits, width, x_ref, out_ref, *refs):
-    n = len(bits)
-    send = refs[:n]
-    recv = refs[n:2 * n]
-    acc = refs[2 * n:3 * n]
-    send_sem, recv_sem = refs[3 * n:]
-    rows = x_ref.shape[1]
-    f32, bf16 = jnp.float32, jnp.bfloat16
-    me = place(bits)
-    orders = [list(reversed(o)) for o in routes(bits)]
-    greet(bits)
-
-    def spread(half, stage, j, own):
-        left = sorted(orders[half][stage:])
-        b = orders[half][stage]
-        rest = [i for i in left if i != b]
-        index = 0
-        for i in left:
-            if i == b:
-                bit = me[b] if own else 1 - me[b]
-            else:
-                bit = lax.rem(j // (1 << (len(rest) - 1 - rest.index(i))), 2)
-            index = index * 2 + bit
-        return index
-
-    def block(half, stage, at):
-        if stage == 0:
-            low = x_ref[at, :, half * 2 * width:half * 2 * width + width]
-            high = x_ref[at, :, half * 2 * width + width:(half + 1) * 2 * width]
-            return jnp.concatenate([low, high], axis=0)
-        return acc[stage - 1][half, at]
-
-    for stage in range(n):
-        size = 1 << (n - 1 - stage)
-        copies = []
-        for half in (0, 1):
-            def fill(j, _, half=half, stage=stage):
-                send[stage][half, j] = block(half, stage, spread(half, stage, j, False)).astype(bf16)
-                return 0
-            lax.fori_loop(0, size, fill, 0)
-            copy = pltpu.make_async_remote_copy(
-                src_ref=send[stage].at[half], dst_ref=recv[stage].at[half],
-                send_sem=send_sem.at[half, stage], recv_sem=recv_sem.at[half, stage],
-                device_id=partner(bits[orders[half][stage]]), device_id_type=MESH)
-            copy.start()
-            copies.append(copy)
-        for half in (0, 1):
-            copies[half].wait()
-
-            def add(j, _, half=half, stage=stage):
-                own = block(half, stage, spread(half, stage, j, True))
-                acc[stage][half, j] = own + recv[stage][half, j].astype(f32)
-                return 0
-            lax.fori_loop(0, size, add, 0)
-    for half in (0, 1):
-        total = acc[n - 1][half, 0]
-        out_ref[:, half * 2 * width:half * 2 * width + width] = total[:rows]
-        out_ref[:, half * 2 * width + width:(half + 1) * 2 * width] = total[rows:]
-
-
-def scatter(x, n_seq, n_rows, collective_id):
-    bits = bits_of(n_seq, n_rows)
-    n, rows, columns = x.shape
-    width = columns // 4
-    shapes = [(2, 1 << (len(bits) - 1 - s), 2 * rows, width) for s in range(len(bits))]
-    return pl.pallas_call(
-        functools.partial(scatter_kernel, bits, width),
-        out_shape=jax.ShapeDtypeStruct((rows, columns), jnp.float32),
-        in_specs=[pl.BlockSpec(memory_space=pltpu.VMEM)],
-        out_specs=pl.BlockSpec(memory_space=pltpu.VMEM),
-        scratch_shapes=[pltpu.VMEM(s, jnp.bfloat16) for s in shapes]
-        + [pltpu.VMEM(s, jnp.bfloat16) for s in shapes]
-        + [pltpu.VMEM(s, jnp.float32) for s in shapes]
-        + [pltpu.SemaphoreType.DMA((2, len(bits))), pltpu.SemaphoreType.DMA((2, len(bits)))],
-        compiler_params=pltpu.CompilerParams(
-            collective_id=collective_id, has_side_effects=True, vmem_limit_bytes=40 << 20),
-        name="scatter",
-    )(x)
+    last = [i for i in (near, near + 1) if i < n - 1]
+    last += [i for i in range(n - 1) if i not in last] + [n - 1]
+    early, late = list(range(n)), list(range(2, n + 2))
+    split = list(range(2)) + list(range(4, n + 2))
+    unit = squares // 48 * 16
+    head = hidden // 12 // 16 * 16
+    tail = hidden // 6 // 16 * 16
+    rest = (hidden - 2 * head - tail) // 2
+    return [
+        (0, 0, 16, one, early), (0, 16, 16, other, early),
+        (1, 0, unit, one, early), (1, unit, squares - unit, other, early),
+        (2, 0, head, one, early), (2, head, head, other, early),
+        (2, 2 * head, rest, one, late), (2, 2 * head + rest, rest, other, late),
+        (2, 2 * head + 2 * rest, tail, last, split),
+    ]
 
 
 def front_kernel(
-    bits, here, M, chunk,
-    x_ref, c_ref, scale_ref, norm_ref, near_ref, far_ref, sq_ref, pr_ref,
-    q_ref, g_ref, kv_ref, xa_ref, xf_ref, b_ref, wide_ref, wp,
-    sq_all, pr_all, stage_q, stage_o, stage_p,
-    own_sem, send_sem, recv_sem, kv_send, kv_recv,
+    bits, here, M, chunk, streams,
+    x_ref, c_ref, scale_ref, norm_ref, near_ref, far_ref, query_ref, pair_ref, output_ref, up_ref, down_ref,
+    q_ref, g_ref, kv_ref, xa_ref, xf_ref, b_ref, wide_ref, wp, hidden_ref,
+    pr_all, sq_all, hidden_own, stage_q, stage_o, stage_p,
+    own_sem, send_sem, recv_sem,
 ):
     f32, bf16 = jnp.float32, jnp.bfloat16
     T, D = x_ref.shape
     n = len(bits)
     me = place(bits)
-    seq_bits = [i for i in range(n) if bits[i][0] == "seq"]
-    own = [pltpu.make_async_copy(s, d.at[tuple(me)], own_sem.at[i])
-           for i, (s, d) in enumerate(((sq_ref, sq_all), (pr_ref, pr_all)))]
-    for copy in own:
-        copy.start()
+    owned = query_ref.shape[0]
+    tiles = up_ref.shape[1] // D
+    rows = hidden_own.shape[0] // 2
+    up = up_ref[...].astype(f32)
+    hidden_own[:rows, :] = jnp.concatenate([up[:, j * D:(j + 1) * D] for j in range(tiles)], axis=0).astype(bf16)
+    hidden_own[rows:, :] = down_ref[...]
+    own = pltpu.make_async_copy(hidden_own, hidden_ref.at[tuple(me)], own_sem)
+    own.start()
+    squares = jnp.concatenate([query_ref[...].astype(f32), output_ref[...].astype(f32)], axis=0)
+    sq_all[tuple(me)] = squares.astype(bf16)
+    pairs = jnp.concatenate([pair_ref[...].astype(f32), jnp.zeros((pr_all.shape[-2] - owned, 128), f32)], axis=0)
+    pr_all[tuple(me)] = pairs.astype(bf16)
     greet(bits)
-    for copy in own:
-        copy.wait()
+    own.wait()
 
     def normalize(i):
         r = slice(i * chunk, (i + 1) * chunk)
@@ -615,74 +591,32 @@
         part = i * chunk // (T // here)
         b_ref[r, :] = (c_ref[r, :].astype(f32) * scale_ref[part:part + 1, :]).astype(bf16)
 
-    orders = routes(bits)
-    held = [set(), set()]
-    chunks = T // chunk
-    for stage in range(n):
-        copies = []
-        for half in (0, 1):
-            b = orders[half][stage]
-            for a, full in enumerate((pr_all, sq_all)):
-                rows = full.shape[-2]
-                if half == 0:
-                    part = pl.ds(0, rows // 32 * 16)
-                else:
-                    part = pl.ds(rows // 32 * 16, rows - rows // 32 * 16)
-                where = tuple(slice(None) if i in held[half] else me[i] for i in range(n))
-                piece = full.at[where + (part,)]
-                copy = pltpu.make_async_remote_copy(
-                    src_ref=piece, dst_ref=piece,
-                    send_sem=send_sem.at[a, half, stage], recv_sem=recv_sem.at[a, half, stage],
-                    device_id=partner(bits[b]), device_id_type=MESH)
-                copy.start()
-                copies.append(copy)
-            held[half].add(b)
-        for i in range(chunks):
-            if i % n == stage:
-                normalize(i)
-        for copy in copies:
-            copy.wait()
-
-    owned = D // (1 << n)
-    for d in range(1 << n):
-        at = tuple((d >> (n - 1 - i)) & 1 for i in range(n))
-        r = slice(d * owned, (d + 1) * owned)
-        squares = sq_all[at].astype(f32)
-        stage_q[r, :] = squares[:owned]
-        stage_o[r, :] = squares[owned:2 * owned]
-        stage_p[r, :] = pr_all[at].astype(f32)[:owned]
-    wp[...] = stage_p[...].astype(bf16)
+    def unpack():
+        for d in range(1 << n):
+            at = tuple((d >> (n - 1 - i)) & 1 for i in range(n))
+            r = slice(d * owned, (d + 1) * owned)
+            both = sq_all[at].astype(f32)
+            stage_q[r, :] = both[:owned]
+            stage_o[r, :] = both[owned:2 * owned]
+            stage_p[r, :] = pr_all[at].astype(f32)[:owned]
+        wp[...] = stage_p[...].astype(bf16)
+        wide_ref[0] = stage_q[...].astype(bf16)
+        wide_ref[1] = stage_o[...].astype(bf16)
 
     block = lax.axis_index("seq")
     per = T // here // M
     tables = []
     for j in range(per):
         tables.append(turn_factors(near_ref[...], far_ref[pl.ds(block * per + j, 1), :]))
-
     first = lax.broadcasted_iota(jnp.int32, (M, 128), 1) < HD
-    at = tuple(me[i] for i in seq_bits)
-    for s in range(here):
-        for j in range(per):
-            r = slice((s * per + j) * M, (s * per + j + 1) * M)
-            kv = dot(xa_ref[r, :], wp[...], 1, 0)
-            turned = turn(kv, *tables[j])
-            kv_ref[at + (s, pl.ds(j * M, M))] = jnp.where(first, turned, kv).astype(bf16)
-
-    def kv_stage(k, held):
-        copies = []
-        for half in (0, 1):
-            order = seq_bits if half == 0 else seq_bits[-1:] + seq_bits[:-1]
-            b = order[k]
-            rows = T // here // 2
-            where = tuple(slice(None) if i in held[half] else me[i] for i in seq_bits)
-            piece = kv_ref.at[where + (slice(None), pl.ds(half * rows, rows))]
-            copy = pltpu.make_async_remote_copy(
-                src_ref=piece, dst_ref=piece, send_sem=kv_send.at[half, k], recv_sem=kv_recv.at[half, k],
-                device_id=partner(bits[b]), device_id_type=MESH)
-            copy.start()
-            copies.append(copy)
-            held[half].add(b)
-        return copies
+
+    def keys(i):
+        r = slice(i * chunk, (i + 1) * chunk)
+        kv = dot(xa_ref[r, :], wp[...], 1, 0)
+        for j in range(chunk // M):
+            part = kv[j * M:(j + 1) * M]
+            turned = turn(part, *tables[(i * chunk // M + j) % per])
+            kv_ref[i * chunk + j * M:i * chunk + (j + 1) * M, :] = jnp.where(first, turned, part).astype(bf16)
 
     def queries(i):
         r = slice(i * chunk, (i + 1) * chunk)
@@ -698,53 +632,295 @@
         r = slice(i * chunk, (i + 1) * chunk)
         g_ref[r, :] = dot(b_ref[r, :], wide_ref[1], 1, 1).astype(bf16)
 
-    held = [set(), set()]
-    jobs = [functools.partial(f, i) for f in (queries, gradients) for i in range(chunks)]
-    for k in range(len(seq_bits)):
-        copies = kv_stage(k, held)
-        if k == 0:
-            wide_ref[0] = stage_q[...].astype(bf16)
-            wide_ref[1] = stage_o[...].astype(bf16)
-        for i, job in enumerate(jobs):
-            if i * len(seq_bits) // len(jobs) == k:
-                job()
+    chunks = T // chunk
+    rounds = max(s[4][-1] for s in streams) + 1
+    jobs = [[] for _ in range(rounds)]
+    for i in range(chunks):
+        jobs[min(i, n - 1)].append(functools.partial(normalize, i))
+    jobs[min(n, rounds - 1)] += [unpack] + [functools.partial(f, i) for f in (keys, queries, gradients) for i in range(chunks)]
+    arrays = (pr_all, sq_all, hidden_ref)
+    held = [set() for _ in streams]
+    for now in range(rounds):
+        copies = []
+        for i, (a, start, size, order, when) in enumerate(streams):
+            if now not in when:
+                continue
+            stage = when.index(now)
+            where = tuple(slice(None) if b in held[i] else me[b] for b in range(n))
+            piece = arrays[a].at[where + (pl.ds(start, size),)]
+            copy = pltpu.make_async_remote_copy(
+                src_ref=piece, dst_ref=piece, send_sem=send_sem.at[i, stage], recv_sem=recv_sem.at[i, stage],
+                device_id=partner(bits[order[stage]]), device_id_type=MESH)
+            copy.start()
+            copies.append(copy)
+            held[i].add(order[stage])
+        for job in jobs[now]:
+            job()
         for copy in copies:
             copy.wait()
 
 
-def front(x, c, scale, norms, squares, pairs, here, length, M, n_seq, n_rows, collective_id, chunk=256):
+def front(x, c, scale, norms, query, pair, output, up, down, here, length, M, n_seq, n_rows, collective_id, chunk=256):
     bits = bits_of(n_seq, n_rows)
     n = len(bits)
-    n_s = n_seq.bit_length() - 1
     T, D = x.shape
+    owned, hidden = query.shape[0], 2 * down.shape[0]
     f32, bf16 = jnp.float32, jnp.bfloat16
     near, far = turn_tables(length, M)
     vmem = pl.BlockSpec(memory_space=pltpu.VMEM)
     token = jax.ShapeDtypeStruct((T, D), bf16)
-    outs = pl.pallas_call(
-        functools.partial(front_kernel, bits, here, M, chunk),
-        out_shape=[token, token, jax.ShapeDtypeStruct((2,) * n_s + (here, T // here, 128), bf16), token, token, token,
-                   jax.ShapeDtypeStruct((2, D, D), bf16), jax.ShapeDtypeStruct((D, 128), bf16)],
-        in_specs=[vmem] * 8,
-        out_specs=[vmem] * 8,
+    streams = streams_of(bits, 2 * owned, hidden)
+    q, g, kv, xa, xf, b, wide, wp, packed = pl.pallas_call(
+        functools.partial(front_kernel, bits, here, M, chunk, streams),
+        out_shape=[token, token, jax.ShapeDtypeStruct((T, 128), bf16), token, token, token,
+                   jax.ShapeDtypeStruct((2, D, D), bf16), jax.ShapeDtypeStruct((D, 128), bf16),
+                   jax.ShapeDtypeStruct((2,) * n + (hidden, D), bf16)],
+        in_specs=[vmem] * 11,
+        out_specs=[vmem] * 8 + [pl.BlockSpec(memory_space=pl.ANY)],
         scratch_shapes=[
-            pltpu.VMEM((2,) * n + squares.shape, bf16),
-            pltpu.VMEM((2,) * n + pairs.shape, bf16),
+            pltpu.VMEM((2,) * n + (32, 128), bf16),
+            pltpu.VMEM((2,) * n + (2 * owned, D), bf16),
+            pltpu.VMEM((hidden, D), bf16),
             pltpu.VMEM((D, D), f32),
             pltpu.VMEM((D, D), f32),
             pltpu.VMEM((D, 128), f32),
-            pltpu.SemaphoreType.DMA((2,)),
-            pltpu.SemaphoreType.DMA((2, 2, n)),
-            pltpu.SemaphoreType.DMA((2, 2, n)),
-            pltpu.SemaphoreType.DMA((2, n_s)),
-            pltpu.SemaphoreType.DMA((2, n_s)),
+            pltpu.SemaphoreType.DMA,
+            pltpu.SemaphoreType.DMA((len(streams), n)),
+            pltpu.SemaphoreType.DMA((len(streams), n)),
         ],
         compiler_params=pltpu.CompilerParams(
             collective_id=collective_id, has_side_effects=True, vmem_limit_bytes=56 << 20),
         name="front",
-    )(x, c, scale, norms, near, far, squares, pairs)
-    q, g, kv, xa, xf, b, wide, pair = outs
-    return q, g, kv.reshape(n_seq, here, T // here, 128), xa, xf, b, wide, pair
+    )(x, c, scale, norms, near, far, query, pair, output, up, down)
+    return q, g, kv, xa, xf, b, wide, wp, packed.reshape(1 << n, hidden, D)
+
+
+class Halving:
+    def __init__(self, bits, order, me, first, send, recv, acc, send_sem, recv_sem):
+        self.bits, self.order, self.me, self.first = bits, order, me, first
+        self.send, self.recv, self.acc = send, recv, acc
+        self.send_sem, self.recv_sem = send_sem, recv_sem
+        self.copy = None
+
+    def spot(self, stage, j, own):
+        left = sorted(self.order[stage:])
+        b = self.order[stage]
+        rest = [i for i in left if i != b]
+        index = 0
+        for i in left:
+            if i == b:
+                bit = self.me[b] if own else 1 - self.me[b]
+            else:
+                bit = lax.rem(j // (1 << (len(rest) - 1 - rest.index(i))), 2)
+            index = index * 2 + bit
+        return index
+
+    def block(self, stage, at):
+        return self.first(at) if stage == 0 else self.acc[stage - 1][at]
+
+    def start(self, stage):
+        def fill(j, _):
+            self.send[stage][j] = self.block(stage, self.spot(stage, j, False)).astype(jnp.bfloat16)
+            return 0
+
+        lax.fori_loop(0, 1 << (len(self.order) - 1 - stage), fill, 0)
+        self.copy = pltpu.make_async_remote_copy(
+            src_ref=self.send[stage], dst_ref=self.recv[stage],
+            send_sem=self.send_sem.at[stage], recv_sem=self.recv_sem.at[stage],
+            device_id=partner(self.bits[self.order[stage]]), device_id_type=MESH)
+        self.copy.start()
+
+    def finish(self, stage):
+        self.copy.wait()
+
+        def add(j, _):
+            own = self.block(stage, self.spot(stage, j, True))
+            self.acc[stage][j] = own + self.recv[stage][j].astype(jnp.float32)
+            return 0
+
+        lax.fori_loop(0, 1 << (len(self.order) - 1 - stage), add, 0)
+
+
+def halving_shapes(stages, rows, columns):
+    sizes = [(1 << (stages - 1 - s), rows, columns) for s in range(stages)]
+    half = [pltpu.VMEM(s, jnp.bfloat16) for s in sizes]
+    return half + half + [pltpu.VMEM(s, jnp.float32) for s in sizes] + [
+        pltpu.SemaphoreType.DMA((stages,)), pltpu.SemaphoreType.DMA((stages,))]
+
+
+def post_kernel(bits, here, M, order, moved, chunk, *refs):
+    (sums_ref, o_hbm, dq_hbm, *refs) = refs
+    backs, refs = refs[:len(order)], refs[len(order):]
+    (xa_ref, b_ref, x_hbm, c_hbm, out_hbm, dx_hbm, wide_ref, wp_ref, norm_ref, scale_ref, near_ref, far_ref,
+     layer_ref, states_ref, square_ref, small_ref, *refs) = refs
+    f32, bf16 = jnp.float32, jnp.bfloat16
+    T, D = xa_ref.shape
+    n = len(bits)
+    seq_bits = [i for i in range(n) if bits[i][0] == "seq"]
+    n_s = len(seq_bits)
+    me = place(bits)
+    o_ref, dq_ref, x_ref, c_ref, out_ref, dx_ref, ai_ref, gq, go, gs, load_sem, *refs = refs
+
+    def take(stages):
+        nonlocal refs
+        mine, refs = refs[:3 * stages + 2], refs[3 * stages + 2:]
+        return mine[:stages], mine[stages:2 * stages], mine[2 * stages:3 * stages], mine[-2], mine[-1]
+
+    loads = [pltpu.make_async_copy(s, d, load_sem.at[i])
+             for i, (s, d) in enumerate((
+                 (dq_hbm.at[:T], dq_ref), (o_hbm.at[:T], o_ref), (out_hbm, out_ref),
+                 (x_hbm, x_ref), (dx_hbm, dx_ref), (c_hbm, c_ref)))]
+    for load in loads:
+        load.start()
+    greet(bits)
+
+    owned = D >> n
+    local = T // here
+    per = local // M
+    wide = sums_ref.shape[2] >> n_s
+
+    def keys_first(s):
+        return lambda at: sums_ref[s, :, pl.ds(pl.multiple_of(at * wide, 128), wide)]
+
+    def square_first(ref):
+        def get(at):
+            r = pl.ds(pl.multiple_of(at * owned, 8), owned)
+            return jnp.concatenate([ref[r, :D // 2], ref[r, D // 2:]], axis=0)
+        return get
+
+    def small_first(at):
+        r = pl.ds(pl.multiple_of(at * owned, 8), owned)
+        return jnp.concatenate([gs[r, :128], gs[r, 128:]], axis=0)
+
+    x_first = seq_bits[::-1]
+    z_first = x_first[1:] + x_first[:1]
+    kv = [Halving(bits, z_first if s % 2 else x_first, me, keys_first(s), *take(n_s)) for s in range(here)]
+    routes_back = [list(reversed(o)) for o in routes(bits)]
+    squares = [Halving(bits, routes_back[i], me, square_first(ref), *take(n)) for i, ref in enumerate((gq, go))]
+    small = Halving(bits, routes_back[0], me, small_first, *take(n))
+
+    for h in kv:
+        h.start(0)
+
+    block = lax.axis_index("seq")
+    loads[0].wait()
+    loads[1].wait()
+    for k, at in enumerate(order):
+        r = slice(at * M, (at + 1) * M)
+        away = functools.reduce(jnp.logical_or, [block == i for i in range(len(moved)) if moved[i] > k])
+        o_ref[r, :] = jnp.where(away, backs[k][0], o_ref[r, :])
+        dq_ref[r, :] = jnp.where(away, backs[k][1], dq_ref[r, :])
+
+    gq[...] = dot(xa_ref[...], dq_ref[...], 0, 0)
+    squares[0].start(0)
+    go[...] = dot(o_ref[...], b_ref[...], 0, 0)
+    squares[1].start(0)
+    for h in kv:
+        h.finish(0)
+        h.start(1)
+    loads[2].wait()
+    loads[3].wait()
+    chunks = T // chunk
+
+    def forward(i):
+        r = slice(i * chunk, (i + 1) * chunk)
+        total = x_ref[r, :].astype(f32) + (dot(o_ref[r, :], wide_ref[1], 1, 0) + out_ref[r, :])
+        layer_ref[r, :] = total.astype(bf16)
+
+    def backward(i):
+        r = slice(i * chunk, (i + 1) * chunk)
+        ai_ref[r, :] = dot(dq_ref[r, :], wide_ref[0], 1, 1)
+
+    jobs = [functools.partial(f, i) for f in (forward, backward) for i in range(chunks)]
+    gaps = n - 1
+    for stage in range(n):
+        for h in squares:
+            h.finish(stage)
+            if stage + 1 < n:
+                h.start(stage + 1)
+        for i, job in enumerate(jobs):
+            if i * gaps // len(jobs) == stage:
+                job()
+        if 0 < stage < n_s:
+            for h in kv:
+                h.finish(stage)
+                if stage + 1 < n_s:
+                    h.start(stage + 1)
+    for i, h in enumerate(squares):
+        total = h.acc[n - 1][0]
+        square_ref[i, :, :D // 2] = total[:owned]
+        square_ref[i, :, D // 2:] = total[owned:]
+
+    first = lax.broadcasted_iota(jnp.int32, (M, 128), 1) < HD
+    grads = []
+    for s in range(here):
+        home = kv[s].acc[n_s - 1][0].T
+        for j in range(per):
+            factors = turn_factors(near_ref[...], far_ref[pl.ds(block * per + j, 1), :])
+            part = home[j * M:(j + 1) * M]
+            turned = turn_back(part, *factors) * LN2
+            grads.append(jnp.where(first, turned, part).astype(bf16))
+    pairs = jnp.concatenate(grads, axis=0)
+    gs[:, :128] = dot(xa_ref[...], pairs, 0, 0)
+    loads[4].wait()
+    loads[5].wait()
+    totals = [jnp.zeros((1, D), f32) for _ in range(4)]
+    for i in range(chunks):
+        r = slice(i * chunk, (i + 1) * chunk)
+        x = x_ref[r, :].astype(f32)
+        x = x - jnp.mean(x, axis=1, keepdims=True)
+        inverse = lax.rsqrt(jnp.mean(x * x, axis=1, keepdims=True) + 1e-05)
+        unit = x * inverse
+        ai = ai_ref[r, :] + dot(pairs[r], wp_ref[...], 1, 1)
+        fi = dx_ref[r, :]
+        for k, part in enumerate((ai * unit, ai, fi * unit, fi)):
+            totals[k] = totals[k] + jnp.sum(part, axis=0, keepdims=True)
+        both = ai * norm_ref[0:1, :] + fi * norm_ref[2:3, :]
+        middle = jnp.mean(both, axis=1, keepdims=True)
+        slope = jnp.mean(both * unit, axis=1, keepdims=True)
+        part = i * chunk // local
+        up = c_ref[r, :].astype(f32) * scale_ref[part:part + 1, :]
+        states_ref[r, :] = (up + inverse * (both - middle - unit * slope)).astype(bf16)
+    rows = jnp.concatenate(totals + [jnp.zeros((124, D), f32)], axis=0)
+    gs[:, 128:] = rows.T
+    for stage in range(n):
+        small.start(stage)
+        small.finish(stage)
+    total = small.acc[n - 1][0]
+    small_ref[:, :128] = total[:owned]
+    small_ref[:, 128:] = total[owned:]
+
+
+def post(sums, o, dq, backs, order, moved, xa, b, x, c, out, dx, wide, wp, norms, scales,
+         here, length, M, n_seq, n_rows, collective_id, chunk=256):
+    bits = bits_of(n_seq, n_rows)
+    n, n_s = len(bits), n_seq.bit_length() - 1
+    T, D = xa.shape
+    owned = D >> n
+    f32, bf16 = jnp.float32, jnp.bfloat16
+    near, far = turn_tables(length, M)
+    vmem, anywhere = pl.BlockSpec(memory_space=pltpu.VMEM), pl.BlockSpec(memory_space=pl.ANY)
+    token = jax.ShapeDtypeStruct((T, D), bf16)
+    scratch = [
+        *[pltpu.VMEM((T, D), bf16)] * 4, *[pltpu.VMEM((T, D), f32)] * 3,
+        pltpu.VMEM((D, D), f32), pltpu.VMEM((D, D), f32), pltpu.VMEM((D, 256), f32),
+        pltpu.SemaphoreType.DMA((6,)),
+    ]
+    for _ in range(here):
+        scratch += halving_shapes(n_s, 128, length // n_seq)
+    for _ in range(2):
+        scratch += halving_shapes(n, 2 * owned, D // 2)
+    scratch += halving_shapes(n, 2 * owned, 128)
+    return pl.pallas_call(
+        functools.partial(post_kernel, bits, here, M, tuple(order), tuple(moved), chunk),
+        out_shape=[token, token, jax.ShapeDtypeStruct((2, owned, D), f32), jax.ShapeDtypeStruct((owned, 256), f32)],
+        in_specs=[vmem, anywhere, anywhere] + [vmem] * len(backs) + [vmem] * 2 + [anywhere] * 4 + [vmem] * 6,
+        out_specs=[vmem] * 4,
+        scratch_shapes=scratch,
+        compiler_params=pltpu.CompilerParams(
+            collective_id=collective_id, has_side_effects=True, vmem_limit_bytes=60 << 20),
+        name="post",
+    )(sums, o, dq, *backs, xa, b, x, c, out, dx, wide, wp, norms, scales, near, far)
 
 
 def layer_norm(values):
@@ -796,11 +972,10 @@
     mean = sum(cost(t) + cost(k) for t, k in zip(takes, keeps)) / n
     lists = ([], [], [])
     for take, keep in zip(takes, keeps):
-        keep = list(keep)
-        head, middle = [], list(take)
-        while keep and cost(head) + price(keep[0][2]) / 2 < 0.22 * mean:
+        keep, head, middle = list(keep), list(take[:1]), list(take[1:])
+        while len(keep) > 1 and cost(head) + price(keep[0][2]) / 2 < 0.32 * mean:
             head.append(keep.pop(0))
-        while keep and cost(middle) + price(keep[0][2]) / 2 < 0.56 * mean and cost(keep) > 0.22 * mean:
+        while len(keep) > 1 and cost(middle) + price(keep[0][2]) / 2 < 0.42 * mean and cost(keep) > 0.24 * mean:
             middle.append(keep.pop(0))
         for part, steps in zip(lists, (head, middle, keep)):
             part.append(steps)
@@ -832,32 +1007,24 @@
     P = 2 * HD
     scale = HD ** -0.5
     own_rows = query_projection.shape[0]
-    aligned = (2 * own_rows) % 16 == 0 and own_rows % 8 == 0
+    aligned = own_rows % 8 == 0 and here % 2 == 0
 
     rows_here = offset + jnp.arange(length_here, dtype=jnp.int32)
     cosine, sine_vals = rotary_tables(rows_here.astype(f32))
-    source = states.astype(f32).reshape(T, D)
-    unit, inverse = layer_norm(source)
     table_rows = jnp.arange(subset_weight.shape[0], dtype=jnp.int32)
     row_scale = jnp.sum(
         jnp.where(table_rows[None, :] == subsets[:, None], subset_weight[None, :], 0.0), axis=1
     )
-    upstream = (cotangent.astype(f32) * row_scale[:, None, None]).reshape(T, D)
-
     if aligned:
-        tiles = FF // D
-        packed = jnp.concatenate([
-            jnp.swapaxes(up_projection.reshape(own_rows, tiles, D), 0, 1).reshape(-1, D), down_projection])
-        packed = lax.all_gather(packed, both, axis=0)
-        squares = jnp.concatenate([query_projection, output_projection], axis=0)
-        pairs = jnp.pad(pair_projection, ((0, -own_rows % 32), (0, 0)))
         norms = jnp.stack([gain_attn, shift_attn, gain_ffn, shift_ffn])
         scales = jnp.broadcast_to(row_scale[:, None], (here, D))
-        queries, out_grad, all_kv, attention_input, feedforward_input, branch_grad, squares, full_pair = front(
-            states.reshape(T, D), cotangent.reshape(T, D), scales, norms, squares, pairs,
-            here, length, M, n_seq, n_rows, 1)
-        full_query, full_output = squares[0], squares[1]
+        queries, out_grad, own_kv, attention_input, feedforward_input, branch_grad, wide, full_pair, packed = front(
+            states.reshape(T, D), cotangent.reshape(T, D), scales, norms, query_projection, pair_projection,
+            output_projection, up_projection, down_projection, here, length, M, n_seq, n_rows, 1)
     else:
+        source = states.astype(f32).reshape(T, D)
+        unit, inverse = layer_norm(source)
+        upstream = (cotangent.astype(f32) * row_scale[:, None, None]).reshape(T, D)
         big = jnp.stack([up_projection, down_projection.reshape(up_projection.shape)])
         big = lax.all_gather(big, both, axis=1, tiled=True)
         full_up, full_down = big[0], big[1].reshape(FF, D)
@@ -884,43 +1051,58 @@
 
     order, moved, most, tables = plan(n_seq, here, per, M, tk)
     own = here * per
-    q_tiles, g_tiles = queries.reshape(own, M, D), out_grad.reshape(own, M, D)
-    others = []
-    for k in range(most):
-        s, j = order[k]
-        pairs_of = [(i, n_seq - 1 - i) for i in range(n_seq) if moved[i] > k]
-        others.append(lax.ppermute(jnp.stack([q_tiles[s * per + j], g_tiles[s * per + j]]), "seq", pairs_of))
+    at_slots = [s * per + j for s, j in order[:most]]
     steps = []
     for table in tables:
         mine = jnp.asarray(table)[block]
         steps.append(tuple(mine[:, c] for c in range(4)))
-    done = attention(steps[0], queries, out_grad, None, all_kv, M, tk, most)
-
-    ffn_x, done = lax.optimization_barrier((feedforward_input, done))
+    q_tiles, g_tiles = queries.reshape(own, M, D), out_grad.reshape(own, M, D)
+
+    def send(k):
+        pairs_of = [(i, n_seq - 1 - i) for i in range(n_seq) if moved[i] > k]
+        return lax.ppermute(jnp.stack([q_tiles[at_slots[k]], g_tiles[at_slots[k]]]), "seq", pairs_of)
+
+    def send_back(done, k):
+        pairs_of = [(n_seq - 1 - i, i) for i in range(n_seq) if moved[i] > k]
+        tile = slice((own + k) * M, (own + k + 1) * M)
+        return lax.ppermute(jnp.stack([done[0][tile], done[1][tile]]), "seq", pairs_of)
+
     if aligned:
-        ffn_out, ffn_input_grad, ffn_grads = ffn_packed(ffn_x, branch_grad, packed, n_seq, n_rows)
+        ffn_out, ffn_input_grad, ffn_grads, all_kv, first_taken = ffn_packed(
+            feedforward_input, branch_grad, packed, own_kv.reshape(here, length_here, P), queries, out_grad,
+            at_slots[:1], moved, M, n_seq, 3)
     else:
-        ffn_out, ffn_input_grad, grad_up, grad_down = ffn(ffn_x, branch_grad, full_up, full_down)
-        ffn_grads = jnp.concatenate(
-            [grad_up.reshape(n_seq, n_rows, -1, D), grad_down.reshape(n_seq, n_rows, -1, D)], axis=2)
-        ffn_grads = jnp.swapaxes(ffn_grads, 0, 1)
-    done, ffn_out = lax.optimization_barrier((done, ffn_out))
-    ffn_grads = lax.psum_scatter(ffn_grads, "rows", scatter_dimension=0, tiled=True)[0]
-    ffn_grads = lax.psum_scatter(ffn_grads, "seq", scatter_dimension=0, tiled=True)[0]
+        first_taken = send(0)[None]
+        ffn_out, ffn_input_grad, grad_up, grad_down = ffn(feedforward_input, branch_grad, full_up, full_down)
+        ffn_grads = jnp.concatenate([grad_up.reshape(n, -1, D), grad_down.reshape(n, -1, D)], axis=1)
+    ffn_grads = lax.psum_scatter(ffn_grads, both, scatter_dimension=0, tiled=True)[0]
+    done = attention(steps[0], queries, out_grad, first_taken, 0, all_kv, M, tk, most)
+    backs = [send_back(done, 0)]
+    if most > 1:
+        taken = jnp.stack([send(k) for k in range(1, most)])
+        done = attention(steps[1], queries, out_grad, taken, 1, all_kv, M, tk, most, done)
+    else:
+        done = attention(steps[1], queries, out_grad, None, 0, all_kv, M, tk, most, done)
+    backs += [send_back(done, k) for k in range(1, most)]
     half = ffn_grads.shape[0] // 2
     final_up = ffn_grads[:half]
     if aligned:
         final_up = jnp.swapaxes(final_up.reshape(FF // D, own_rows, D), 0, 1)
     final_up = final_up.reshape(-1, FF).astype(f32)
     final_down = ffn_grads[half:].astype(f32)
-
-    done = attention(steps[1], queries, out_grad, jnp.stack(others), all_kv, M, tk, most, done)
-    backs = []
-    for k in range(most):
-        pairs_of = [(n_seq - 1 - i, i) for i in range(n_seq) if moved[i] > k]
-        tile = slice((own + k) * M, (own + k + 1) * M)
-        backs.append(lax.ppermute(jnp.stack([done[0][tile], done[1][tile]]), "seq", pairs_of))
-    attended, query_pre_grad, pair_terms = attention(steps[2], queries, out_grad, None, all_kv, M, tk, most, done)
+    attended, query_pre_grad, pair_terms = attention(steps[2], queries, out_grad, None, 0, all_kv, M, tk, most, done)
+    if aligned:
+        layer_out, grad_states, squares, small = post(
+            pair_terms, attended, query_pre_grad, backs, at_slots, moved, attention_input, branch_grad,
+            states.reshape(T, D), cotangent.reshape(T, D), ffn_out, ffn_input_grad, wide, full_pair, norms, scales,
+            here, length, M, n_seq, n_rows, 2)
+        vectors = small[:, P:]
+        return (
+            layer_out.reshape(states.shape), grad_states.reshape(states.shape),
+            vectors[:, 0], vectors[:, 1], vectors[:, 2], vectors[:, 3],
+            squares[0], small[:, :P], squares[1], final_up, final_down,
+        )
+
     a_own, d_own = list(attended.reshape(-1, M, D)[:own]), list(query_pre_grad.reshape(-1, M, D)[:own])
     count = jnp.asarray(np.array(moved, np.int32))[block]
     for k in range(most):
@@ -960,11 +1142,7 @@
     grad_states = grad_states.astype(bf16).reshape(here, length_here, D)
 
     last = jnp.concatenate([grad_query, grad_pair, jnp.pad(sums, ((0, 0), (0, 124))), grad_output], axis=1)
-    if aligned:
-        last = jnp.pad(last, ((0, 0), (0, -last.shape[1] % 512)))
-        last = scatter(last.reshape(n, own_rows, -1), n_seq, n_rows, 3)
-    else:
-        last = lax.psum_scatter(last.astype(bf16), both, scatter_dimension=0, tiled=True).astype(f32)
+    last = lax.psum_scatter(last.astype(bf16), both, scatter_dimension=0, tiled=True).astype(f32)
     vectors = last[:, D + P:]
     at = D + P + 128
     return (

time: 575 us -> 426 us (0.74)
  waiting for transfers between devices: 59.7 us -> 0.03 us
  starting transfers between devices: 39.8 us -> 6.56 us
  other arithmetic: 30.5 us -> 4.36 us
  matrix products: 16.8 us -> 0 us
  local copies, waits for them, and re-layouts: 33 us -> 20.7 us
    ppermute x6 -> x5, waiting for transfers between devices: 59.7 us -> 0.01 us  [the longest x3 0.01 us: send_back(): lax.ppermute(jnp.stack([done[0][tile], done[1][tile]]), 'seq', pairs_of)]
    all_to_all x1 -> x0, starting transfers between devices: 26.4 us -> none  [local(): lax.all_to_all(pair_terms, 'seq', split_axis=0, concat_axis=0, tiled=True)]
    dot_general x6 -> x0, matrix products: 16.8 us -> none  [the longest x1 6.32 us: local(): lax.dot_general(query_pre_grad, full_query, (((1,), (1,)), ((), ())), pre...]
    concatenate x6 -> x0, other arithmetic: 7.47 us -> none  [the longest x1 2.66 us: local(): jnp.concatenate([grad_query, grad_pair, jnp.pad(sums, ((0, 0), (0, 124)))...]
    ppermute x6 -> x5, starting transfers between devices: 13.4 us -> 6.53 us  [the longest x3 3.94 us: send_back(): lax.ppermute(jnp.stack([done[0][tile], done[1][tile]]), 'seq', pairs_of)]
    unnamed x49 -> x12, local copies, waits for them, and re-layouts: 10 us -> 3.27 us
  transfers between devices with their start and end apart: 10 -> 6, of which waited for: 6 -> 0; matrix products, arithmetic and copies ran while one was open for 13% -> 3% of each run, Pallas kernels for 57% -> 53%
where the time goes in v3:
time: 426 us; the launch traced here: 421 us
  Pallas kernels  375 us (88%)
  local copies, waits for them, and re-layouts  20.7 us (5%)
  between operations  14.5 us (3%)
  starting transfers between devices  6.56 us (2%)
  other arithmetic  4.36 us (1%)
    pallas_call x3, Pallas kernels, attention(): pl.pallas_call(kernel, grid_spec=pltpu.PrefetchScalarGridSpec(num_scalar_...  138 us
    pallas_call x1, Pallas kernels, front(): pl.pallas_call(functools.partial(front_kernel, bits, here, M, chunk, stre...  86.6 us
    pallas_call x1, Pallas kernels, post(): pl.pallas_call(functools.partial(post_kernel, bits, here, M, tuple(order)...  85.9 us
    pallas_call x1, Pallas kernels, ffn_packed(): pl.pallas_call(functools.partial(ffn_packed_kernel, C, bits, M, tuple(ord...  63.9 us
  transfers between devices with their start and end apart: 6, of which 0 were waited for; matrix products, arithmetic and copies ran while one was open for 3% of the time, Pallas kernels for 53%

profile of v3, /device:TPU:0, one launch (start us, length us, event | category | flops | bytes accessed | tf_op | source)
XLA Modules:
  0.0 421.0 jit_solution(8062916132688052465)
XLA Ops:
  10.0 0.9 fusion.1
  12.1 86.6 %front.1 = (bf16[1024,768]{1,0:T(8,128)(2,1)}, bf16[1024,768]{1,0:T(8,128)(2,1)}, bf16[1024,128]{1,0:T(8,128)(2,1)}, bf16[1024,768]{1,0:T(8,128)(2,1)}, bf16[102...) custom-call(bf16[1024,768]{1,0:T(8,128)(2,1)} %bitcast.63, ...), custom_call_target="tpu_custom_call" | custom-call | tf_op jit(solution)/shard_map/front/pallas_call | solution.py:673
  98.7 63.9 %feedforward.1 = (f32[1024,768]{1,0:T(8,128)}, f32[1024,768]{1,0:T(8,128)}, bf16[32,192,768]{2,1,0:T(8,128)(2,1)}, bf16[2,2,2,2,512,128]{5,4,3,2,1,0:T(8,128)(2,1)}, bf16[1,2,128,768]{3,2,1,0:T(8,128)(2,1)}) custom-call(bf16[1024,768]{1,0:T(8,128)(2,1)} %get-tuple-element.40.x_ref, bf16[1024,768]{1,0:T(8,128)(2,1)} %get-tuple-element.41.b_ref.refs_7_, ...), custom_call_target="tpu_custom_call" | custom-call | flops 1048576 | bytes 65536 | tf_op jit(solution)/shard_map/feedforward/pallas_call | solution.py:499
  162.7 1.3 slice_bitcast_fusion.8
  164.0 1.3 collective-permute-start.1
  165.3 1.3 collective-permute-start
  168.1 47.1 %attention.3 = (bf16[1408,768]{1,0:T(8,128)(2,1)}, bf16[1408,768]{1,0:T(8,128)(2,1)}, f32[2,128,4096]{2,1,0:T(8,128)}) custom-call(s32[4]{0:T(128)} %get-tuple-element.72.slot_ref, s32[4]{0:T(128)} %get-tuple-element.71.seq_ref, s32[4]{0:T(128)} %get-tuple-element.70.row_ref, s32[4]{0:T(128)} %get-tuple-element.69.on_ref, ...), custom_call_target="tpu_custom_call" | custom-call | flops 1048576 | bytes 65536 | tf_op jit(solution)/shard_map/attention/pallas_call | solution.py:228
  215.2 0.9 slice_bitcast_fusion.5
  216.1 0.9 slice_bitcast_fusion.4
  217.1 1.3 collective-permute-start.2
  219.2 0.9 pad_maximum_fusion.other_ref
  220.1 55.5 %attention.4 = (bf16[1408,768]{1,0:T(8,128)(2,1)}, bf16[1408,768]{1,0:T(8,128)(2,1)}, f32[2,128,4096]{2,1,0:T(8,128)}) custom-call(s32[4]{0:T(128)} %get-tuple-element.76.slot_ref, s32[4]{0:T(128)} %get-tuple-element.75.seq_ref, s32[4]{0:T(128)} %get-tuple-element.74.row_ref, ...), custom_call_target="tpu_custom_call", output_to_operand_aliasing={{0}: (10, {}), {1}: (11, {}), {2}: (12, {})} | custom-call | flops 1048576 | bytes 65536 | tf_op jit(solution)/shard_map/attention/pallas_call | solution.py:228
  275.7 1.1 slice_bitcast_fusion.1
  276.7 1.0 slice_bitcast_fusion
  277.8 1.3 collective-permute-start.3
  279.2 1.3 collective-permute-start.4
  281.7 35.8 %attention.5 = (bf16[1408,768]{1,0:T(8,128)(2,1)}, bf16[1408,768]{1,0:T(8,128)(2,1)}, f32[2,128,4096]{2,1,0:T(8,128)}) custom-call(s32[5]{0:T(128)} %get-tuple-element.92.a, s32[5]{0:T(128)} %get-tuple-element.91.b, s32[5]{0:T(128)} %get-tuple-element.90.c, s32[5]{0:T(128)} %get-tuple-element.89.d, ...), custom_call_target="tpu_custom_call", output_to_operand_aliasing={{0}: (9, {}), {1}: (10, {}), {2}: (11, {})} | custom-call | flops 1048576 | bytes 65536 | tf_op jit(solution)/shard_map/attention/pallas_call | solution.py:228
  318.6 85.9 %post.1 = (bf16[1024,768]{1,0:T(8,128)(2,1)}, bf16[1024,768]{1,0:T(8,128)(2,1)}, f32[2,24,768]{2,1,0:T(8,128)}, f32[24,256]{1,0:T(8,128)}) custom-call(f32[2,128,4096]{2,1,0:T(8,128)} %get-tuple-element.52.refs_0_, bf16[1408,768]{1,0:T(8,128)(2,1)} %get-tuple-element.53.refs_1_, bf16[1408,768]{1,0:T(8,128)(2,1)} %get-tuple-element.54.refs_2_, ...), custom_call_target="tpu_custom_call" | custom-call | tf_op jit(solution)/shard_map/post/pallas_call | solution.py:914
  404.5 1.4 slice.143
  405.9 1.6 slice_reduce_fusion
  407.5 1.6 slice_bitcast_fusion.11
  409.1 1.7 fusion
  411.6 1.1 copy.55
  412.8 1.1 copy.56
  (36 shorter events, 9.4 us)
Async XLA Ops:
  7.2 401.9 %reduce-scatter.2.cloned.1.call-start = ((), (), s32[]{:S(2)}) async-start(), calls=%async_computation.1 | async-start | bytes 9732096 | tf_op jit(solution)/shard_map/reduce_scatter | solution.py:1078
  164.0 55.2 %collective-permute-start.1 = (bf16[2,128,768]{2,1,0:T(8,128)(2,1)S(1)}, bf16[2,128,768]{2,1,0:T(8,128)(2,1)S(1)}, u32[]{:S(2)}, u32[]{:S(2)}) collective-permute-start(bf16[2,128,768]{2,1,0:T(8,128)(2,1)S(1)} %pad_maximum_fusion.2), channel_id=1, source_target_pairs={{24,4},{28,0},{25,5},{29,1},{26,6},{30,2},{27,7},{31,3}} | collective-permute-start | bytes 1179656 | tf_op jit(solution)/shard_map/ppermute | solution.py:1063
  165.3 53.8 %collective-permute-start = (bf16[2,128,768]{2,1,0:T(8,128)(2,1)S(1)}, bf16[2,128,768]{2,1,0:T(8,128)(2,1)S(1)}, u32[]{:S(2)}, u32[]{:S(2)}) collective-permute-start(bf16[2,128,768]{2,1,0:T(8,128)(2,1)S(1)} %pad_maximum_fusion.1), channel_id=1, source_target_pairs={{20,8},{24,4},{28,0},{21,9},{25,5},{29,1},{22,10},{26,6},{30,2},{2... | collective-permute-start | bytes 1179656 | tf_op jit(solution)/shard_map/ppermute | solution.py:1063
  217.1 100.4 %collective-permute-start.2 = (bf16[2,128,768]{2,1,0:T(8,128)(2,1)S(1)}, bf16[2,128,768]{2,1,0:T(8,128)(2,1)S(1)}, u32[]{:S(2)}, u32[]{:S(2)}) collective-permute-start(bf16[2,128,768]{2,1,0:T(8,128)(2,1)S(1)} %pad_maximum_fusion.3), channel_id=1, source_target_pairs={{12,16},{8,20},{4,24},{0,28},{13,17},{9,21},{5,25},{1,29},{14,18},... | collective-permute-start | bytes 1179656 | tf_op jit(solution)/shard_map/ppermute | solution.py:1068
  277.8 39.8 %collective-permute-start.3 = (bf16[2,128,768]{2,1,0:T(8,128)(2,1)S(1)}, bf16[2,128,768]{2,1,0:T(8,128)(2,1)S(1)}, u32[]{:S(2)}, u32[]{:S(2)}) collective-permute-start(bf16[2,128,768]{2,1,0:T(8,128)(2,1)S(1)} %pad_maximum_fusion.4), channel_id=1, source_target_pairs={{8,20},{4,24},{0,28},{9,21},{5,25},{1,29},{10,22},{6,26},{2,30},{1... | collective-permute-start | bytes 1179656 | tf_op jit(solution)/shard_map/ppermute | solution.py:1068
  279.2 38.4 %collective-permute-start.4 = (bf16[2,128,768]{2,1,0:T(8,128)(2,1)S(1)}, bf16[2,128,768]{2,1,0:T(8,128)(2,1)S(1)}, u32[]{:S(2)}, u32[]{:S(2)}) collective-permute-start(bf16[2,128,768]{2,1,0:T(8,128)(2,1)S(1)} %pad_maximum_fusion.5), channel_id=1, source_target_pairs={{4,24},{0,28},{5,25},{1,29},{6,26},{2,30},{7,27},{3,31}} | collective-permute-start | bytes 1179656 | tf_op jit(solution)/shard_map/ppermute | solution.py:1068
  317.6 0.7 copy-start.2
  317.6 0.9 copy-start.3
  317.6 1.0 copy-start.4
  404.5 7.1 %copy-start.1 = (bf16[1024,768]{1,0:T(8,128)(2,1)S(1)}, bf16[1024,768]{1,0:T(8,128)(2,1)}, u32[]{:S(2)}) copy-start(bf16[1024,768]{1,0:T(8,128)(2,1)} %get-tuple-element.60) | copy-start | bytes 4718596
  410.8 1.9 copy-start
Sparse Core Ops, SparseCore 0:
  162.8 166.5 reduce-scatter.1

commit v4 on v3

--- a/solution.py
+++ b/solution.py
@@ -62,10 +62,12 @@
     q_ref, g_ref, other_ref, near_ref, far_ref, kv_ref, *refs,
 ):
     if not first_call:
-        refs = refs[2:]
-        before_ref, refs = refs[0], refs[1:]
-    o_ref, dq_ref, dkv_ref = refs[:3]
-    ka, va, qs, gs, qt, gt, stash, oacc, dqacc, top, limit = refs[3:]
+        before_ref, refs = refs[2], refs[3:]
+    o_ref, dq_ref, sums_ref, *refs = refs
+    given_ref = None
+    if other_ref is not None:
+        given_ref, *refs = refs
+    ka, va, qs, gs, qt, gt, stash, oacc, dqacc, top, delta, dkv_ref, limit, sum_sem = refs
     t = pl.program_id(0)
     seq = seq_ref[t]
     row0 = row_ref[t]
@@ -75,59 +77,74 @@
     f32, bf16 = jnp.float32, jnp.bfloat16
     parts_, count, block, _ = kv_ref.shape
 
+    row_head = lax.broadcasted_iota(jnp.int32, (128, 128), 0) // HD
+    spread = (row_head == lax.broadcasted_iota(jnp.int32, (128, 128), 1) // HD).astype(bf16)
+    only_keys = (row_head == 0).astype(bf16)
+
     @pl.when(t == 0)
     def _():
         if first_call:
             dkv_ref[...] = jnp.zeros_like(dkv_ref)
         else:
-            dkv_ref[...] = before_ref[...]
-        lane = lax.broadcasted_iota(jnp.int32, (block, HD), 1)
-        ones = jnp.where(lane < 3, 1.0, 0.0).astype(bf16)
+            pltpu.make_async_copy(before_ref, dkv_ref, sum_sem).start()
+        lower = lax.broadcasted_iota(jnp.int32, (block, 128), 1) < HD
+        one = jnp.ones((block, 128), bf16)
 
         def arrange(i, most):
             for s in range(count):
                 kv = kv_ref[i, s]
                 rows = pl.ds(pl.multiple_of(i * block, block), block)
-                ka[s, rows, :] = jnp.concatenate([kv[:, :HD], ones], axis=1)
-                va[s, rows, :] = jnp.concatenate([kv[:, HD:], ones], axis=1)
-                k = kv[:, :HD].astype(f32)
-                most = jnp.maximum(most, jnp.max(jnp.sum(k * k, axis=1, keepdims=True)))
+                ka[s, rows, :] = jnp.where(lower, kv, one)
+                va[s, rows, :] = jnp.where(lower, one, kv)
+                most = jnp.maximum(most, dot(kv * kv, only_keys, 1, 0))
             return most
 
-        limit[0] = lax.fori_loop(0, parts_, arrange, jnp.float32(0.0))
+        limit[0] = jnp.max(lax.fori_loop(0, parts_, arrange, jnp.zeros((block, 128), f32)))
 
     @pl.when(on_ref[t] != 0)
     def _():
         taken = slot_ref[t] >= own
         q_in = q_ref[...] if other_ref is None else jnp.where(taken, other_ref[0, 0], q_ref[...])
         g_in = g_ref[...] if other_ref is None else jnp.where(taken, other_ref[0, 1], g_ref[...])
-        for h in range(H):
-            qs[heads[h], :HD] = q_in[:, h * HD:(h + 1) * HD]
-            qs[heads[h], HD:] = jnp.zeros((M, 128 - HD), bf16)
+        lane = lax.broadcasted_iota(jnp.int32, (M, 128), 1)
+        low_half = lane < HD
+        most = jnp.zeros((M, 128), f32)
+        for p in range(H // 2):
+            pair = q_in[:, p * 128:(p + 1) * 128]
+            most = jnp.maximum(most, dot(pair * pair, spread, 1, 0))
+            pair = pair.astype(f32)
+            qs[heads[2 * p], :] = jnp.where(low_half, pair, 0.0).astype(bf16)
+            qs[heads[2 * p + 1], :] = jnp.where(low_half, pltpu.roll(pair, HD, 1), 0.0).astype(bf16)
         oacc[...] = jnp.zeros_like(oacc)
         dqacc[...] = jnp.zeros_like(dqacc)
         n_full = row0 // tk
 
-        def keys(ref, kt):
-            return ref[seq, pl.ds(pl.multiple_of(kt * tk, tk), tk), :]
-
-        def allowed(kt):
-            row = row0 + (lax.broadcasted_iota(jnp.int32, (G, tk), 0) & (M - 1))
-            col = kt * tk + lax.broadcasted_iota(jnp.int32, (G, tk), 1)
+        def keys(ref, kt, size=tk):
+            return ref[seq, pl.ds(pl.multiple_of(kt * tk, tk), size), :]
+
+        def allowed(kt, size):
+            row = row0 + (lax.broadcasted_iota(jnp.int32, (G, size), 0) & (M - 1))
+            col = kt * tk + lax.broadcasted_iota(jnp.int32, (G, size), 1)
             return col <= row
 
-        def scores(kt, r, masked):
-            s = dot(qs[r, :], keys(ka, kt), 1, 1)
+        def scores(kt, r, masked, size=tk):
+            s = dot(qs[r, :], keys(ka, kt, size), 1, 1)
             if masked:
-                s = jnp.where(allowed(kt), s, -1e30)
+                s = jnp.where(allowed(kt, size), s, -1e30)
             return s
 
-        most = jnp.float32(0.0)
-        for r in groups:
-            q = qs[r, :].astype(f32)
-            most = jnp.maximum(most, jnp.max(jnp.sum(q * q, axis=1, keepdims=True)))
-
-        @pl.when(most * limit[0] > 3600.0)
+        short = row0 + M - n_full * tk <= tk // 2
+
+        def last(step):
+            @pl.when(short)
+            def _():
+                step(tk // 2)
+
+            @pl.when(jnp.logical_not(short))
+            def _():
+                step(tk)
+
+        @pl.when(jnp.max(most) * limit[0] > 3600.0)
         def _():
             top[...] = jnp.full_like(top, -1e30)
 
@@ -146,55 +163,80 @@
                 for j, part in enumerate(three_parts(best)):
                     qs[r, HD + j:HD + j + 1] = part
 
-        def first(kt, masked):
-            v = keys(va, kt)
+        def first(kt, masked, size=tk):
+            v = keys(va, kt, size)
             for r in groups:
-                e = jnp.exp2(scores(kt, r, masked)).astype(bf16)
-                stash[kt, r, :] = e
+                e = jnp.exp2(scores(kt, r, masked, size)).astype(bf16)
+                stash[kt, r, :size] = e
                 oacc[r, :] += dot(e, v, 1, 0)
 
         lax.fori_loop(0, n_full, lambda kt, _: (first(kt, False), 0)[1], 0)
-        first(n_full, True)
-
+        last(lambda size: first(n_full, True, size))
+
+        ones = jnp.ones((3 * 128, 128), bf16)
         for p in range(H // 2):
+            grads = g_in[:, p * 128:(p + 1) * 128].astype(f32)
             outs = []
             for h in (2 * p, 2 * p + 1):
                 r = heads[h]
                 acc = oacc[r, :]
-                inverse = 1.0 / acc[:, HD:HD + 1]
-                out = acc[:, :HD] * inverse
+                inverse = pltpu.roll(1.0 / acc, HD, 1)
+                out = acc * inverse
                 outs.append(out)
-                low = (g_in[:, h * HD:(h + 1) * HD].astype(f32) * inverse).astype(bf16)
-                delta = -jnp.sum(low.astype(f32) * out, axis=1, keepdims=True)
-                gs[r, :] = jnp.concatenate(
-                    [low, *three_parts(delta), jnp.zeros((M, 128 - HD - 3), bf16)], axis=1)
-            o_ref[:, p * 128:(p + 1) * 128] = jnp.concatenate(outs, axis=1).astype(bf16)
+                grad = grads if h % 2 == 1 else pltpu.roll(grads, HD, 1)
+                low = jnp.where(low_half, 0.0, grad * inverse).astype(bf16).astype(f32)
+                delta[r, :] = dot(jnp.concatenate(three_parts(low * out), axis=1), ones, 1, 0)
+                gs[r, :] = low.astype(bf16)
+            out = jnp.where(low_half, pltpu.roll(outs[0], HD, 1), outs[1]).astype(bf16)
+            o_ref[:, p * 128:(p + 1) * 128] = out
+            if given_ref is not None:
+                @pl.when(taken)
+                def _(p=p, out=out):
+                    given_ref[0, 0, :, p * 128:(p + 1) * 128] = out
         qt[...] = qs[...].T
         gt[...] = gs[...].T
 
-        def second(kt):
-            k = keys(ka, kt)
-            v = keys(va, kt)
-            dk = jnp.zeros((HD, tk), f32)
-            dv = jnp.zeros((HD, tk), f32)
+        if not first_call:
+            @pl.when(t == 0)
+            def _():
+                pltpu.make_async_copy(before_ref, dkv_ref, sum_sem).wait()
+
+        def second(kt, size=tk):
+            k = keys(ka, kt, size)
+            v = keys(va, kt, size)
+            dk = jnp.zeros((HD, size), f32)
+            dv = jnp.zeros((HD, size), f32)
             for r in groups:
-                e = stash[kt, r, :]
-                slope = (e.astype(f32) * dot(gs[r, :], v, 1, 1)).astype(bf16)
+                e = stash[kt, r, :size]
+                slope = e.astype(f32) * (dot(gs[r, :], v, 1, 1) - jnp.tile(delta[r, :], (1, size // 128)))
+                slope = slope.astype(bf16)
                 dqacc[r, :] += dot(slope, k, 1, 0)
                 dk = dk + dot(qt[:HD, r], slope, 1, 0)
-                dv = dv + dot(gt[:HD, r], e, 1, 0)
-            c = pl.ds(pl.multiple_of(kt * tk, tk), tk)
+                dv = dv + dot(gt[HD:, r], e, 1, 0)
+            c = pl.ds(pl.multiple_of(kt * tk, tk), size)
             dkv_ref[seq, :HD, c] += dk
             dkv_ref[seq, HD:, c] += dv
 
-        lax.fori_loop(0, n_full + 1, lambda kt, _: (second(kt), 0)[1], 0)
+        lax.fori_loop(0, n_full, lambda kt, _: (second(kt), 0)[1], 0)
+        last(lambda size: second(n_full, size))
         factors = turn_factors(near_ref[...], far_ref[pl.ds(row0 // M, 1), :])
         for p in range(H // 2):
-            z = jnp.concatenate([dqacc[heads[h], :HD] for h in (2 * p, 2 * p + 1)], axis=1)
-            dq_ref[:, p * 128:(p + 1) * 128] = (turn_back(z, *factors) * HD ** -0.5).astype(bf16)
-
-
-def attention(tables, q, g, others, skip, kv, M, tk, most, before=None):
+            z = jnp.where(low_half, dqacc[heads[2 * p], :], pltpu.roll(dqacc[heads[2 * p + 1], :], HD, 1))
+            z = (turn_back(z, *factors) * HD ** -0.5).astype(bf16)
+            dq_ref[:, p * 128:(p + 1) * 128] = z
+            if given_ref is not None:
+                @pl.when(taken)
+                def _(p=p, z=z):
+                    given_ref[0, 1, :, p * 128:(p + 1) * 128] = z
+
+    @pl.when(t == pl.num_programs(0) - 1)
+    def _():
+        copy = pltpu.make_async_copy(dkv_ref, sums_ref, sum_sem)
+        copy.start()
+        copy.wait()
+
+
+def attention(tables, q, g, others, skip, kv, M, tk, before=None):
     width = H * HD
     steps = tables[0].shape[0]
     own = q.shape[0] // M
@@ -202,12 +244,11 @@
     L = parts * block
     near, far = turn_tables(L, M)
     whole = pl.Buffered(1)
-    tile = pl.BlockSpec((M, width), lambda t, slot, *_: (slot[t], 0))
+    tile = pl.BlockSpec((M, width), lambda t, slot, *_: (jnp.minimum(slot[t], own), 0))
     near_spec = pl.BlockSpec(near.shape, lambda t, *_: (0, 0), pipeline_mode=whole)
     far_spec = pl.BlockSpec(far.shape, lambda t, *_: (0, 0), pipeline_mode=whole)
     mine = pl.BlockSpec((M, width), lambda t, slot, *_: (jnp.minimum(slot[t], own - 1), 0))
     taken = pl.BlockSpec((1, 2, M, width), lambda t, slot, *_: (jnp.maximum(slot[t] - own - skip, 0), 0, 0, 0))
-    sums = pl.BlockSpec((S, 128, L), lambda t, *_: (0, 0, 0), pipeline_mode=whole)
     anywhere = pl.BlockSpec(memory_space=pl.ANY)
     bf16, f32 = jnp.bfloat16, jnp.float32
     pairs = steps * M * H * L // 3
@@ -223,15 +264,22 @@
     aliases = {}
     if before is not None:
         aliases = {4 + len(operands) + i: i for i in range(3)}
-        operands, specs = operands + list(before), specs + [anywhere, anywhere, sums]
-    slots = jax.ShapeDtypeStruct(((own + most) * M, width), bf16)
+        operands, specs = operands + list(before), specs + [anywhere] * 3
+    slots = jax.ShapeDtypeStruct(((own + 1) * M, width), bf16)
+    out_shape, out_specs = [slots, slots, jax.ShapeDtypeStruct((S, 128, L), f32)], [tile, tile, anywhere]
+    if others is not None:
+        count = others.shape[0]
+        out_shape.append(jax.ShapeDtypeStruct(others.shape, bf16))
+        out_specs.append(pl.BlockSpec(
+            (1, 2, M, width),
+            lambda t, slot, *_: (jnp.where(slot[t] < own, count - 1, jnp.minimum(slot[t] - own - skip, count - 1)), 0, 0, 0)))
     return pl.pallas_call(
         kernel,
         grid_spec=pltpu.PrefetchScalarGridSpec(
             num_scalar_prefetch=4,
             grid=(steps,),
             in_specs=specs,
-            out_specs=[tile, tile, sums],
+            out_specs=out_specs,
             scratch_shapes=[
                 pltpu.VMEM((S, L, 128), bf16),
                 pltpu.VMEM((S, L, 128), bf16),
@@ -243,10 +291,13 @@
                 pltpu.VMEM((H * M, 128), f32),
                 pltpu.VMEM((H * M, 128), f32),
                 pltpu.VMEM((H * M, 128), f32),
+                pltpu.VMEM((H * M, 128), f32),
+                pltpu.VMEM((S, 128, L), f32),
                 pltpu.SMEM((1,), f32),
+                pltpu.SemaphoreType.DMA,
             ],
         ),
-        out_shape=[slots, slots, jax.ShapeDtypeStruct((S, 128, L), f32)],
+        out_shape=out_shape,
         input_output_aliases=aliases,
         compiler_params=pltpu.CompilerParams(vmem_limit_bytes=58 << 20),
         cost_estimate=pl.CostEstimate(flops=1 << 20, bytes_accessed=1 << 16, transcendentals=0),
@@ -400,31 +451,41 @@
 
     @pl.when(f == 0)
     def _():
-        own = pltpu.make_async_copy(kv_ref, all_kv.at[tuple(me)], own_sem)
-        own.start()
+        pltpu.make_async_copy(kv_ref, all_kv.at[tuple(me)], own_sem).start()
         barrier = pltpu.get_barrier_semaphore()
         for bit in bits:
             pl.semaphore_signal(barrier, inc=1, device_id=partner(bit), device_id_type=MESH)
         pl.semaphore_signal(barrier, inc=1, device_id={"seq": n_seq - 1 - block}, device_id_type=MESH)
-        pl.semaphore_wait(barrier, stages + 1)
-        own.wait()
-
-    for stage in range(stages):
-        @pl.when(f == min(stage, tiles - 1))
-        def _(stage=stage):
-            if stage > 0:
-                for copy in kv_copies(stage - 1):
+
+    end = 2 * tiles - 1
+    when = [min(max(2, 2 * k + 1), end) for k in range(stages)]
+    after = when[-1]
+
+    def progress(point):
+        if point == when[0]:
+            pl.semaphore_wait(pltpu.get_barrier_semaphore(), stages + 1)
+            pltpu.make_async_copy(kv_ref, all_kv.at[tuple(me)], own_sem).wait()
+        for stage in range(stages):
+            if when[stage] == point:
+                for copy in kv_copies(stage - 1) if stage else []:
                     copy.wait()
-            for copy in kv_copies(stage):
-                copy.start()
-
-    @pl.when(f == 1)
-    def _():
-        for k in range(len(order)):
-            @pl.when(among([i for i in range(n_seq) if moved[i] > k]))
-            def _(k=k):
-                for copy in tile_copies(k):
+                for copy in kv_copies(stage):
                     copy.start()
+        if after == point:
+            for k in range(len(order)):
+                @pl.when(among([i for i in range(n_seq) if moved[i] > k]))
+                def _(k=k):
+                    for copy in tile_copies(k):
+                        copy.start()
+
+    def progress_at(parity):
+        for point in sorted(set(when + [after])):
+            if point % 2 == parity:
+                @pl.when(f == point // 2)
+                def _(point=point):
+                    progress(point)
+
+    progress_at(0)
 
     @pl.when(f == 0)
     def _():
@@ -445,6 +506,8 @@
     up = ups[f]
     down = down_ref[...].reshape(D, D)
     for c in range(T // C):
+        if c == T // C // 2:
+            progress_at(1)
         r = slice(c * C, (c + 1) * C)
         u = dot(x_ref[r, :], up, 1, 0)
         a = dot(b_ref[r, :], down, 1, 1)
@@ -557,7 +620,7 @@
 
 def front_kernel(
     bits, here, M, chunk, streams,
-    x_ref, c_ref, scale_ref, norm_ref, near_ref, far_ref, query_ref, pair_ref, output_ref, up_ref, down_ref,
+    x_ref, c_ref, weight_ref, subset_ref, ga_ref, sa_ref, gf_ref, sf_ref, near_ref, far_ref, query_ref, pair_ref, output_ref, up_ref, down_ref,
     q_ref, g_ref, kv_ref, xa_ref, xf_ref, b_ref, wide_ref, wp, hidden_ref,
     pr_all, sq_all, hidden_own, stage_q, stage_o, stage_p,
     own_sem, send_sem, recv_sem,
@@ -581,15 +644,17 @@
     greet(bits)
     own.wait()
 
+    gains = [ref[...].reshape(1, D) for ref in (ga_ref, sa_ref, gf_ref, sf_ref)]
+
     def normalize(i):
         r = slice(i * chunk, (i + 1) * chunk)
         x = x_ref[r, :].astype(f32)
         x = x - jnp.mean(x, axis=1, keepdims=True)
         unit = x * lax.rsqrt(jnp.mean(x * x, axis=1, keepdims=True) + 1e-05)
-        xa_ref[r, :] = (unit * norm_ref[0:1, :] + norm_ref[1:2, :]).astype(bf16)
-        xf_ref[r, :] = (unit * norm_ref[2:3, :] + norm_ref[3:4, :]).astype(bf16)
+        xa_ref[r, :] = (unit * gains[0] + gains[1]).astype(bf16)
+        xf_ref[r, :] = (unit * gains[2] + gains[3]).astype(bf16)
         part = i * chunk // (T // here)
-        b_ref[r, :] = (c_ref[r, :].astype(f32) * scale_ref[part:part + 1, :]).astype(bf16)
+        b_ref[r, :] = (c_ref[r, :].astype(f32) * weight_ref[subset_ref[part]]).astype(bf16)
 
     def unpack():
         for d in range(1 << n):
@@ -660,7 +725,7 @@
             copy.wait()
 
 
-def front(x, c, scale, norms, query, pair, output, up, down, here, length, M, n_seq, n_rows, collective_id, chunk=256):
+def front(x, c, weights, subsets, norms, query, pair, output, up, down, here, length, M, n_seq, n_rows, collective_id, chunk=256):
     bits = bits_of(n_seq, n_rows)
     n = len(bits)
     T, D = x.shape
@@ -668,6 +733,7 @@
     f32, bf16 = jnp.float32, jnp.bfloat16
     near, far = turn_tables(length, M)
     vmem = pl.BlockSpec(memory_space=pltpu.VMEM)
+    smem = pl.BlockSpec(memory_space=pltpu.SMEM)
     token = jax.ShapeDtypeStruct((T, D), bf16)
     streams = streams_of(bits, 2 * owned, hidden)
     q, g, kv, xa, xf, b, wide, wp, packed = pl.pallas_call(
@@ -675,7 +741,7 @@
         out_shape=[token, token, jax.ShapeDtypeStruct((T, 128), bf16), token, token, token,
                    jax.ShapeDtypeStruct((2, D, D), bf16), jax.ShapeDtypeStruct((D, 128), bf16),
                    jax.ShapeDtypeStruct((2,) * n + (hidden, D), bf16)],
-        in_specs=[vmem] * 11,
+        in_specs=[vmem] * 2 + [smem] * 2 + [vmem] * 11,
         out_specs=[vmem] * 8 + [pl.BlockSpec(memory_space=pl.ANY)],
         scratch_shapes=[
             pltpu.VMEM((2,) * n + (32, 128), bf16),
@@ -691,7 +757,7 @@
         compiler_params=pltpu.CompilerParams(
             collective_id=collective_id, has_side_effects=True, vmem_limit_bytes=56 << 20),
         name="front",
-    )(x, c, scale, norms, near, far, query, pair, output, up, down)
+    )(x, c, weights, subsets, *norms, near, far, query, pair, output, up, down)
     return q, g, kv, xa, xf, b, wide, wp, packed.reshape(1 << n, hidden, D)
 
 
@@ -748,10 +814,11 @@
         pltpu.SemaphoreType.DMA((stages,)), pltpu.SemaphoreType.DMA((stages,))]
 
 
-def post_kernel(bits, here, M, order, moved, chunk, *refs):
+def post_kernel(bits, here, M, order, moved, counts, chunk, *refs):
     (sums_ref, o_hbm, dq_hbm, *refs) = refs
-    backs, refs = refs[:len(order)], refs[len(order):]
-    (xa_ref, b_ref, x_hbm, c_hbm, out_hbm, dx_hbm, wide_ref, wp_ref, norm_ref, scale_ref, near_ref, far_ref,
+    backs, refs = refs[:len(counts)], refs[len(counts):]
+    backs = [ref.at[k] for ref, count in zip(backs, counts) for k in range(count)]
+    (xa_ref, b_ref, x_hbm, c_hbm, out_hbm, dx_hbm, wide_ref, wp_ref, ga_ref, gf_ref, weight_ref, subset_ref, near_ref, far_ref,
      layer_ref, states_ref, square_ref, small_ref, *refs) = refs
     f32, bf16 = jnp.float32, jnp.bfloat16
     T, D = xa_ref.shape
@@ -759,7 +826,7 @@
     seq_bits = [i for i in range(n) if bits[i][0] == "seq"]
     n_s = len(seq_bits)
     me = place(bits)
-    o_ref, dq_ref, x_ref, c_ref, out_ref, dx_ref, ai_ref, gq, go, gs, load_sem, *refs = refs
+    o_ref, dq_ref, x_ref, c_ref, out_ref, dx_ref, ai_ref, gq, go, gs, inv_ref, load_sem, *refs = refs
 
     def take(stages):
         nonlocal refs
@@ -815,41 +882,57 @@
     squares[0].start(0)
     go[...] = dot(o_ref[...], b_ref[...], 0, 0)
     squares[1].start(0)
-    for h in kv:
-        h.finish(0)
-        h.start(1)
-    loads[2].wait()
-    loads[3].wait()
     chunks = T // chunk
+
+    def backward(i):
+        r = slice(i * chunk, (i + 1) * chunk)
+        ai_ref[r, :] = dot(dq_ref[r, :], wide_ref[0], 1, 1)
 
     def forward(i):
         r = slice(i * chunk, (i + 1) * chunk)
         total = x_ref[r, :].astype(f32) + (dot(o_ref[r, :], wide_ref[1], 1, 0) + out_ref[r, :])
         layer_ref[r, :] = total.astype(bf16)
 
-    def backward(i):
+    totals = [jnp.zeros((1, D), f32) for _ in range(4)]
+
+    def hidden(i):
         r = slice(i * chunk, (i + 1) * chunk)
-        ai_ref[r, :] = dot(dq_ref[r, :], wide_ref[0], 1, 1)
-
-    jobs = [functools.partial(f, i) for f in (forward, backward) for i in range(chunks)]
-    gaps = n - 1
-    for stage in range(n):
+        x = x_ref[r, :].astype(f32)
+        x = x - jnp.mean(x, axis=1, keepdims=True)
+        inverse = lax.rsqrt(jnp.mean(x * x, axis=1, keepdims=True) + 1e-05)
+        unit = x * inverse
+        fi = dx_ref[r, :]
+        totals[2] = totals[2] + jnp.sum(fi * unit, axis=0, keepdims=True)
+        totals[3] = totals[3] + jnp.sum(fi, axis=0, keepdims=True)
+        dx_ref[r, :] = fi * gf_ref[...].reshape(1, D)
+        out_ref[r, :] = unit
+        inv_ref[r, :] = inverse
+
+    moved_on = [0]
+
+    def advance():
+        stage = moved_on[0]
+        moved_on[0] += 1
         for h in squares:
             h.finish(stage)
             if stage + 1 < n:
                 h.start(stage + 1)
-        for i, job in enumerate(jobs):
-            if i * gaps // len(jobs) == stage:
-                job()
-        if 0 < stage < n_s:
-            for h in kv:
-                h.finish(stage)
-                if stage + 1 < n_s:
-                    h.start(stage + 1)
-    for i, h in enumerate(squares):
-        total = h.acc[n - 1][0]
-        square_ref[i, :, :D // 2] = total[:owned]
-        square_ref[i, :, D // 2:] = total[owned:]
+
+    for i in range(chunks):
+        backward(i)
+    advance()
+    for load in loads[2:5]:
+        load.wait()
+    for i in range(chunks):
+        forward(i)
+        hidden(i)
+    for stage in range(n_s):
+        for h in kv:
+            h.finish(stage)
+            if stage + 1 < n_s:
+                h.start(stage + 1)
+        if moved_on[0] < n - 1:
+            advance()
 
     first = lax.broadcasted_iota(jnp.int32, (M, 128), 1) < HD
     grads = []
@@ -862,36 +945,37 @@
             grads.append(jnp.where(first, turned, part).astype(bf16))
     pairs = jnp.concatenate(grads, axis=0)
     gs[:, :128] = dot(xa_ref[...], pairs, 0, 0)
-    loads[4].wait()
     loads[5].wait()
-    totals = [jnp.zeros((1, D), f32) for _ in range(4)]
     for i in range(chunks):
         r = slice(i * chunk, (i + 1) * chunk)
-        x = x_ref[r, :].astype(f32)
-        x = x - jnp.mean(x, axis=1, keepdims=True)
-        inverse = lax.rsqrt(jnp.mean(x * x, axis=1, keepdims=True) + 1e-05)
-        unit = x * inverse
+        unit = out_ref[r, :]
         ai = ai_ref[r, :] + dot(pairs[r], wp_ref[...], 1, 1)
-        fi = dx_ref[r, :]
-        for k, part in enumerate((ai * unit, ai, fi * unit, fi)):
-            totals[k] = totals[k] + jnp.sum(part, axis=0, keepdims=True)
-        both = ai * norm_ref[0:1, :] + fi * norm_ref[2:3, :]
+        totals[0] = totals[0] + jnp.sum(ai * unit, axis=0, keepdims=True)
+        totals[1] = totals[1] + jnp.sum(ai, axis=0, keepdims=True)
+        both = ai * ga_ref[...].reshape(1, D) + dx_ref[r, :]
         middle = jnp.mean(both, axis=1, keepdims=True)
         slope = jnp.mean(both * unit, axis=1, keepdims=True)
-        part = i * chunk // local
-        up = c_ref[r, :].astype(f32) * scale_ref[part:part + 1, :]
-        states_ref[r, :] = (up + inverse * (both - middle - unit * slope)).astype(bf16)
+        up = c_ref[r, :].astype(f32) * weight_ref[subset_ref[i * chunk // local]]
+        states_ref[r, :] = (up + inv_ref[r, :] * (both - middle - unit * slope)).astype(bf16)
     rows = jnp.concatenate(totals + [jnp.zeros((124, D), f32)], axis=0)
     gs[:, 128:] = rows.T
+    small.start(0)
+    while moved_on[0] < n:
+        advance()
+    for i, h in enumerate(squares):
+        total = h.acc[n - 1][0]
+        square_ref[i, :, :D // 2] = total[:owned]
+        square_ref[i, :, D // 2:] = total[owned:]
     for stage in range(n):
-        small.start(stage)
         small.finish(stage)
+        if stage + 1 < n:
+            small.start(stage + 1)
     total = small.acc[n - 1][0]
     small_ref[:, :128] = total[:owned]
     small_ref[:, 128:] = total[owned:]
 
 
-def post(sums, o, dq, backs, order, moved, xa, b, x, c, out, dx, wide, wp, norms, scales,
+def post(sums, o, dq, backs, order, moved, xa, b, x, c, out, dx, wide, wp, norms, weights, subsets,
          here, length, M, n_seq, n_rows, collective_id, chunk=256):
     bits = bits_of(n_seq, n_rows)
     n, n_s = len(bits), n_seq.bit_length() - 1
@@ -900,11 +984,12 @@
     f32, bf16 = jnp.float32, jnp.bfloat16
     near, far = turn_tables(length, M)
     vmem, anywhere = pl.BlockSpec(memory_space=pltpu.VMEM), pl.BlockSpec(memory_space=pl.ANY)
+    smem = pl.BlockSpec(memory_space=pltpu.SMEM)
     token = jax.ShapeDtypeStruct((T, D), bf16)
     scratch = [
         *[pltpu.VMEM((T, D), bf16)] * 4, *[pltpu.VMEM((T, D), f32)] * 3,
         pltpu.VMEM((D, D), f32), pltpu.VMEM((D, D), f32), pltpu.VMEM((D, 256), f32),
-        pltpu.SemaphoreType.DMA((6,)),
+        pltpu.VMEM((T, 1), f32), pltpu.SemaphoreType.DMA((6,)),
     ]
     for _ in range(here):
         scratch += halving_shapes(n_s, 128, length // n_seq)
@@ -912,15 +997,15 @@
         scratch += halving_shapes(n, 2 * owned, D // 2)
     scratch += halving_shapes(n, 2 * owned, 128)
     return pl.pallas_call(
-        functools.partial(post_kernel, bits, here, M, tuple(order), tuple(moved), chunk),
+        functools.partial(post_kernel, bits, here, M, tuple(order), tuple(moved), tuple(b.shape[0] for b in backs), chunk),
         out_shape=[token, token, jax.ShapeDtypeStruct((2, owned, D), f32), jax.ShapeDtypeStruct((owned, 256), f32)],
-        in_specs=[vmem, anywhere, anywhere] + [vmem] * len(backs) + [vmem] * 2 + [anywhere] * 4 + [vmem] * 6,
+        in_specs=[vmem, anywhere, anywhere] + [vmem] * len(backs) + [vmem] * 2 + [anywhere] * 4 + [vmem] * 4 + [smem] * 2 + [vmem] * 2,
         out_specs=[vmem] * 4,
         scratch_shapes=scratch,
         compiler_params=pltpu.CompilerParams(
             collective_id=collective_id, has_side_effects=True, vmem_limit_bytes=60 << 20),
         name="post",
-    )(sums, o, dq, *backs, xa, b, x, c, out, dx, wide, wp, norms, scales, near, far)
+    )(sums, o, dq, *backs, xa, b, x, c, out, dx, wide, wp, norms[0], norms[2], weights, subsets, near, far)
 
 
 def layer_norm(values):
@@ -957,7 +1042,7 @@
 def plan(n, here, per, M, tk):
     order = [(s, j) for j in reversed(range(per)) for s in range(here)]
     row = lambda i, j: (i * per + j) * M
-    price = lambda first: first // tk + 1.4
+    price = lambda first: first // tk + (0.5 if first % tk + M <= tk // 2 else 1.0) + 1.1
     moved = [0] * n
     for i in range(n // 2, n):
         load = lambda k: max(
@@ -972,10 +1057,11 @@
     mean = sum(cost(t) + cost(k) for t, k in zip(takes, keeps)) / n
     lists = ([], [], [])
     for take, keep in zip(takes, keeps):
+        ahead, between = (0.32, 0.42) if take else (0.24, 0.40)
         keep, head, middle = list(keep), list(take[:1]), list(take[1:])
-        while len(keep) > 1 and cost(head) + price(keep[0][2]) / 2 < 0.32 * mean:
+        while len(keep) > 1 and cost(head) + price(keep[0][2]) / 2 < ahead * mean:
             head.append(keep.pop(0))
-        while len(keep) > 1 and cost(middle) + price(keep[0][2]) / 2 < 0.42 * mean and cost(keep) > 0.24 * mean:
+        while len(keep) > 1 and cost(middle) + price(keep[0][2]) / 2 < between * mean and cost(keep) > 0.24 * mean:
             middle.append(keep.pop(0))
         for part, steps in zip(lists, (head, middle, keep)):
             part.append(steps)
@@ -1011,17 +1097,16 @@
 
     rows_here = offset + jnp.arange(length_here, dtype=jnp.int32)
     cosine, sine_vals = rotary_tables(rows_here.astype(f32))
-    table_rows = jnp.arange(subset_weight.shape[0], dtype=jnp.int32)
-    row_scale = jnp.sum(
-        jnp.where(table_rows[None, :] == subsets[:, None], subset_weight[None, :], 0.0), axis=1
-    )
     if aligned:
-        norms = jnp.stack([gain_attn, shift_attn, gain_ffn, shift_ffn])
-        scales = jnp.broadcast_to(row_scale[:, None], (here, D))
+        norms = (gain_attn, shift_attn, gain_ffn, shift_ffn)
         queries, out_grad, own_kv, attention_input, feedforward_input, branch_grad, wide, full_pair, packed = front(
-            states.reshape(T, D), cotangent.reshape(T, D), scales, norms, query_projection, pair_projection,
+            states.reshape(T, D), cotangent.reshape(T, D), subset_weight, subsets, norms, query_projection, pair_projection,
             output_projection, up_projection, down_projection, here, length, M, n_seq, n_rows, 1)
     else:
+        table_rows = jnp.arange(subset_weight.shape[0], dtype=jnp.int32)
+        row_scale = jnp.sum(
+            jnp.where(table_rows[None, :] == subsets[:, None], subset_weight[None, :], 0.0), axis=1
+        )
         source = states.astype(f32).reshape(T, D)
         unit, inverse = layer_norm(source)
         upstream = (cotangent.astype(f32) * row_scale[:, None, None]).reshape(T, D)
@@ -1058,43 +1143,42 @@
         steps.append(tuple(mine[:, c] for c in range(4)))
     q_tiles, g_tiles = queries.reshape(own, M, D), out_grad.reshape(own, M, D)
 
-    def send(k):
-        pairs_of = [(i, n_seq - 1 - i) for i in range(n_seq) if moved[i] > k]
-        return lax.ppermute(jnp.stack([q_tiles[at_slots[k]], g_tiles[at_slots[k]]]), "seq", pairs_of)
-
-    def send_back(done, k):
-        pairs_of = [(n_seq - 1 - i, i) for i in range(n_seq) if moved[i] > k]
-        tile = slice((own + k) * M, (own + k + 1) * M)
-        return lax.ppermute(jnp.stack([done[0][tile], done[1][tile]]), "seq", pairs_of)
+    def send(tiles):
+        pairs_of = [(i, n_seq - 1 - i) for i in range(n_seq) if moved[i] > tiles[0]]
+        return lax.ppermute(
+            jnp.stack([jnp.stack([q_tiles[at_slots[k]], g_tiles[at_slots[k]]]) for k in tiles]), "seq", pairs_of)
+
+    def send_back(given, first):
+        return lax.ppermute(given, "seq", [(n_seq - 1 - i, i) for i in range(n_seq) if moved[i] > first])
 
     if aligned:
         ffn_out, ffn_input_grad, ffn_grads, all_kv, first_taken = ffn_packed(
             feedforward_input, branch_grad, packed, own_kv.reshape(here, length_here, P), queries, out_grad,
             at_slots[:1], moved, M, n_seq, 3)
     else:
-        first_taken = send(0)[None]
+        first_taken = send([0])
         ffn_out, ffn_input_grad, grad_up, grad_down = ffn(feedforward_input, branch_grad, full_up, full_down)
         ffn_grads = jnp.concatenate([grad_up.reshape(n, -1, D), grad_down.reshape(n, -1, D)], axis=1)
     ffn_grads = lax.psum_scatter(ffn_grads, both, scatter_dimension=0, tiled=True)[0]
-    done = attention(steps[0], queries, out_grad, first_taken, 0, all_kv, M, tk, most)
-    backs = [send_back(done, 0)]
+    *done, given = attention(steps[0], queries, out_grad, first_taken, 0, all_kv, M, tk)
+    backs = [send_back(given, 0)]
     if most > 1:
-        taken = jnp.stack([send(k) for k in range(1, most)])
-        done = attention(steps[1], queries, out_grad, taken, 1, all_kv, M, tk, most, done)
+        *done, given = attention(
+            steps[1], queries, out_grad, send(list(range(1, most))), 1, all_kv, M, tk, done)
+        backs.append(send_back(given, 1))
     else:
-        done = attention(steps[1], queries, out_grad, None, 0, all_kv, M, tk, most, done)
-    backs += [send_back(done, k) for k in range(1, most)]
+        done = attention(steps[1], queries, out_grad, None, 0, all_kv, M, tk, done)
     half = ffn_grads.shape[0] // 2
     final_up = ffn_grads[:half]
     if aligned:
         final_up = jnp.swapaxes(final_up.reshape(FF // D, own_rows, D), 0, 1)
     final_up = final_up.reshape(-1, FF).astype(f32)
     final_down = ffn_grads[half:].astype(f32)
-    attended, query_pre_grad, pair_terms = attention(steps[2], queries, out_grad, None, 0, all_kv, M, tk, most, done)
+    attended, query_pre_grad, pair_terms = attention(steps[2], queries, out_grad, None, 0, all_kv, M, tk, done)
     if aligned:
         layer_out, grad_states, squares, small = post(
             pair_terms, attended, query_pre_grad, backs, at_slots, moved, attention_input, branch_grad,
-            states.reshape(T, D), cotangent.reshape(T, D), ffn_out, ffn_input_grad, wide, full_pair, norms, scales,
+            states.reshape(T, D), cotangent.reshape(T, D), ffn_out, ffn_input_grad, wide, full_pair, norms, subset_weight, subsets,
             here, length, M, n_seq, n_rows, 2)
         vectors = small[:, P:]
         return (
@@ -1105,11 +1189,9 @@
 
     a_own, d_own = list(attended.reshape(-1, M, D)[:own]), list(query_pre_grad.reshape(-1, M, D)[:own])
     count = jnp.asarray(np.array(moved, np.int32))[block]
-    for k in range(most):
-        s, j = order[k]
-        at = s * per + j
-        a_own[at] = jnp.where(count > k, backs[k][0], a_own[at])
-        d_own[at] = jnp.where(count > k, backs[k][1], d_own[at])
+    for k, back in enumerate(tile for part in backs for tile in part):
+        a_own[at_slots[k]] = jnp.where(count > k, back[0], a_own[at_slots[k]])
+        d_own[at_slots[k]] = jnp.where(count > k, back[1], d_own[at_slots[k]])
     attended, query_pre_grad = jnp.concatenate(a_own), jnp.concatenate(d_own)
 
     pair_terms = pair_terms.astype(bf16).reshape(here, P, n_seq, length_here)

time: 426 us -> 410 us (0.962)
  local copies, waits for them, and re-layouts: 20.7 us -> 14.9 us
  Pallas kernels: 375 us -> 370 us
    pallas_call x3, Pallas kernels: 138 us -> 131 us  [attention(): pl.pallas_call(kernel, grid_spec=pltpu.PrefetchScalarGridSpec(num_scalar_...]
    another operation x8 -> x0, local copies, waits for them, and re-layouts: 6.74 us -> none  [the longest x4 3.98 us: send_back(): jnp.stack([done[0][tile], done[1][tile]])]
  transfers between devices with their start and end apart: 6 -> 4, of which waited for: 0 -> 0; matrix products, arithmetic and copies ran while one was open for 3% -> 2% of each run, Pallas kernels for 53% -> 54%
where the time goes in v4:
time: 410 us; the launch traced here: 405 us
  Pallas kernels  370 us (90%)
  local copies, waits for them, and re-layouts  14.9 us (4%)
  between operations  14.5 us (4%)
    pallas_call x3, Pallas kernels, attention(): pl.pallas_call(kernel, grid_spec=pltpu.PrefetchScalarGridSpec(num_scalar_...  131 us
    pallas_call x1, Pallas kernels, post(): pl.pallas_call(functools.partial(post_kernel, bits, here, M, tuple(order)...  88.7 us
    pallas_call x1, Pallas kernels, front(): pl.pallas_call(functools.partial(front_kernel, bits, here, M, chunk, stre...  86.7 us
    pallas_call x1, Pallas kernels, ffn_packed(): pl.pallas_call(functools.partial(ffn_packed_kernel, C, bits, M, tuple(ord...  63.6 us
  transfers between devices with their start and end apart: 4, of which 0 were waited for; matrix products, arithmetic and copies ran while one was open for 2% of the time, Pallas kernels for 54%

profile of v4, /device:TPU:0, one launch (start us, length us, event | category | flops | bytes accessed | tf_op | source)
XLA Modules:
  0.0 405.0 jit_solution(5851670505091079876)
XLA Ops:
  7.2 86.7 %front.1 = (bf16[1024,768]{1,0:T(8,128)(2,1)}, bf16[1024,768]{1,0:T(8,128)(2,1)}, bf16[1024,128]{1,0:T(8,128)(2,1)}, bf16[1024,768]{1,0:T(8,128)(2,1)}, bf16[102...) custom-call(bf16[1024,768]{1,0:T(8,128)(2,1)} %bitcast.53, ...), custom_call_target="tpu_custom_call" | custom-call | tf_op jit(solution)/shard_map/front/pallas_call | solution.py:739
  93.9 63.6 %feedforward.1 = (f32[1024,768]{1,0:T(8,128)}, f32[1024,768]{1,0:T(8,128)}, bf16[32,192,768]{2,1,0:T(8,128)(2,1)}, bf16[2,2,2,2,512,128]{5,4,3,2,1,0:T(8,128)(2,1)}, bf16[1,2,128,768]{3,2,1,0:T(8,128)(2,1)}) custom-call(bf16[1024,768]{1,0:T(8,128)(2,1)} %get-tuple-element.42.x_ref, bf16[1024,768]{1,0:T(8,128)(2,1)} %get-tuple-element.43.b_ref.refs_6_, ...), custom_call_target="tpu_custom_call" | custom-call | flops 1048576 | bytes 65536 | tf_op jit(solution)/shard_map/feedforward/pallas_call | solution.py:562
  157.6 1.3 slice_bitcast_fusion.2
  159.0 1.3 collective-permute-start
  160.3 0.7 dynamic-slice_bitcast_fusion
  161.0 0.7 slice_reduce_fusion.4
  161.8 44.3 %attention.3 = (bf16[1152,768]{1,0:T(8,128)(2,1)}, bf16[1152,768]{1,0:T(8,128)(2,1)}, f32[2,128,4096]{2,1,0:T(8,128)}, bf16[1,2,128,768]{3,2,1,0:T(8,128)(2,1)}) custom-call(s32[3]{0:T(128)} %get-tuple-element.76.slot_ref, s32[3]{0:T(128)} %get-tuple-element.75.seq_ref, s32[3]{0:T(128)} %get-tuple-element.74.row_ref, s32[3]{0:T(128)} %get-tuple-element.73.on_ref, ...), custom_call_target="tpu_custom_call" | custom-call | flops 1048576 | bytes 65536 | tf_op jit(solution)/shard_map/attention/pallas_call | solution.py:276
  206.1 0.7 dynamic-slice_bitcast_fusion.1
  206.8 0.7 slice_reduce_fusion.8
  207.5 0.9 copy-done.3
  208.4 55.3 %attention.4 = (bf16[1152,768]{1,0:T(8,128)(2,1)}, bf16[1152,768]{1,0:T(8,128)(2,1)}, f32[2,128,4096]{2,1,0:T(8,128)}, bf16[2,2,128,768]{3,2,1,0:T(8,128)(2,1)}) custom-call(s32[4]{0:T(128)} %get-tuple-element.80.slot_ref, s32[4]{0:T(128)} %get-tuple-element.79.seq_ref, ...), custom_call_target="tpu_custom_call", output_to_operand_aliasing={{0}: (10, {}), {1}: (11, {}), {2}: (12, {})} | custom-call | flops 1048576 | bytes 65536 | tf_op jit(solution)/shard_map/attention/pallas_call | solution.py:276
  263.7 1.3 collective-permute-start.2
  265.1 1.3 collective-permute-start.1
  266.4 0.7 dynamic-slice_bitcast_fusion.2
  267.6 31.2 %attention.5 = (bf16[1152,768]{1,0:T(8,128)(2,1)}, bf16[1152,768]{1,0:T(8,128)(2,1)}, f32[2,128,4096]{2,1,0:T(8,128)}) custom-call(s32[6]{0:T(128)} %get-tuple-element.92.a, s32[6]{0:T(128)} %get-tuple-element.91.b, s32[6]{0:T(128)} %get-tuple-element.90.c, s32[6]{0:T(128)} %get-tuple-element.89.d, ...), custom_call_target="tpu_custom_call", output_to_operand_aliasing={{0}: (9, {}), {1}: (10, {}), {2}: (11, {})} | custom-call | flops 1048576 | bytes 65536 | tf_op jit(solution)/shard_map/attention/pallas_call | solution.py:276
  298.8 0.7 copy-done.4
  299.8 88.7 %post.1 = (bf16[1024,768]{1,0:T(8,128)(2,1)}, bf16[1024,768]{1,0:T(8,128)(2,1)}, f32[2,24,768]{2,1,0:T(8,128)}, f32[24,256]{1,0:T(8,128)}) custom-call(f32[2,128,4096]{2,1,0:T(8,128)} %get-tuple-element.54.refs_0_, bf16[1152,768]{1,0:T(8,128)(2,1)} %get-tuple-element.55.refs_1_, bf16[1152,768]{1,0:T(8,128)(2,1)} %get-tuple-element.56.refs_2_, ...), custom_call_target="tpu_custom_call" | custom-call | tf_op jit(solution)/shard_map/post/pallas_call | solution.py:999
  388.5 1.4 slice.119
  390.0 1.6 slice_reduce_fusion
  391.6 1.6 slice_bitcast_fusion.5
  393.1 1.7 fusion
  394.9 0.7 copy.45
  395.6 1.1 copy.54
  396.8 1.1 copy.55
  (21 shorter events, 1.0 us)
Async XLA Ops:
  7.2 386.0 %reduce-scatter.2.cloned.1.call-start = ((), (), s32[]{:S(2)}) async-start(), calls=%async_computation.1 | async-start | bytes 9732096 | tf_op jit(solution)/shard_map/reduce_scatter | solution.py:1162
  159.0 48.5 %collective-permute-start = (bf16[2,2,128,768]{3,2,1,0:T(8,128)(2,1)S(1)}, bf16[2,2,128,768]{3,2,1,0:T(8,128)(2,1)S(1)}, u32[]{:S(2)}, u32[]{:S(2)}) collective-permute-start(bf16[2,2,128,768]{3,2,1,0:T(8,128)(2,1)S(1)} %pad_maximum_fusion), channel_id=1, source_target_pairs={{20,8},{24,4},{28,0},{21,9},{25,5},{29,1},{22,10},{26,6},{30,2},{2... | collective-permute-start | bytes 2359304 | tf_op jit(solution)/shard_map/ppermute | solution.py:1148
  207.5 0.9 copy-start.3
  208.4 56.6 %copy-start.5 = (bf16[1,2,128,768]{3,2,1,0:T(8,128)(2,1)S(1)}, bf16[1,2,128,768]{3,2,1,0:T(8,128)(2,1)}, u32[]{:S(2)}) copy-start(bf16[1,2,128,768]{3,2,1,0:T(8,128)(2,1)} %get-tuple-element.57) | copy-start | bytes 1179652
  263.7 35.1 %collective-permute-start.2 = (bf16[2,2,128,768]{3,2,1,0:T(8,128)(2,1)}, bf16[2,2,128,768]{3,2,1,0:T(8,128)(2,1)S(1)}, u32[]{:S(2)}, u32[]{:S(2)}) collective-permute-start(bf16[2,2,128,768]{3,2,1,0:T(8,128)(2,1)} %get-tuple-element.58), channel_id=1, source_target_pairs={{8,20},{4,24},{0,28},{9,21},{5,25},{1,29},{10,22},{6,26},{2,30},{1... | collective-permute-start | bytes 2359304 | tf_op jit(solution)/shard_map/ppermute | solution.py:1152
  265.1 33.7 %collective-permute-start.1 = (bf16[1,2,128,768]{3,2,1,0:T(8,128)(2,1)S(1)}, bf16[1,2,128,768]{3,2,1,0:T(8,128)(2,1)S(1)}, u32[]{:S(2)}, u32[]{:S(2)}) collective-permute-start(bf16[1,2,128,768]{3,2,1,0:T(8,128)(2,1)S(1)} %copy-done.5), channel_id=1, source_target_pairs={{12,16},{8,20},{4,24},{0,28},{13,17},{9,21},{5,25},{1,29},{14,18},... | collective-permute-start | bytes 1179656 | tf_op jit(solution)/shard_map/ppermute | solution.py:1152
  298.8 0.8 copy-start.4
  298.8 1.0 copy-start.2
  388.5 7.1 %copy-start.1 = (bf16[1024,768]{1,0:T(8,128)(2,1)S(1)}, bf16[1024,768]{1,0:T(8,128)(2,1)}, u32[]{:S(2)}) copy-start(bf16[1024,768]{1,0:T(8,128)(2,1)} %get-tuple-element.64) | copy-start | bytes 4718596
  394.9 1.9 copy-start
Sparse Core Ops, SparseCore 0:
  157.7 160.2 reduce-scatter.1

commit v5 on v4

--- a/solution.py
+++ b/solution.py
@@ -451,20 +451,20 @@
 
     @pl.when(f == 0)
     def _():
-        pltpu.make_async_copy(kv_ref, all_kv.at[tuple(me)], own_sem).start()
+        own = pltpu.make_async_copy(kv_ref, all_kv.at[tuple(me)], own_sem)
+        own.start()
         barrier = pltpu.get_barrier_semaphore()
         for bit in bits:
             pl.semaphore_signal(barrier, inc=1, device_id=partner(bit), device_id_type=MESH)
         pl.semaphore_signal(barrier, inc=1, device_id={"seq": n_seq - 1 - block}, device_id_type=MESH)
+        pl.semaphore_wait(barrier, stages + 1)
+        own.wait()
 
     end = 2 * tiles - 1
-    when = [min(max(2, 2 * k + 1), end) for k in range(stages)]
+    when = [min(2 * k - 1, end) if k else 0 for k in range(stages)]
     after = when[-1]
 
     def progress(point):
-        if point == when[0]:
-            pl.semaphore_wait(pltpu.get_barrier_semaphore(), stages + 1)
-            pltpu.make_async_copy(kv_ref, all_kv.at[tuple(me)], own_sem).wait()
         for stage in range(stages):
             if when[stage] == point:
                 for copy in kv_copies(stage - 1) if stage else []:
@@ -818,15 +818,15 @@
     (sums_ref, o_hbm, dq_hbm, *refs) = refs
     backs, refs = refs[:len(counts)], refs[len(counts):]
     backs = [ref.at[k] for ref, count in zip(backs, counts) for k in range(count)]
-    (xa_ref, b_ref, x_hbm, c_hbm, out_hbm, dx_hbm, wide_ref, wp_ref, ga_ref, gf_ref, weight_ref, subset_ref, near_ref, far_ref,
+    (xa_hbm, b_hbm, x_hbm, c_hbm, out_hbm, dx_hbm, wide_hbm, wp_ref, ga_ref, gf_ref, weight_ref, subset_ref, near_ref, far_ref,
      layer_ref, states_ref, square_ref, small_ref, *refs) = refs
     f32, bf16 = jnp.float32, jnp.bfloat16
-    T, D = xa_ref.shape
+    T, D = xa_hbm.shape
     n = len(bits)
     seq_bits = [i for i in range(n) if bits[i][0] == "seq"]
     n_s = len(seq_bits)
     me = place(bits)
-    o_ref, dq_ref, x_ref, c_ref, out_ref, dx_ref, ai_ref, gq, go, gs, inv_ref, load_sem, *refs = refs
+    o_ref, dq_ref, xa_ref, b_ref, wide_ref, x_ref, c_ref, out_ref, dx_ref, ai_ref, gq, go, gs, inv_ref, load_sem, *refs = refs
 
     def take(stages):
         nonlocal refs
@@ -835,8 +835,8 @@
 
     loads = [pltpu.make_async_copy(s, d, load_sem.at[i])
              for i, (s, d) in enumerate((
-                 (dq_hbm.at[:T], dq_ref), (o_hbm.at[:T], o_ref), (out_hbm, out_ref),
-                 (x_hbm, x_ref), (dx_hbm, dx_ref), (c_hbm, c_ref)))]
+                 (dq_hbm.at[:T], dq_ref), (xa_hbm, xa_ref), (o_hbm.at[:T], o_ref), (b_hbm, b_ref), (wide_hbm, wide_ref),
+                 (out_hbm, out_ref), (x_hbm, x_ref), (dx_hbm, dx_ref), (c_hbm, c_ref)))]
     for load in loads:
         load.start()
     greet(bits)
@@ -870,8 +870,8 @@
         h.start(0)
 
     block = lax.axis_index("seq")
-    loads[0].wait()
-    loads[1].wait()
+    for load in loads[:4]:
+        load.wait()
     for k, at in enumerate(order):
         r = slice(at * M, (at + 1) * M)
         away = functools.reduce(jnp.logical_or, [block == i for i in range(len(moved)) if moved[i] > k])
@@ -918,10 +918,11 @@
             if stage + 1 < n:
                 h.start(stage + 1)
 
+    loads[4].wait()
     for i in range(chunks):
         backward(i)
     advance()
-    for load in loads[2:5]:
+    for load in loads[5:8]:
         load.wait()
     for i in range(chunks):
         forward(i)
@@ -945,7 +946,7 @@
             grads.append(jnp.where(first, turned, part).astype(bf16))
     pairs = jnp.concatenate(grads, axis=0)
     gs[:, :128] = dot(xa_ref[...], pairs, 0, 0)
-    loads[5].wait()
+    loads[8].wait()
     for i in range(chunks):
         r = slice(i * chunk, (i + 1) * chunk)
         unit = out_ref[r, :]
@@ -987,9 +988,10 @@
     smem = pl.BlockSpec(memory_space=pltpu.SMEM)
     token = jax.ShapeDtypeStruct((T, D), bf16)
     scratch = [
-        *[pltpu.VMEM((T, D), bf16)] * 4, *[pltpu.VMEM((T, D), f32)] * 3,
+        *[pltpu.VMEM((T, D), bf16)] * 4, pltpu.VMEM((2, D, D), bf16), *[pltpu.VMEM((T, D), bf16)] * 2,
+        *[pltpu.VMEM((T, D), f32)] * 3,
         pltpu.VMEM((D, D), f32), pltpu.VMEM((D, D), f32), pltpu.VMEM((D, 256), f32),
-        pltpu.VMEM((T, 1), f32), pltpu.SemaphoreType.DMA((6,)),
+        pltpu.VMEM((T, 1), f32), pltpu.SemaphoreType.DMA((9,)),
     ]
     for _ in range(here):
         scratch += halving_shapes(n_s, 128, length // n_seq)
@@ -999,7 +1001,7 @@
     return pl.pallas_call(
         functools.partial(post_kernel, bits, here, M, tuple(order), tuple(moved), tuple(b.shape[0] for b in backs), chunk),
         out_shape=[token, token, jax.ShapeDtypeStruct((2, owned, D), f32), jax.ShapeDtypeStruct((owned, 256), f32)],
-        in_specs=[vmem, anywhere, anywhere] + [vmem] * len(backs) + [vmem] * 2 + [anywhere] * 4 + [vmem] * 4 + [smem] * 2 + [vmem] * 2,
+        in_specs=[vmem, anywhere, anywhere] + [vmem] * len(backs) + [anywhere] * 7 + [vmem] * 3 + [smem] * 2 + [vmem] * 2,
         out_specs=[vmem] * 4,
         scratch_shapes=scratch,
         compiler_params=pltpu.CompilerParams(
@@ -1057,11 +1059,11 @@
     mean = sum(cost(t) + cost(k) for t, k in zip(takes, keeps)) / n
     lists = ([], [], [])
     for take, keep in zip(takes, keeps):
-        ahead, between = (0.32, 0.42) if take else (0.24, 0.40)
+        ahead = 0.32 if take else 0.24
         keep, head, middle = list(keep), list(take[:1]), list(take[1:])
         while len(keep) > 1 and cost(head) + price(keep[0][2]) / 2 < ahead * mean:
             head.append(keep.pop(0))
-        while len(keep) > 1 and cost(middle) + price(keep[0][2]) / 2 < between * mean and cost(keep) > 0.24 * mean:
+        while len(keep) > 1 and cost(middle) + price(keep[0][2]) / 2 < 0.2 * mean:
             middle.append(keep.pop(0))
         for part, steps in zip(lists, (head, middle, keep)):
             part.append(steps)

time: 410 us -> 394 us (0.961)
  Pallas kernels: 370 us -> 353 us
    pallas_call x1, Pallas kernels: 88.7 us -> 72.5 us  [post(): pl.pallas_call(functools.partial(post_kernel, bits, here, M, tuple(order)...]
  transfers between devices with their start and end apart: 4 -> 4, of which waited for: 0 -> 0; matrix products, arithmetic and copies ran while one was open for 2% -> 3% of each run, Pallas kernels for 54% -> 52%
where the time goes in v5:
time: 394 us; the launch traced here: 388 us
  Pallas kernels  353 us (90%)
  local copies, waits for them, and re-layouts  14.8 us (4%)
  between operations  14.5 us (4%)
  starting transfers between devices  3.98 us (1%)
    pallas_call x3, Pallas kernels, attention(): pl.pallas_call(kernel, grid_spec=pltpu.PrefetchScalarGridSpec(num_scalar_...  131 us
    pallas_call x1, Pallas kernels, front(): pl.pallas_call(functools.partial(front_kernel, bits, here, M, chunk, stre...  86.7 us
    pallas_call x1, Pallas kernels, post(): pl.pallas_call(functools.partial(post_kernel, bits, here, M, tuple(order)...  72.5 us
    pallas_call x1, Pallas kernels, ffn_packed(): pl.pallas_call(functools.partial(ffn_packed_kernel, C, bits, M, tuple(ord...  62.5 us
  transfers between devices with their start and end apart: 4, of which 0 were waited for; matrix products, arithmetic and copies ran while one was open for 3% of the time, Pallas kernels for 52%

profile of v5, /device:TPU:0, one launch (start us, length us, event | category | flops | bytes accessed | tf_op | source)
XLA Modules:
  0.0 387.8 jit_solution(5952882192373459521)
XLA Ops:
  7.2 86.7 %front.1 = (bf16[1024,768]{1,0:T(8,128)(2,1)}, bf16[1024,768]{1,0:T(8,128)(2,1)}, bf16[1024,128]{1,0:T(8,128)(2,1)}, bf16[1024,768]{1,0:T(8,128)(2,1)}, bf16[102...) custom-call(bf16[1024,768]{1,0:T(8,128)(2,1)} %bitcast.53, ...), custom_call_target="tpu_custom_call" | custom-call | tf_op jit(solution)/shard_map/front/pallas_call | solution.py:739
  93.9 62.5 %feedforward.1 = (f32[1024,768]{1,0:T(8,128)}, f32[1024,768]{1,0:T(8,128)}, bf16[32,192,768]{2,1,0:T(8,128)(2,1)}, bf16[2,2,2,2,512,128]{5,4,3,2,1,0:T(8,128)(2,1)}, bf16[1,2,128,768]{3,2,1,0:T(8,128)(2,1)}) custom-call(bf16[1024,768]{1,0:T(8,128)(2,1)} %get-tuple-element.42.x_ref, bf16[1024,768]{1,0:T(8,128)(2,1)} %get-tuple-element.43.b_ref.refs_6_, ...), custom_call_target="tpu_custom_call" | custom-call | flops 1048576 | bytes 65536 | tf_op jit(solution)/shard_map/feedforward/pallas_call | solution.py:562
  156.4 1.3 slice_bitcast_fusion.2
  157.9 1.3 collective-permute-start
  159.2 0.7 dynamic-slice_bitcast_fusion
  159.9 0.7 slice_reduce_fusion.4
  160.6 44.2 %attention.3 = (bf16[1152,768]{1,0:T(8,128)(2,1)}, bf16[1152,768]{1,0:T(8,128)(2,1)}, f32[2,128,4096]{2,1,0:T(8,128)}, bf16[1,2,128,768]{3,2,1,0:T(8,128)(2,1)}) custom-call(s32[3]{0:T(128)} %get-tuple-element.76.slot_ref, s32[3]{0:T(128)} %get-tuple-element.75.seq_ref, s32[3]{0:T(128)} %get-tuple-element.74.row_ref, s32[3]{0:T(128)} %get-tuple-element.73.on_ref, ...), custom_call_target="tpu_custom_call" | custom-call | flops 1048576 | bytes 65536 | tf_op jit(solution)/shard_map/attention/pallas_call | solution.py:276
  204.8 0.7 dynamic-slice_bitcast_fusion.2
  205.5 0.7 slice_reduce_fusion.8
  206.3 0.9 copy-done.3
  207.1 55.4 %attention.4 = (bf16[1152,768]{1,0:T(8,128)(2,1)}, bf16[1152,768]{1,0:T(8,128)(2,1)}, f32[2,128,4096]{2,1,0:T(8,128)}, bf16[2,2,128,768]{3,2,1,0:T(8,128)(2,1)}) custom-call(s32[2]{0:T(128)} %get-tuple-element.80.slot_ref, s32[2]{0:T(128)} %get-tuple-element.79.seq_ref, ...), custom_call_target="tpu_custom_call", output_to_operand_aliasing={{0}: (10, {}), {1}: (11, {}), {2}: (12, {})} | custom-call | flops 1048576 | bytes 65536 | tf_op jit(solution)/shard_map/attention/pallas_call | solution.py:276
  262.6 1.3 collective-permute-start.2
  263.9 1.3 collective-permute-start.1
  265.2 0.7 dynamic-slice_bitcast_fusion.1
  266.5 31.3 %attention.5 = (bf16[1152,768]{1,0:T(8,128)(2,1)}, bf16[1152,768]{1,0:T(8,128)(2,1)}, f32[2,128,4096]{2,1,0:T(8,128)}) custom-call(s32[6]{0:T(128)} %get-tuple-element.92.a, s32[6]{0:T(128)} %get-tuple-element.91.b, s32[6]{0:T(128)} %get-tuple-element.90.c, s32[6]{0:T(128)} %get-tuple-element.89.d, ...), custom_call_target="tpu_custom_call", output_to_operand_aliasing={{0}: (9, {}), {1}: (10, {}), {2}: (11, {})} | custom-call | flops 1048576 | bytes 65536 | tf_op jit(solution)/shard_map/attention/pallas_call | solution.py:276
  297.8 0.7 copy-done.4
  298.8 72.5 %post.1 = (bf16[1024,768]{1,0:T(8,128)(2,1)}, bf16[1024,768]{1,0:T(8,128)(2,1)}, f32[2,24,768]{2,1,0:T(8,128)}, f32[24,256]{1,0:T(8,128)}) custom-call(f32[2,128,4096]{2,1,0:T(8,128)} %get-tuple-element.54.refs_0_, bf16[1152,768]{1,0:T(8,128)(2,1)} %get-tuple-element.55.refs_1_, bf16[1152,768]{1,0:T(8,128)(2,1)} %get-tuple-element.56.refs_2_, ...), custom_call_target="tpu_custom_call" | custom-call | tf_op jit(solution)/shard_map/post/pallas_call | solution.py:1001
  371.3 1.4 slice.119
  372.7 1.6 slice_reduce_fusion
  374.3 1.6 slice_bitcast_fusion.5
  375.9 1.7 fusion
  377.6 0.7 copy.45
  378.4 1.1 copy.54
  379.5 1.1 copy.55
  (21 shorter events, 1.0 us)
Async XLA Ops:
  7.2 368.7 %reduce-scatter.2.cloned.1.call-start = ((), (), s32[]{:S(2)}) async-start(), calls=%async_computation.1 | async-start | bytes 9732096 | tf_op jit(solution)/shard_map/reduce_scatter | solution.py:1164
  157.9 48.4 %collective-permute-start = (bf16[2,2,128,768]{3,2,1,0:T(8,128)(2,1)S(1)}, bf16[2,2,128,768]{3,2,1,0:T(8,128)(2,1)S(1)}, u32[]{:S(2)}, u32[]{:S(2)}) collective-permute-start(bf16[2,2,128,768]{3,2,1,0:T(8,128)(2,1)S(1)} %pad_maximum_fusion), channel_id=1, source_target_pairs={{20,8},{24,4},{28,0},{21,9},{25,5},{29,1},{22,10},{26,6},{30,2},{2... | collective-permute-start | bytes 2359304 | tf_op jit(solution)/shard_map/ppermute | solution.py:1150
  206.2 0.9 copy-start.3
  207.1 56.8 %copy-start.5 = (bf16[1,2,128,768]{3,2,1,0:T(8,128)(2,1)S(1)}, bf16[1,2,128,768]{3,2,1,0:T(8,128)(2,1)}, u32[]{:S(2)}) copy-start(bf16[1,2,128,768]{3,2,1,0:T(8,128)(2,1)} %get-tuple-element.57) | copy-start | bytes 1179652
  262.6 35.2 %collective-permute-start.2 = (bf16[2,2,128,768]{3,2,1,0:T(8,128)(2,1)}, bf16[2,2,128,768]{3,2,1,0:T(8,128)(2,1)S(1)}, u32[]{:S(2)}, u32[]{:S(2)}) collective-permute-start(bf16[2,2,128,768]{3,2,1,0:T(8,128)(2,1)} %get-tuple-element.58), channel_id=1, source_target_pairs={{8,20},{4,24},{0,28},{9,21},{5,25},{1,29},{10,22},{6,26},{2,30},{1... | collective-permute-start | bytes 2359304 | tf_op jit(solution)/shard_map/ppermute | solution.py:1154
  263.9 33.8 %collective-permute-start.1 = (bf16[1,2,128,768]{3,2,1,0:T(8,128)(2,1)S(1)}, bf16[1,2,128,768]{3,2,1,0:T(8,128)(2,1)S(1)}, u32[]{:S(2)}, u32[]{:S(2)}) collective-permute-start(bf16[1,2,128,768]{3,2,1,0:T(8,128)(2,1)S(1)} %copy-done.5), channel_id=1, source_target_pairs={{12,16},{8,20},{4,24},{0,28},{13,17},{9,21},{5,25},{1,29},{14,18},... | collective-permute-start | bytes 1179656 | tf_op jit(solution)/shard_map/ppermute | solution.py:1154
  297.7 0.8 copy-start.4
  297.8 1.0 copy-start.2
  371.2 7.1 %copy-start.1 = (bf16[1024,768]{1,0:T(8,128)(2,1)S(1)}, bf16[1024,768]{1,0:T(8,128)(2,1)}, u32[]{:S(2)}) copy-start(bf16[1024,768]{1,0:T(8,128)(2,1)} %get-tuple-element.64) | copy-start | bytes 4718596
  377.6 1.9 copy-start
Sparse Core Ops, SparseCore 0:
  156.5 166.5 reduce-scatter.1

commit v6 on v5

--- a/solution.py
+++ b/solution.py
@@ -58,7 +58,7 @@
 
 def attn_kernel(
     M, tk, own, first_call,
-    slot_ref, seq_ref, row_ref, on_ref,
+    block_ref, table_ref,
     q_ref, g_ref, other_ref, near_ref, far_ref, kv_ref, *refs,
 ):
     if not first_call:
@@ -67,10 +67,10 @@
     given_ref = None
     if other_ref is not None:
         given_ref, *refs = refs
-    ka, va, qs, gs, qt, gt, stash, oacc, dqacc, top, delta, dkv_ref, limit, sum_sem = refs
+    ka, va, qs, gs, qt, gt, stash, oacc, dqacc, top, delta, dkv_ref, limit, sum_sem, other_sem = refs
     t = pl.program_id(0)
-    seq = seq_ref[t]
-    row0 = row_ref[t]
+    at = (block_ref[0] * pl.num_programs(0) + t) * 4
+    slot, seq, row0, on = (table_ref[at + i] for i in range(4))
     G = 4 * M
     groups = [slice(g * G, (g + 1) * G) for g in range(H // 4)]
     heads = [slice(h * M, (h + 1) * M) for h in range(H)]
@@ -101,9 +101,19 @@
 
         limit[0] = jnp.max(lax.fori_loop(0, parts_, arrange, jnp.zeros((block, 128), f32)))
 
-    @pl.when(on_ref[t] != 0)
+    def ready():
+        for s in range(count):
+            @pl.when(s != seq)
+            def _(s=s):
+                pltpu.make_async_copy(dkv_ref.at[s], sums_ref.at[s], other_sem.at[s]).start()
+
+    @pl.when((on == 0) & (t == pl.num_programs(0) - 1))
     def _():
-        taken = slot_ref[t] >= own
+        ready()
+
+    @pl.when(on != 0)
+    def _():
+        taken = slot >= own
         q_in = q_ref[...] if other_ref is None else jnp.where(taken, other_ref[0, 0], q_ref[...])
         g_in = g_ref[...] if other_ref is None else jnp.where(taken, other_ref[0, 1], g_ref[...])
         lane = lax.broadcasted_iota(jnp.int32, (M, 128), 1)
@@ -201,6 +211,10 @@
             def _():
                 pltpu.make_async_copy(before_ref, dkv_ref, sum_sem).wait()
 
+        @pl.when(t == pl.num_programs(0) - 1)
+        def _():
+            ready()
+
         def second(kt, size=tk):
             k = keys(ka, kt, size)
             v = keys(va, kt, size)
@@ -231,24 +245,29 @@
 
     @pl.when(t == pl.num_programs(0) - 1)
     def _():
-        copy = pltpu.make_async_copy(dkv_ref, sums_ref, sum_sem)
+        copy = pltpu.make_async_copy(dkv_ref.at[seq], sums_ref.at[seq], sum_sem)
         copy.start()
         copy.wait()
-
-
-def attention(tables, q, g, others, skip, kv, M, tk, before=None):
+        for s in range(count):
+            @pl.when(s != seq)
+            def _(s=s):
+                pltpu.make_async_copy(dkv_ref.at[s], sums_ref.at[s], other_sem.at[s]).wait()
+
+
+def attention(place_of, table, q, g, others, skip, kv, M, tk, before=None):
     width = H * HD
-    steps = tables[0].shape[0]
+    steps = table.shape[1]
+    slot_of = lambda t, block, table: table[(block[0] * steps + t) * 4]
     own = q.shape[0] // M
     parts, S, block, _ = kv.shape
     L = parts * block
     near, far = turn_tables(L, M)
     whole = pl.Buffered(1)
-    tile = pl.BlockSpec((M, width), lambda t, slot, *_: (jnp.minimum(slot[t], own), 0))
+    tile = pl.BlockSpec((M, width), lambda t, *s: (jnp.minimum(slot_of(t, *s), own), 0))
     near_spec = pl.BlockSpec(near.shape, lambda t, *_: (0, 0), pipeline_mode=whole)
     far_spec = pl.BlockSpec(far.shape, lambda t, *_: (0, 0), pipeline_mode=whole)
-    mine = pl.BlockSpec((M, width), lambda t, slot, *_: (jnp.minimum(slot[t], own - 1), 0))
-    taken = pl.BlockSpec((1, 2, M, width), lambda t, slot, *_: (jnp.maximum(slot[t] - own - skip, 0), 0, 0, 0))
+    mine = pl.BlockSpec((M, width), lambda t, *s: (jnp.minimum(slot_of(t, *s), own - 1), 0))
+    taken = pl.BlockSpec((1, 2, M, width), lambda t, *s: (jnp.maximum(slot_of(t, *s) - own - skip, 0), 0, 0, 0))
     anywhere = pl.BlockSpec(memory_space=pl.ANY)
     bf16, f32 = jnp.bfloat16, jnp.float32
     pairs = steps * M * H * L // 3
@@ -256,14 +275,14 @@
     operands, specs = [q, g], [mine, mine]
     if others is None:
         inner = kernel
-        kernel = lambda a, b, c, d, q_ref, g_ref, *refs: inner(a, b, c, d, q_ref, g_ref, None, *refs)
+        kernel = lambda a, b, q_ref, g_ref, *refs: inner(a, b, q_ref, g_ref, None, *refs)
     else:
         operands, specs = operands + [others], specs + [taken]
     operands += [near, far, kv]
     specs += [near_spec, far_spec, pl.BlockSpec(kv.shape, lambda t, *_: (0, 0, 0, 0), pipeline_mode=whole)]
     aliases = {}
     if before is not None:
-        aliases = {4 + len(operands) + i: i for i in range(3)}
+        aliases = {2 + len(operands) + i: i for i in range(3)}
         operands, specs = operands + list(before), specs + [anywhere] * 3
     slots = jax.ShapeDtypeStruct(((own + 1) * M, width), bf16)
     out_shape, out_specs = [slots, slots, jax.ShapeDtypeStruct((S, 128, L), f32)], [tile, tile, anywhere]
@@ -272,11 +291,12 @@
         out_shape.append(jax.ShapeDtypeStruct(others.shape, bf16))
         out_specs.append(pl.BlockSpec(
             (1, 2, M, width),
-            lambda t, slot, *_: (jnp.where(slot[t] < own, count - 1, jnp.minimum(slot[t] - own - skip, count - 1)), 0, 0, 0)))
+            lambda t, *s: (jnp.where(
+                slot_of(t, *s) < own, count - 1, jnp.minimum(slot_of(t, *s) - own - skip, count - 1)), 0, 0, 0)))
     return pl.pallas_call(
         kernel,
         grid_spec=pltpu.PrefetchScalarGridSpec(
-            num_scalar_prefetch=4,
+            num_scalar_prefetch=2,
             grid=(steps,),
             in_specs=specs,
             out_specs=out_specs,
@@ -295,6 +315,7 @@
                 pltpu.VMEM((S, 128, L), f32),
                 pltpu.SMEM((1,), f32),
                 pltpu.SemaphoreType.DMA,
+                pltpu.SemaphoreType.DMA((S,)),
             ],
         ),
         out_shape=out_shape,
@@ -302,7 +323,7 @@
         compiler_params=pltpu.CompilerParams(vmem_limit_bytes=58 << 20),
         cost_estimate=pl.CostEstimate(flops=1 << 20, bytes_accessed=1 << 16, transcendentals=0),
         name="attention",
-    )(*tables, *operands)
+    )(place_of, jnp.asarray(table.reshape(-1)), *operands)
 
 
 MESH = pl.DeviceIdType.MESH
@@ -819,7 +840,7 @@
     backs, refs = refs[:len(counts)], refs[len(counts):]
     backs = [ref.at[k] for ref, count in zip(backs, counts) for k in range(count)]
     (xa_hbm, b_hbm, x_hbm, c_hbm, out_hbm, dx_hbm, wide_hbm, wp_ref, ga_ref, gf_ref, weight_ref, subset_ref, near_ref, far_ref,
-     layer_ref, states_ref, square_ref, small_ref, *refs) = refs
+     layer_ref, states_ref, query_out, output_out, pair_out, vector_out, *refs) = refs
     f32, bf16 = jnp.float32, jnp.bfloat16
     T, D = xa_hbm.shape
     n = len(bits)
@@ -963,17 +984,17 @@
     small.start(0)
     while moved_on[0] < n:
         advance()
-    for i, h in enumerate(squares):
+    for h, ref in zip(squares, (query_out, output_out)):
         total = h.acc[n - 1][0]
-        square_ref[i, :, :D // 2] = total[:owned]
-        square_ref[i, :, D // 2:] = total[owned:]
+        ref[:, :D // 2] = total[:owned]
+        ref[:, D // 2:] = total[owned:]
     for stage in range(n):
         small.finish(stage)
         if stage + 1 < n:
             small.start(stage + 1)
     total = small.acc[n - 1][0]
-    small_ref[:, :128] = total[:owned]
-    small_ref[:, 128:] = total[owned:]
+    pair_out[...] = total[:owned]
+    vector_out[...] = total[owned:]
 
 
 def post(sums, o, dq, backs, order, moved, xa, b, x, c, out, dx, wide, wp, norms, weights, subsets,
@@ -1000,9 +1021,9 @@
     scratch += halving_shapes(n, 2 * owned, 128)
     return pl.pallas_call(
         functools.partial(post_kernel, bits, here, M, tuple(order), tuple(moved), tuple(b.shape[0] for b in backs), chunk),
-        out_shape=[token, token, jax.ShapeDtypeStruct((2, owned, D), f32), jax.ShapeDtypeStruct((owned, 256), f32)],
+        out_shape=[token, token] + [jax.ShapeDtypeStruct((owned, w), f32) for w in (D, D, 128, 128)],
         in_specs=[vmem, anywhere, anywhere] + [vmem] * len(backs) + [anywhere] * 7 + [vmem] * 3 + [smem] * 2 + [vmem] * 2,
-        out_specs=[vmem] * 4,
+        out_specs=[vmem] * 6,
         scratch_shapes=scratch,
         compiler_params=pltpu.CompilerParams(
             collective_id=collective_id, has_side_effects=True, vmem_limit_bytes=60 << 20),
@@ -1139,10 +1160,7 @@
     order, moved, most, tables = plan(n_seq, here, per, M, tk)
     own = here * per
     at_slots = [s * per + j for s, j in order[:most]]
-    steps = []
-    for table in tables:
-        mine = jnp.asarray(table)[block]
-        steps.append(tuple(mine[:, c] for c in range(4)))
+    here_at = block.reshape(1).astype(jnp.int32)
     q_tiles, g_tiles = queries.reshape(own, M, D), out_grad.reshape(own, M, D)
 
     def send(tiles):
@@ -1162,31 +1180,30 @@
         ffn_out, ffn_input_grad, grad_up, grad_down = ffn(feedforward_input, branch_grad, full_up, full_down)
         ffn_grads = jnp.concatenate([grad_up.reshape(n, -1, D), grad_down.reshape(n, -1, D)], axis=1)
     ffn_grads = lax.psum_scatter(ffn_grads, both, scatter_dimension=0, tiled=True)[0]
-    *done, given = attention(steps[0], queries, out_grad, first_taken, 0, all_kv, M, tk)
+    *done, given = attention(here_at, tables[0], queries, out_grad, first_taken, 0, all_kv, M, tk)
     backs = [send_back(given, 0)]
     if most > 1:
         *done, given = attention(
-            steps[1], queries, out_grad, send(list(range(1, most))), 1, all_kv, M, tk, done)
+            here_at, tables[1], queries, out_grad, send(list(range(1, most))), 1, all_kv, M, tk, done)
         backs.append(send_back(given, 1))
     else:
-        done = attention(steps[1], queries, out_grad, None, 0, all_kv, M, tk, done)
+        done = attention(here_at, tables[1], queries, out_grad, None, 0, all_kv, M, tk, done)
     half = ffn_grads.shape[0] // 2
     final_up = ffn_grads[:half]
     if aligned:
         final_up = jnp.swapaxes(final_up.reshape(FF // D, own_rows, D), 0, 1)
     final_up = final_up.reshape(-1, FF).astype(f32)
     final_down = ffn_grads[half:].astype(f32)
-    attended, query_pre_grad, pair_terms = attention(steps[2], queries, out_grad, None, 0, all_kv, M, tk, done)
+    attended, query_pre_grad, pair_terms = attention(here_at, tables[2], queries, out_grad, None, 0, all_kv, M, tk, done)
     if aligned:
-        layer_out, grad_states, squares, small = post(
+        layer_out, grad_states, grad_query, grad_output, grad_pair, vectors = post(
             pair_terms, attended, query_pre_grad, backs, at_slots, moved, attention_input, branch_grad,
             states.reshape(T, D), cotangent.reshape(T, D), ffn_out, ffn_input_grad, wide, full_pair, norms, subset_weight, subsets,
             here, length, M, n_seq, n_rows, 2)
-        vectors = small[:, P:]
         return (
             layer_out.reshape(states.shape), grad_states.reshape(states.shape),
             vectors[:, 0], vectors[:, 1], vectors[:, 2], vectors[:, 3],
-            squares[0], small[:, :P], squares[1], final_up, final_down,
+            grad_query, grad_pair, grad_output, final_up, final_down,
         )
 
     a_own, d_own = list(attended.reshape(-1, M, D)[:own]), list(query_pre_grad.reshape(-1, M, D)[:own])

time: 394 us -> 392 us (level)
  local copies, waits for them, and re-layouts: 14.8 us -> 9.68 us
  Pallas kernels: 353 us -> 357 us
    pallas_call x1, Pallas kernels: 72.5 us -> 78.9 us  [post(): pl.pallas_call(functools.partial(post_kernel, bits, here, M, tuple(order)...]
    squeeze x5 -> x0, local copies, waits for them, and re-layouts: 4.18 us -> none  [the longest x3 2.07 us: local(): mine = jnp.asarray(table)[block]]
  transfers between devices with their start and end apart: 4 -> 4, of which waited for: 0 -> 1; matrix products, arithmetic and copies ran while one was open for 3% -> 1% of each run, Pallas kernels for 52% -> 54%
where the time goes in v6:
time: 392 us; the launch traced here: 387 us
  Pallas kernels  357 us (91%)
  between operations  14.5 us (4%)
  local copies, waits for them, and re-layouts  9.68 us (2%)
  starting transfers between devices  3.98 us (1%)
    pallas_call x3, Pallas kernels, attention(): pl.pallas_call(kernel, grid_spec=pltpu.PrefetchScalarGridSpec(num_scalar_...  129 us
    pallas_call x1, Pallas kernels, front(): pl.pallas_call(functools.partial(front_kernel, bits, here, M, chunk, stre...  86.7 us
    pallas_call x1, Pallas kernels, post(): pl.pallas_call(functools.partial(post_kernel, bits, here, M, tuple(order)...  78.9 us
    pallas_call x1, Pallas kernels, ffn_packed(): pl.pallas_call(functools.partial(ffn_packed_kernel, C, bits, M, tuple(ord...  62.5 us
  transfers between devices with their start and end apart: 4, of which 1 were waited for; matrix products, arithmetic and copies ran while one was open for 1% of the time, Pallas kernels for 54%

profile of v6, /device:TPU:0, one launch (start us, length us, event | category | flops | bytes accessed | tf_op | source)
XLA Modules:
  0.0 386.9 jit_solution(7477208913867650292)
XLA Ops:
  7.2 0.0 reduce-scatter.2.cloned.1.call-start
  7.2 86.7 %front.1 = (bf16[1024,768]{1,0:T(8,128)(2,1)}, bf16[1024,768]{1,0:T(8,128)(2,1)}, bf16[1024,128]{1,0:T(8,128)(2,1)}, bf16[1024,768]{1,0:T(8,128)(2,1)}, bf16[102...) custom-call(bf16[1024,768]{1,0:T(8,128)(2,1)} %bitcast.36, ...), custom_call_target="tpu_custom_call" | custom-call | tf_op jit(solution)/shard_map/front/pallas_call | solution.py:760
  93.9 62.5 %feedforward.1 = (f32[1024,768]{1,0:T(8,128)}, f32[1024,768]{1,0:T(8,128)}, bf16[32,192,768]{2,1,0:T(8,128)(2,1)}, bf16[2,2,2,2,512,128]{5,4,3,2,1,0:T(8,128)(2,1)}, bf16[1,2,128,768]{3,2,1,0:T(8,128)(2,1)}) custom-call(bf16[1024,768]{1,0:T(8,128)(2,1)} %get-tuple-element.44.x_ref, bf16[1024,768]{1,0:T(8,128)(2,1)} %get-tuple-element.45.b_ref.refs_6_, ...), custom_call_target="tpu_custom_call" | custom-call | flops 1048576 | bytes 65536 | tf_op jit(solution)/shard_map/feedforward/pallas_call | solution.py:583
  156.4 1.3 slice_bitcast_fusion.2
  157.8 0.1 pad_maximum_fusion
  157.9 1.3 collective-permute-start
  159.2 43.7 %attention.3 = (bf16[1152,768]{1,0:T(8,128)(2,1)}, bf16[1152,768]{1,0:T(8,128)(2,1)}, f32[2,128,4096]{2,1,0:T(8,128)}, bf16[1,2,128,768]{3,2,1,0:T(8,128)(2,1)}) custom-call(s32[1]{0:T(128)} %bitcast.block_ref.a, s32[96]{0:T(128)} %constant.18.clone.table_ref, bf16[1024,768]{1,0:T(8,128)(2,1)} %get-tuple-element.42.q_ref, ...), custom_call_target="tpu_custom_call" | custom-call | flops 1048576 | bytes 65536 | tf_op jit(solution)/shard_map/attention/pallas_call | solution.py:296
  202.9 0.9 copy-done.3
  203.7 54.2 %attention.4 = (bf16[1152,768]{1,0:T(8,128)(2,1)}, bf16[1152,768]{1,0:T(8,128)(2,1)}, f32[2,128,4096]{2,1,0:T(8,128)}, bf16[2,2,128,768]{3,2,1,0:T(8,128)(2,1)}) custom-call(s32[1]{0:T(128)} %bitcast.block_ref.a, s32[64]{0:T(128)} %constant.19.clone.table_ref, ...), custom_call_target="tpu_custom_call", output_to_operand_aliasing={{0}: (8, {}), {1}: (9, {}), {2}: (10, {})} | custom-call | flops 1048576 | bytes 65536 | tf_op jit(solution)/shard_map/attention/pallas_call | solution.py:296
  258.0 1.3 collective-permute-start.2
  259.3 1.3 collective-permute-start.1
  260.7 30.6 %attention.5 = (bf16[1152,768]{1,0:T(8,128)(2,1)}, bf16[1152,768]{1,0:T(8,128)(2,1)}, f32[2,128,4096]{2,1,0:T(8,128)}) custom-call(s32[1]{0:T(128)} %bitcast.block_ref.a, s32[192]{0:T(256)} %constant.20.clone.b, bf16[1024,768]{1,0:T(8,128)(2,1)} %get-tuple-element.42.q_ref, ...), custom_call_target="tpu_custom_call", output_to_operand_aliasing={{0}: (7, {}), {1}: (8, {}), {2}: (9, {})} | custom-call | flops 1048576 | bytes 65536 | tf_op jit(solution)/shard_map/attention/pallas_call | solution.py:296
  291.3 0.2 collective-permute-done.1.refs_3_
  291.5 0.7 copy-done.4
  292.3 0.3 copy-done.2
  292.5 78.9 %post.1 = (bf16[1024,768]{1,0:T(8,128)(2,1)}, bf16[1024,768]{1,0:T(8,128)(2,1)}, f32[24,768]{1,0:T(8,128)}, f32[24,768]{1,0:T(8,128)}, f32[24,128]{1,0:T(8,128)}, /*index=5*/f32[24,128]{1,0:T(8,128)}) custom-call(f32[2,128,4096]{2,1,0:T(8,128)} %get-tuple-element.56.refs_0_, bf16[1152,768]{1,0:T(8,128)(2,1)} %get-tuple-element.57.refs_1_, ...), custom_call_target="tpu_custom_call" | custom-call | tf_op jit(solution)/shard_map/post/pallas_call | solution.py:1022
  371.5 1.6 slice_reduce_fusion
  373.1 1.7 fusion
  374.9 0.7 copy.45
  375.6 1.1 copy.57
  376.8 1.1 copy.58
  377.9 0.6 copy.59
  378.6 0.6 copy.60
  379.2 0.6 copy.61
  (22 shorter events, 0.2 us)
Async XLA Ops:
  7.2 365.9 %reduce-scatter.2.cloned.1.call-start = ((), (), s32[]{:S(2)}) async-start(), calls=%async_computation.1 | async-start | bytes 9732096 | tf_op jit(solution)/shard_map/reduce_scatter | solution.py:1182
  157.9 45.0 %collective-permute-start = (bf16[2,2,128,768]{3,2,1,0:T(8,128)(2,1)S(1)}, bf16[2,2,128,768]{3,2,1,0:T(8,128)(2,1)S(1)}, u32[]{:S(2)}, u32[]{:S(2)}) collective-permute-start(bf16[2,2,128,768]{3,2,1,0:T(8,128)(2,1)S(1)} %pad_maximum_fusion), channel_id=1, source_target_pairs={{20,8},{24,4},{28,0},{21,9},{25,5},{29,1},{22,10},{26,6},{30,2},{2... | collective-permute-start | bytes 2359304 | tf_op jit(solution)/shard_map/ppermute | solution.py:1168
  202.9 0.9 copy-start.3
  203.7 55.6 %copy-start.8 = (bf16[1,2,128,768]{3,2,1,0:T(8,128)(2,1)S(1)}, bf16[1,2,128,768]{3,2,1,0:T(8,128)(2,1)}, u32[]{:S(2)}) copy-start(bf16[1,2,128,768]{3,2,1,0:T(8,128)(2,1)} %get-tuple-element.59) | copy-start | bytes 1179652
  258.0 33.6 %collective-permute-start.2 = (bf16[2,2,128,768]{3,2,1,0:T(8,128)(2,1)}, bf16[2,2,128,768]{3,2,1,0:T(8,128)(2,1)S(1)}, u32[]{:S(2)}, u32[]{:S(2)}) collective-permute-start(bf16[2,2,128,768]{3,2,1,0:T(8,128)(2,1)} %get-tuple-element.60), channel_id=1, source_target_pairs={{8,20},{4,24},{0,28},{9,21},{5,25},{1,29},{10,22},{6,26},{2,30},{1... | collective-permute-start | bytes 2359304 | tf_op jit(solution)/shard_map/ppermute | solution.py:1172
  259.3 32.2 %collective-permute-start.1 = (bf16[1,2,128,768]{3,2,1,0:T(8,128)(2,1)S(1)}, bf16[1,2,128,768]{3,2,1,0:T(8,128)(2,1)S(1)}, u32[]{:S(2)}, u32[]{:S(2)}) collective-permute-start(bf16[1,2,128,768]{3,2,1,0:T(8,128)(2,1)S(1)} %copy-done.8), channel_id=1, source_target_pairs={{12,16},{8,20},{4,24},{0,28},{13,17},{9,21},{5,25},{1,29},{14,18},... | collective-permute-start | bytes 1179656 | tf_op jit(solution)/shard_map/ppermute | solution.py:1172
  291.5 0.8 copy-start.4
  291.5 1.0 copy-start.2
  371.5 4.1 %copy-start.1 = (bf16[1024,768]{1,0:T(8,128)(2,1)S(1)}, bf16[1024,768]{1,0:T(8,128)(2,1)}, u32[]{:S(2)}) copy-start(bf16[1024,768]{1,0:T(8,128)(2,1)} %get-tuple-element.66) | copy-start | bytes 4718596
  374.9 1.9 copy-start
  376.8 1.2 copy-start.6
  376.8 1.8 copy-start.7
  376.8 2.4 copy-start.5
Sparse Core Ops, SparseCore 0:
  156.5 168.8 reduce-scatter.1
